TPU v7x, 512 devices: a whole 4x8x8 slice. The times are simulated.
512 devices in a mesh: gx: 32 (over y, x), gy: 16 (over z, core).
Axes of the slice: x: 4, y: 8, z: 8, core: 2. Of those that a mesh axis runs over, the one named last changes fastest.
Arguments:
- panel: bfloat16 [32, 16, 2, 128, 1024], P('gx', 'gy'), may hold values from -0.5 to 0.5
- corner_panel: bfloat16 [32, 16, 2, 24, 128], P('gx', 'gy'), may hold values from -0.5 to 0.5
- interface_diag: float32 [32, 16, 2, 1024], P('gx', 'gy'), may hold values from 0.5 to 2
- coarse_diag: float32 [32, 512], P('gx'), may hold values from 0.5 to 2
- scaling: float32 [32, 16, 8, 128], P('gx', 'gy'), may hold values from 0.5 to 2
- dual_rhs: float32 [32, 16, 8, 128], P('gx', 'gy'), may hold values from -6 to 6
- block_map: int32 [32, 16, 2, 8], P('gx', 'gy'), may hold values from 0 to 39
- corner_map: int32 [32, 16, 2, 24], P('gx', 'gy'), may hold values from 0 to 511
- counts: int32 [32, 16], P('gx', 'gy'), may hold values from 1 to 2, as said below
Outputs:
- multipliers: float32 [32, 16, 8, 128], P('gx', 'gy')
- residual: float32 [32, 16, 8, 128], P('gx', 'gy')
Inputs may be any that keep to these rules, and one draw needn't show every extreme that they name: `counts`: every device holds one or more live subdomains in its first slots; some device has all 2 slots live and some has one.
All inputs are finite; a program needn't handle non-finite values.
Results may differ from a plain program's by a relative error of at most 0.0003.
Values sent between devices are 32-bit elements; how exact they have to be, the bound alone decides.
No kernel may reach another device: no remote copies, remote signals or barrier semaphores. Data moves between devices by JAX's collectives and lax.ppermute only.
A program may use at most 64 MiB of HBM per device.

v0:
```python
import jax
import jax.numpy as jnp
from jax import lax
from jax.sharding import PartitionSpec as P

ITERS = 3


def extended(block, sides, width):
    for axis, dim in sides:
        count = lax.axis_size(axis)
        forward = [(i, i + 1) for i in range(count - 1)]
        backward = [(target, source) for source, target in forward]
        low = lax.ppermute(
            lax.slice_in_dim(block, block.shape[dim] - width, None, axis=dim), axis, forward
        )
        high = lax.ppermute(lax.slice_in_dim(block, 0, width, axis=dim), axis, backward)
        block = jnp.concatenate([low, block, high], axis=dim)
    return block


def weighted_norm(residual, precond):
    return lax.psum(jnp.sum(residual * precond), ("gx", "gy"))


def shards(
    panel,
    corner_panel,
    interface_diag,
    coarse_diag,
    scaling,
    dual_rhs,
    block_map,
    corner_map,
    counts,
):
    highest = lax.Precision.HIGHEST
    slots = panel.shape[2]
    width = panel.shape[4]
    owned = scaling.shape[2]
    block_size = scaling.shape[3]
    blocks_sub = width // block_size
    coarse_size = coarse_diag.shape[1]
    live = (lax.iota(jnp.int32, slots) < counts[0, 0]).astype(jnp.float32)
    factors = panel[0, 0]
    corners = corner_panel[0, 0]
    schur = jnp.einsum("sni,snj->sij", factors, factors, preferred_element_type=jnp.float32)
    width_eye = (lax.iota(jnp.int32, width)[:, None] == lax.iota(jnp.int32, width)[None, :]).astype(
        jnp.float32
    )
    schur = schur + interface_diag[0, 0][:, :, None] * width_eye[None]
    coupling = jnp.einsum("scn,sni->sci", corners, factors, preferred_element_type=jnp.float32)
    corner_block = (
        jnp.einsum("scn,sdn->scd", corners, corners, preferred_element_type=jnp.float32)
        * live[:, None, None]
    )
    local_map = block_map[0, 0]
    signs = jnp.where(local_map < owned, 1.0, -1.0) * live[:, None]
    picker = (local_map[:, :, None] == lax.iota(jnp.int32, 5 * owned)[None, None, :]).astype(
        jnp.float32
    ) * signs[:, :, None]
    coarse_iota = lax.iota(jnp.int32, coarse_size)
    own_hot = (corner_map[0, 0][:, :, None] == coarse_iota[None, None, :]).astype(jnp.float32)
    spread = jnp.einsum("sco,scd->sod", own_hot, corner_block, precision=highest)
    assembled = lax.psum(jnp.einsum("sod,sdp->op", spread, own_hot, precision=highest), "gy")
    coarse_eye = (coarse_iota[:, None] == coarse_iota[None, :]).astype(jnp.float32)
    system = assembled + coarse_diag[0][:, None] * coarse_eye
    lower = jnp.linalg.cholesky(system)

    def operate(field):
        padded = extended(field, (("gx", 0), ("gy", 1)), 1)
        candidates = jnp.concatenate(
            [padded[1, 1], padded[2, 1], padded[0, 1], padded[1, 2], padded[1, 0]], axis=0
        )
        gathered = jnp.einsum("sbk,kc->sbc", picker, candidates, precision=highest).reshape(
            slots, width
        )
        result = jnp.einsum("sij,sj->si", schur, gathered, precision=highest)
        corner_values = (
            jnp.einsum("sci,si->sc", coupling, gathered, precision=highest) * live[:, None]
        )
        coarse_right = lax.psum(
            jnp.einsum("sco,sc->o", own_hot, corner_values, precision=highest), "gy"
        )
        coarse_sol = jax.scipy.linalg.cho_solve((lower, True), coarse_right)
        back_values = jnp.einsum("sco,o->sc", own_hot, coarse_sol, precision=highest)
        result = result + jnp.einsum("sci,sc->si", coupling, back_values, precision=highest)
        contrib = jnp.einsum(
            "sbk,sbc->kc", picker, result.reshape(slots, blocks_sub, block_size), precision=highest
        )
        outgoing = contrib[owned:].reshape(4, owned, block_size)[None, None]
        incoming = extended(outgoing, (("gx", 0), ("gy", 1)), 1)
        image = field[0, 0] + contrib[:owned]
        image = (
            image + incoming[0, 1, 0] + incoming[2, 1, 1] + incoming[1, 0, 2] + incoming[1, 2, 3]
        )
        return image[None, None]

    multipliers = jnp.zeros_like(dual_rhs)
    residual = dual_rhs
    direction = scaling * residual
    norm_now = weighted_norm(residual, direction)
    for sweep_index in range(ITERS):
        image = operate(direction)
        alpha = norm_now / lax.psum(jnp.sum(direction * image), ("gx", "gy"))
        multipliers = multipliers + alpha * direction
        residual = dual_rhs - operate(multipliers)
        precond = scaling * residual
        norm_next = weighted_norm(residual, precond)
        direction = precond + norm_next / norm_now * direction
        norm_now = norm_next
    return (multipliers, residual)


def solution(mesh):
    return jax.shard_map(
        shards,
        mesh=mesh,
        in_specs=(
            P("gx", "gy", None, None, None),
            P("gx", "gy", None, None, None),
            P("gx", "gy", None, None),
            P("gx", None),
            P("gx", "gy", None, None),
            P("gx", "gy", None, None),
            P("gx", "gy", None, None),
            P("gx", "gy", None, None),
            P("gx", "gy"),
        ),
        out_specs=(P("gx", "gy", None, None), P("gx", "gy", None, None)),
        check_vma=False,
    )
```

profile of v0, /device:TPU:32, one launch (start us, length us, event | category | flops | bytes accessed | tf_op | source)
XLA Modules:
  0.0 1205.0 jit_solution(11194242693486896263)
XLA Ops:
  8.0 3.4 collective-permute-start.1
  11.4 5.8 collective-permute-start
  24.2 4.7 multiply_add_fusion
  31.6 4.4 collective-permute-done.2
  36.7 31.1 %psum.93 = f32[512]{0:T(512)S(1)} all-reduce(f32[512]{0:T(512)S(1)} %bitcast.1267), channel_id=1, replica_groups=mesh['gx'=32,'gy'=16] {'gy'}, use_global_device_ids=true, to_apply=%region_11.12 | all-reduce | flops 512 | bytes 4096 | tf_op jit(solution)/shard_map/psum | solution.py:82
  67.9 9.6 fusion.440
  77.5 64.2 %all-reduce.4.cloned.1.call-done = f32[512,512]{0,1:T(8,128)} async-done(((f32[512,512]{0,1:T(8,128)}), f32[512,512]{0,1:T(8,128)}) %all-reduce.4.cloned.1.call-update) | async-done | bytes 1048592 | tf_op jit(solution)/shard_map/psum | solution.py:65
  144.8 11.7 cholesky.103
  156.6 9.8 custom-call.32
  167.2 11.7 cholesky.215
  179.1 10.2 custom-call.33
  190.4 11.7 cholesky.236
  202.3 9.8 custom-call.34
  212.9 11.9 cholesky.253
  229.3 10.5 while.12
  239.9 40.1 %custom-call.40 = f32[4,128,128]{1,2,0:T(8,128)S(1)} custom-call(f32[4,128,128]{2,1,0:T(8,128)} %get-tuple-element.41), custom_call_target="InvertDiagBlocksLowerTriangular" | custom-call | tf_op jit(solution)/shard_map/jit(_cho_solve)/triangular_solve | solution.py:85
  283.8 4.6 collective-permute-start.5
  290.4 7.0 collective-permute-done.4
  298.7 3.0 collective-permute-start.6
  303.2 96.0 %all-reduce.1 = (f32[]{:T(128)}, f32[]{:T(128)}) all-reduce(f32[]{:T(128)} %get-tuple-element.72, f32[]{:T(128)} %get-tuple-element.71), channel_id=1, replica_groups=mesh['gx'=32,'gy'=16] {'gx','gy'}, use_global_device_ids=true, to_apply=%region_1.2 | all-reduce | flops 2 | bytes 16 | tf_op jit(solution)/shard_map/psum | solution.py:23
  400.5 4.0 collective-permute-start.9
  404.5 5.2 collective-permute-start.8
  413.6 4.8 collective-permute-done.10
  418.9 9.4 fusion.443
  428.7 26.0 %psum.95 = f32[512]{0:T(512)S(1)} all-reduce(f32[512]{0:T(512)S(1)} %bitcast.1268), channel_id=1, replica_groups=mesh['gx'=32,'gy'=16] {'gy'}, use_global_device_ids=true, to_apply=%region_14.16 | all-reduce | flops 512 | bytes 4096 | tf_op jit(solution)/shard_map/psum | solution.py:82
  458.5 7.5 collective-permute-start.13
  467.9 7.0 collective-permute-done.12
  476.2 3.0 collective-permute-start.14
  480.7 97.6 %psum.96 = f32[]{:T(128)} all-reduce(f32[]{:T(128)} %get-tuple-element.93), channel_id=1, replica_groups=mesh['gx'=32,'gy'=16] {'gx','gy'}, use_global_device_ids=true, to_apply=%region_16.18 | all-reduce | flops 1 | bytes 8 | tf_op jit(solution)/shard_map/psum | solution.py:23
  579.7 4.0 collective-permute-start.17
  583.6 5.2 collective-permute-start.16
  593.0 4.8 collective-permute-done.18
  598.3 9.4 fusion.446
  608.0 26.0 %psum.97 = f32[512]{0:T(512)S(1)} all-reduce(f32[512]{0:T(512)S(1)} %bitcast.1269), channel_id=1, replica_groups=mesh['gx'=32,'gy'=16] {'gy'}, use_global_device_ids=true, to_apply=%region_17.19 | all-reduce | flops 512 | bytes 4096 | tf_op jit(solution)/shard_map/psum | solution.py:82
  637.8 7.5 collective-permute-start.21
  647.3 7.0 collective-permute-done.20
  655.6 3.0 collective-permute-start.22
  660.1 97.6 %psum.98 = f32[]{:T(128)} all-reduce(f32[]{:T(128)} %fusion.229), channel_id=1, replica_groups=mesh['gx'=32,'gy'=16] {'gx','gy'}, use_global_device_ids=true, to_apply=%region_19.21 | all-reduce | flops 1 | bytes 8 | tf_op jit(solution)/shard_map/psum | solution.py:105
  759.0 4.0 collective-permute-start.25
  763.0 5.2 collective-permute-start.24
  772.1 4.8 collective-permute-done.26
  777.4 9.4 fusion.449
  787.1 26.0 %psum.99 = f32[512]{0:T(512)S(1)} all-reduce(f32[512]{0:T(512)S(1)} %bitcast.1270), channel_id=1, replica_groups=mesh['gx'=32,'gy'=16] {'gy'}, use_global_device_ids=true, to_apply=%region_20.22 | all-reduce | flops 512 | bytes 4096 | tf_op jit(solution)/shard_map/psum | solution.py:82
  816.9 7.5 collective-permute-start.29
  826.4 7.0 collective-permute-done.28
  834.7 3.0 collective-permute-start.30
  839.2 97.8 %psum.100 = f32[]{:T(128)} all-reduce(f32[]{:T(128)} %get-tuple-element.87), channel_id=1, replica_groups=mesh['gx'=32,'gy'=16] {'gx','gy'}, use_global_device_ids=true, to_apply=%region_22.24 | all-reduce | flops 1 | bytes 8 | tf_op jit(solution)/shard_map/psum | solution.py:23
  938.4 4.0 collective-permute-start.33
  942.4 5.2 collective-permute-start.32
  951.5 4.8 collective-permute-done.34
  956.8 9.4 fusion.452
  966.5 26.0 %psum.101 = f32[512]{0:T(512)S(1)} all-reduce(f32[512]{0:T(512)S(1)} %bitcast.1271), channel_id=1, replica_groups=mesh['gx'=32,'gy'=16] {'gy'}, use_global_device_ids=true, to_apply=%region_23.25 | all-reduce | flops 512 | bytes 4096 | tf_op jit(solution)/shard_map/psum | solution.py:82
  996.3 7.5 collective-permute-start.37
  1005.8 7.0 collective-permute-done.36
  1014.1 3.0 collective-permute-start.38
  1018.6 97.6 %psum.102 = f32[]{:T(128)} all-reduce(f32[]{:T(128)} %fusion.216), channel_id=1, replica_groups=mesh['gx'=32,'gy'=16] {'gx','gy'}, use_global_device_ids=true, to_apply=%region_25.27 | all-reduce | flops 1 | bytes 8 | tf_op jit(solution)/shard_map/psum | solution.py:105
  1117.5 4.0 collective-permute-start.41
  1121.5 5.2 collective-permute-start.40
  1130.6 4.8 collective-permute-done.42
  1135.7 9.4 fusion.455
  1145.7 26.0 %psum.103 = f32[512]{0:T(512)S(1)} all-reduce(f32[512]{0:T(512)S(1)} %bitcast.1272), channel_id=1, replica_groups=mesh['gx'=32,'gy'=16] {'gy'}, use_global_device_ids=true, to_apply=%region_26.28 | all-reduce | flops 512 | bytes 4096 | tf_op jit(solution)/shard_map/psum | solution.py:82
  1175.5 7.5 collective-permute-start.45
  1184.9 7.0 collective-permute-done.44
  1193.2 3.0 collective-permute-start.46
  (322 shorter events, 103.8 us)
Async XLA Ops:
  7.2 16.1 %copy-start = (bf16[1,1,2,128,1024]{4,3,2,1,0:T(8,128)(2,1)S(1)}, bf16[1,1,2,128,1024]{4,3,2,1,0:T(8,128)(2,1)}, u32[]{:S(2)}) copy-start(bf16[1,1,2,128,1024]{4,3,2,1,0:T(8,128)(2,1)} %param.11) | copy-start | bytes 1572868
  7.2 134.5 %all-reduce.4.cloned.1.call-start = ((), (), s32[]{:S(2)}) async-start(), calls=%async_computation | async-start | bytes 2097152 | tf_op jit(solution)/shard_map/psum | solution.py:65
  8.0 20.9 %collective-permute-start.1 = (f32[1,1,8,128]{3,2,1,0:T(8,128)S(1)}, f32[1,1,8,128]{3,2,1,0:T(8,128)S(1)}, u32[]{:S(2)}, u32[]{:S(2)}) collective-permute-start(f32[1,1,8,128]{3,2,1,0:T(8,128)S(1)} %get-tuple-element.98), channel_id=1, source_target_pairs={{0,16},{16,32},{32,48},{48,64},{64,80},{80,96},{96,112},{112,128},... | collective-permute-start | bytes 12296 | tf_op jit(solution)/shard_map/ppermute | solution.py:14
  11.4 17.5 %collective-permute-start = (f32[1,1,8,128]{3,2,1,0:T(8,128)S(1)}, f32[1,1,8,128]{3,2,1,0:T(8,128)S(1)}, u32[]{:S(2)}, u32[]{:S(2)}) collective-permute-start(f32[1,1,8,128]{3,2,1,0:T(8,128)S(1)} %get-tuple-element.98), channel_id=1, source_target_pairs={{16,0},{32,16},{48,32},{64,48},{80,64},{96,80},{112,96},{128,112},... | collective-permute-start | bytes 12296 | tf_op jit(solution)/shard_map/ppermute | solution.py:17
  24.2 11.7 copy-start.5
  24.2 12.3 %copy-start.6 = (s32[1,1,2,24]{3,2,1,0:T(2,128)S(1)}, s32[1,1,2,24]{3,2,1,0:T(2,128)}, u32[]{:S(2)}) copy-start(s32[1,1,2,24]{3,2,1,0:T(2,128)} %param.18) | copy-start | bytes 580
  28.9 112.8 %copy-start.4 = (f32[1,512]{1,0:T(1,128)S(1)}, f32[1,512]{1,0:T(1,128)}, u32[]{:S(2)}) copy-start(f32[1,512]{1,0:T(1,128)} %param.14) | copy-start | bytes 6148
  28.9 7.0 collective-permute-start.3
  30.2 5.7 collective-permute-start.2
  143.0 159.6 %copy-start.1 = (f32[1,1,8,128]{3,2,1,0:T(8,128)S(1)}, f32[1,1,8,128]{3,2,1,0:T(8,128)}, u32[]{:S(2)}) copy-start(f32[1,1,8,128]{3,2,1,0:T(8,128)} %param.16) | copy-start | bytes 12292
  229.2 250.9 %copy-start.2 = (f32[1,1,8,128]{3,2,1,0:T(8,128)S(1)}, f32[1,1,8,128]{3,2,1,0:T(8,128)}, u32[]{:S(2)}) copy-start(f32[1,1,8,128]{3,2,1,0:T(8,128)} %param.15) | copy-start | bytes 12292
  283.8 6.5 collective-permute-start.5
  288.4 9.0 collective-permute-start.4
  297.4 4.3 collective-permute-start.7
  298.7 3.9 collective-permute-start.6
  400.5 9.2 collective-permute-start.9
  404.5 6.5 collective-permute-start.8
  411.0 7.4 collective-permute-start.11
  412.3 6.1 collective-permute-start.10
  458.5 9.4 collective-permute-start.13
  466.0 9.0 collective-permute-start.12
  474.9 4.3 collective-permute-start.15
  476.2 3.9 collective-permute-start.14
  579.7 9.2 collective-permute-start.17
  583.6 6.5 collective-permute-start.16
  590.1 7.6 collective-permute-start.19
  591.6 6.1 collective-permute-start.18
  637.8 9.4 collective-permute-start.21
  645.3 9.0 collective-permute-start.20
  654.3 4.3 collective-permute-start.23
  655.6 3.9 collective-permute-start.22
  759.0 9.2 collective-permute-start.25
  763.0 6.5 collective-permute-start.24
  769.5 7.4 collective-permute-start.27
  770.8 6.1 collective-permute-start.26
  816.9 9.4 collective-permute-start.29
  824.5 9.0 collective-permute-start.28
  833.4 4.3 collective-permute-start.31
  834.7 3.9 collective-permute-start.30
  938.4 9.2 collective-permute-start.33
  942.4 6.5 collective-permute-start.32
  948.9 7.4 collective-permute-start.35
  950.2 6.1 collective-permute-start.34
  996.3 9.4 collective-permute-start.37
  1003.8 9.0 collective-permute-start.36
  1012.8 4.3 collective-permute-start.39
  1014.1 3.9 collective-permute-start.38
  1117.5 80.2 %copy-start.3 = (f32[1,1,8,128]{3,2,1,0:T(8,128)}, f32[1,1,8,128]{3,2,1,0:T(8,128)S(1)}, u32[]{:S(2)}) copy-start(f32[1,1,8,128]{3,2,1,0:T(8,128)S(1)} %get-tuple-element.84) | copy-start | bytes 12292
  1117.5 9.2 collective-permute-start.41
  1121.5 6.5 collective-permute-start.40
  1128.0 7.4 collective-permute-start.43
  1129.3 6.1 collective-permute-start.42
  1175.5 9.4 collective-permute-start.45
  1183.0 9.0 collective-permute-start.44
  1192.0 4.3 collective-permute-start.47
  1193.2 3.9 collective-permute-start.46
Sparse Core Ops, SparseCore 0:
  22.1 119.4 all-reduce.3
where the time goes:
time: 1210 us
  blocking collectives  648 us (54%)
  starting transfers between devices  150 us (12%)
  waiting for transfers between devices  146 us (12%)
  other arithmetic  128 us (11%)
  matrix products  95.9 us (8%)
  between operations  25.5 us (2%)
    psum x3, blocking collectives, weighted_norm(): return lax.psum(jnp.sum(residual * precond), ('gx', 'gy'))  291 us
    psum x2, blocking collectives, shards(): alpha = norm_now / lax.psum(jnp.sum(direction * image), ('gx', 'gy'))  195 us
    psum x6, blocking collectives, operate(): lax.psum(jnp.einsum('sco,sc->o', own_hot, corner_values, precision=highes...  161 us
    ppermute x24, starting transfers between devices, extended(): lax.ppermute(lax.slice_in_dim(block, 0, width, axis=dim), axis, backward)  89.3 us
    another operation x14, other arithmetic, shards(): lower = jnp.linalg.cholesky(system)  78.8 us
    psum x1, waiting for transfers between devices, shards(): lax.psum(jnp.einsum('sod,sdp->op', spread, own_hot, precision=highest), '...  64.2 us
    ppermute x24, starting transfers between devices, extended(): lax.ppermute(lax.slice_in_dim(block, block.shape[dim] - width, None, axis...  60.8 us
    dot_general x6, matrix products, operate(): result = jnp.einsum('sij,sj->si', schur, gathered, precision=highest)  56.7 us
  transfers between devices with their start and end apart: 49, of which 24 were waited for; matrix products, arithmetic and copies ran while one was open for 2% of the time, Pallas kernels for 0%

commit v1 on v0

v1 whole, which is shorter than its diff:
```python
import functools

import jax
import jax.numpy as jnp
from jax import lax
from jax.experimental import pallas as pl
from jax.experimental.pallas import tpu as pltpu
from jax.sharding import PartitionSpec as P

F32 = jnp.float32
BF16 = jnp.bfloat16
STEP = 0.00390625
LANES = 128
PIVOTS = 4


def iota(shape, dim):
    return lax.broadcasted_iota(jnp.int32, shape, dim)


def high(a, b):
    return jnp.dot(a, b, precision=lax.Precision.HIGHEST, preferred_element_type=F32)


def thirds(x):
    first = x.astype(BF16).astype(F32)
    rest = x - first
    second = rest.astype(BF16).astype(F32)
    return first, second, rest - second


def stacked(row):
    first, second, third = thirds(row)
    at = iota((16, 1), 0)
    rows = jnp.where(at == 0, first, jnp.where(at == 1, second, jnp.where(at == 2, third, 0.0)))
    return rows.astype(BF16)


def row_times(row, matrix, dim):
    out = lax.dot_general(
        stacked(row), matrix, (((1,), (dim,)), ((), ())), preferred_element_type=F32
    )
    return jnp.sum(out[:8], axis=0, keepdims=True)


def exact_times(x, hot):
    return sum(jnp.dot(piece.astype(BF16), hot, preferred_element_type=F32) for piece in thirds(x))


def inverse2(a, b, c):
    r = 1.0 / (a * c - b * b)
    return c * r, -b * r, a * r


def pivot_inverse(e):
    p = inverse2(e(0, 0), e(0, 1), e(1, 1))
    b = [[e(0, 2), e(0, 3)], [e(1, 2), e(1, 3)]]
    u = [
        [p[0] * b[0][j] + p[1] * b[1][j] for j in (0, 1)],
        [p[1] * b[0][j] + p[2] * b[1][j] for j in (0, 1)],
    ]
    s = inverse2(
        e(2, 2) - (b[0][0] * u[0][0] + b[1][0] * u[1][0]),
        e(2, 3) - (b[0][0] * u[0][1] + b[1][0] * u[1][1]),
        e(3, 3) - (b[0][1] * u[0][1] + b[1][1] * u[1][1]),
    )
    x = [[u[i][0] * s[0] + u[i][1] * s[1], u[i][0] * s[1] + u[i][1] * s[2]] for i in (0, 1)]
    p00 = p[0] + x[0][0] * u[0][0] + x[0][1] * u[0][1]
    p01 = p[1] + x[0][0] * u[1][0] + x[0][1] * u[1][1]
    p11 = p[2] + x[1][0] * u[1][0] + x[1][1] * u[1][1]
    return [
        [p00, p01, -x[0][0], -x[0][1]],
        [p01, p11, -x[1][0], -x[1][1]],
        [-x[0][0], -x[1][0], s[0], s[1]],
        [-x[0][1], -x[1][1], s[1], s[2]],
    ]


def small_inverse(a, n):
    lane = iota((1, n), 1)
    at8 = iota((8, 1), 0)
    for k in range(0, n, PIVOTS):
        rows = [a[k + i : k + i + 1, :] for i in range(PIVOTS)]
        cols = [jnp.broadcast_to(a[:, k + i : k + i + 1], (n, n)) for i in range(PIVOTS)]
        w = pivot_inverse(lambda i, j: cols[j][k + i : k + i + 1, :])
        inside = (lane >= k) & (lane < k + PIVOTS)
        units = [
            jnp.where(inside, jnp.where(lane == k + i, 1.0, 0.0), rows[i]) for i in range(PIVOTS)
        ]
        fresh = [sum(w[i][j] * units[j] for j in range(PIVOTS)) for i in range(PIVOTS)]
        base = jnp.where(inside, 0.0, a)
        for i in range(PIVOTS):
            base = base - cols[i] * fresh[i]
        v = k // 8 * 8
        block = base[v : v + 8]
        for i in range(PIVOTS):
            block = jnp.where(at8 == k + i - v, fresh[i], block)
        a = jnp.concatenate([x for x in (base[:v], block, base[v + 8 :]) if x.shape[0]], axis=0)
    return a


def setup_kernel(
    panel_hbm, corner_hbm, diag_hbm, place_hbm, map_hbm, count_hbm, scale_hbm, rhs_hbm, v_ref,
    scale_ref, rhs_ref, pack_ref, report_ref, rows_ref, facts_ref, panel_ref, corner_ref, diag_ref,
    place_ref, map_ref, count_ref, facts, sems,
):
    slots, rows, width = panel_ref.shape
    corners = corner_ref.shape[1]
    per = map_ref.shape[1]
    total = slots * corners
    at = slots * rows
    moves = (
        (scale_hbm, scale_ref),
        (rhs_hbm, rhs_ref),
        (corner_hbm, corner_ref),
        (place_hbm, place_ref),
        (map_hbm, map_ref),
        (count_hbm, count_ref),
        (diag_hbm, diag_ref),
        (panel_hbm, panel_ref),
    )
    copies = [pltpu.make_async_copy(a, b, sems.at[i]) for i, (a, b) in enumerate(moves)]
    for copy in copies:
        copy.start()
    pack_ref[at:, :] = jnp.zeros((16, width), F32)
    rows_ref[...] = jnp.zeros_like(rows_ref)
    facts[...] = jnp.zeros_like(facts)
    for copy in copies:
        copy.wait()
    v_ref[...] = scale_ref[...] * rhs_ref[...]
    pack_ref[at + 8 : at + 8 + slots, :] = diag_ref[...]
    lane = iota((1, LANES), 1)
    for s in range(slots):
        pack_ref[s * rows : (s + 1) * rows, :] = panel_ref[s].astype(F32)
        rows_ref[s * corners : (s + 1) * corners, :] = corner_ref[s].astype(F32)
        facts[s : s + 1, :corners] = place_ref[s : s + 1, :].astype(F32)
        facts[slots + s : slots + s + 1, :per] = map_ref[s : s + 1, :].astype(F32)
    for i in range(total // 8):
        pack_ref[at : at + 8, i * LANES : (i + 1) * LANES] = rows_ref[8 * i : 8 * i + 8, :]
    narrow = rows_ref[...].astype(BF16)
    square = lax.dot_general(
        narrow, narrow, (((1,), (1,)), ((), ())), preferred_element_type=F32
    )
    part = jnp.zeros((corners, LANES), F32)
    count = count_ref[0, 0]
    fact = jnp.where(lane == total + slots * per, count.astype(F32), 0.0)
    for s in range(slots):
        live = jnp.where(s < count, 1.0, 0.0)
        first = s * corners
        mine = (lane >= first) & (lane < first + corners)
        part = jnp.where(mine, square[first : first + corners, :] * live, part)
        row = facts[s : s + 1, :]
        column = jnp.sum(
            jnp.where(iota((corners, 1), 0) == lane, row, 0.0), axis=1, keepdims=True
        )
        part = jnp.where(lane == total + s, column, part)
        fact = fact + (pltpu.roll(row, first, 1) if s else row)
        fact = fact + pltpu.roll(facts[slots + s : slots + s + 1, :], total + s * per, 1)
    report_ref[:corners, :] = part
    report_ref[corners:, :] = jnp.broadcast_to(fact, (8, LANES))
    facts_ref[...] = jnp.broadcast_to(fact.astype(jnp.int32), (8, LANES))


def flipped(a, b):
    return lax.dot_general(
        a, b, (((1,), (1,)), ((), ())), precision=lax.Precision.HIGHEST, preferred_element_type=F32
    )


def split_inverse(m, n):
    h = n // 2
    a, b, bt, c = m[:h, :h], m[:h, h:], m[h:, :h], m[h:, h:]
    ai = small_inverse(a, h)
    u = high(ai, b)
    si = small_inverse(c - high(bt, u), h)
    x, xt = high(u, si), flipped(si, u)
    top = jnp.concatenate([ai + flipped(x, u), -x], axis=1)
    return jnp.concatenate([top, jnp.concatenate([-xt, si], axis=1)], axis=0)


def coarse_kernel(
    slots, corners, start, y_ref, gathered_ref, diag_ref, out_ref, rows_ref, places_ref, facts_ref,
    hot_ref, spread_ref,
):
    count = gathered_ref.shape[0]
    total = slots * corners
    n = diag_ref.shape[1]
    lane = iota((1, n), 1).astype(F32)
    for y in range(count):
        part = gathered_ref[y, start : start + corners, :]
        rows_ref[y : y + 1, :] = gathered_ref[y, start + corners : start + corners + 1, :]
        for s in range(slots):
            block = part[:, s * corners : (s + 1) * corners]
            place = part[:, total + s : total + s + 1]
            hot = jnp.where(place == lane, 1.0, 0.0)
            at = (y * slots + s) * corners
            hot_ref[at : at + corners, :] = hot
            spread_ref[at : at + corners, :] = exact_times(block, hot.astype(BF16))
    facts_ref[...] = jnp.zeros_like(facts_ref)
    for g, by in enumerate((0, 1, -1)):
        there = y_ref[0] + by
        y = jnp.clip(there, 0, count - 1)
        fact = gathered_ref[y, start + corners : start + corners + 1, :].astype(jnp.int32)
        facts_ref[g : g + 1, :] = jnp.where((there >= 0) & (there < count), fact, 0)
        part = gathered_ref[y, start : start + corners, :]
        for s in range(slots):
            at = g * total + s * corners
            places_ref[at : at + corners, :] = jnp.broadcast_to(
                part[:, total + s : total + s + 1], (corners, LANES)
            )
    hots = hot_ref[...].astype(BF16)
    system = jnp.where(iota((n, 1), 0) == iota((1, n), 1), diag_ref[...], 0.0)
    for piece in thirds(spread_ref[...]):
        system = system + lax.dot_general(
            hots, piece.astype(BF16), (((0,), (0,)), ((), ())), preferred_element_type=F32
        )
    out_ref[...] = system
    b = LANES

    def eliminate(k, carry):
        ro = pl.multiple_of(k * b, b)
        pivots = split_inverse(out_ref[pl.ds(ro, b), pl.ds(ro, b)], b)
        col = out_ref[:, pl.ds(ro, b)]
        out_ref[:, pl.ds(ro, b)] = jnp.zeros((n, b), F32)
        out_ref[pl.ds(ro, b), pl.ds(ro, b)] = jnp.where(iota((b, b), 0) == iota((b, b), 1), 1.0, 0.0)
        fresh = high(pivots, out_ref[pl.ds(ro, b), :])
        out_ref[pl.ds(ro, b), :] = jnp.zeros((b, n), F32)
        at = iota((n, 1), 0)
        others = jnp.where((at >= ro) & (at < ro + b), 0.0, col)
        out_ref[...] = out_ref[...] - high(others, fresh)
        out_ref[pl.ds(ro, b), :] = fresh
        return carry

    lax.fori_loop(0, n // b, eliminate, 0)


def fact_of(facts, slots, corners, per, g, s, b, owned):
    k = facts[g, slots * corners + s * per + b]
    live = jnp.where(s < facts[g, slots * corners + slots * per], 1.0, 0.0)
    return k, jnp.where(k < owned, live, -live)


def gathered_rows(slots, corners, per, owned, g, facts, cand, u_ref):
    for s in range(slots):
        for b in range(per):
            k, sign = fact_of(facts, slots, corners, per, g, s, b, owned)
            row = cand[pl.ds(g * 5 * owned + k, 1), :] * sign
            u_ref[g * slots + s : g * slots + s + 1, b * LANES : (b + 1) * LANES] = row


def before_kernel(slots, corners, per, sweep, groups, parts, v_ref, last_ref, corner_ref, facts_ref, *rest):
    rest, (pay_ref, cand, u_ref, facts, sem) = rest[:-5], rest[-5:]
    packs, halo, extra = rest[:groups], rest[groups : groups + parts], rest[groups + parts :]
    copy = pltpu.make_async_copy(facts_ref, facts, sem)
    copy.start()
    owned = v_ref.shape[0]
    total = slots * corners
    v = v_ref[...]
    if groups > 1:
        cand[...] = jnp.zeros_like(cand)
        cand[9 * owned : 10 * owned, :] = v
        cand[13 * owned : 14 * owned, :] = v
    for i, ref in enumerate((v_ref, *halo)):
        cand[i * owned : (i + 1) * owned, :] = ref[...]
        if i < 3:
            pay_ref[i * owned : (i + 1) * owned, :] = ref[...]
    at = iota((owned, 1), 0)
    lane = iota((1, LANES), 1)
    energy = jnp.sum(v * v, keepdims=True)
    pays = []
    copy.wait()
    for g in range(groups):
        pack = packs[g]
        rows = (pack.shape[0] - 16) // slots
        pay = jnp.zeros((1, LANES), F32)
        gathered_rows(slots, corners, per, owned, g, facts, cand, u_ref)
        for s in range(slots):
            live = jnp.where(s < facts[g, total + slots * per], 1.0, 0.0)
            u = u_ref[g * slots + s : g * slots + s + 1, :]
            t = row_times(u, pack[s * rows : (s + 1) * rows, :].astype(BF16), 1)
            energy = energy + jnp.sum(t * t, keepdims=True)
            weights = pack[slots * rows + 8 + s : slots * rows + 9 + s, :]
            energy = energy + jnp.sum(weights * u * u, keepdims=True)
            first = s * corners
            if g:
                j = slots * rows
                narrow = [
                    pack[j : j + 8, i * LANES : (i + 1) * LANES] for i in range(total // 8)
                ]
                narrow = jnp.concatenate(narrow + [jnp.zeros((LANES - total, LANES), F32)], axis=0)
            else:
                narrow = corner_ref[...]
            c = row_times(t, narrow.astype(BF16), 1) * live
            pay = jnp.where((lane >= first) & (lane < first + corners), c, pay)
        pays.append(pay)
    cross = jnp.sum(v * last_ref[...], keepdims=True)
    pay = pays[0]
    if groups == 1:
        pay = jnp.where(lane == total + 2 * sweep, energy, pay)
    pay = jnp.where(lane == total + 2 * sweep + 1, cross, pay)
    for ref in extra:
        if ref.shape[0] == 1:
            pay = pay + ref[...]
        else:
            pay_ref[4 * owned :, :] = ref[...]
    block = jnp.where(at == 0, pay, 0.0)
    for g in range(1, groups):
        block = jnp.where(at == g, pays[g], block)
    pay_ref[3 * owned : 4 * owned, :] = block


def after_kernel(
    slots, corners, per, sweep, partial, y_ref, gathered_ref, rows_ref, places_ref, facts_ref, inverse_ref,
    *rest,
):
    packs, rest = rest[:3], rest[3:]
    before, rest = rest[: 1 if sweep else 0], rest[1 if sweep else 0 :]
    late, (cand, u_ref, acc, facts, sem) = rest[4:-5], rest[-5:]
    mine, east, west, sums_ref = rest[:4]
    copy = pltpu.make_async_copy(facts_ref, facts, sem)
    copy.start()
    owned = mine.shape[0]
    total = slots * corners
    n = inverse_ref.shape[0]
    count = gathered_ref.shape[0]
    middle = y_ref[0]
    field = {}
    for by in (0, 1, -1, 2, -2):
        y = middle + by
        inside = jnp.where((y >= 0) & (y < count), 1.0, 0.0)
        p = jnp.clip(y, 0, count - 1)
        for i in range(3 if abs(by) < 2 else 1):
            field[by, i] = gathered_ref[p, i * owned : (i + 1) * owned, :] * inside
    for g, by in enumerate((0, 1, -1)):
        parts = (field[by, 0], field[by, 1], field[by, 2])
        parts += (field[by + 1, 0] if by < 2 else None, field[by - 1, 0])
        for i, part in enumerate(parts):
            at = (5 * g + i) * owned
            cand[at : at + owned, :] = part
    lane = iota((1, LANES), 1)
    at = iota((n, 1), 0)
    spread = jnp.zeros((n, LANES), F32)
    totals = jnp.zeros((1, LANES), F32)
    places = rows_ref[...].astype(jnp.int32)
    for p in range(count):
        row = gathered_ref[p, 3 * owned : 3 * owned + 1, :]
        if partial and p > 0:
            row = row + gathered_ref[p - 1, 3 * owned + 1 : 3 * owned + 2, :]
        if partial and p < count - 1:
            row = row + gathered_ref[p + 1, 3 * owned + 2 : 3 * owned + 3, :]
        totals = totals + row
        spread = spread + jnp.where(places[p : p + 1, :] == at, row, 0.0)
    right = jnp.sum(jnp.where(lane < total, spread, 0.0), axis=1, keepdims=True)
    coarse = jnp.sum(inverse_ref[...] * right, axis=0, keepdims=True)
    wide = iota((1, n), 1)
    right_row = jnp.sum(jnp.where(at == wide, right, 0.0), axis=0, keepdims=True)
    energy = jnp.sum(coarse * right_row, keepdims=True)
    totals = totals + jnp.where(lane == total + 2 * sweep, energy, 0.0)
    for ref in before:
        totals = totals + ref[...]
    sums_ref[...] = totals
    acc[...] = jnp.zeros_like(acc)
    acc[:owned, :] = field[0, 0]
    copy.wait()
    for g in range(3):
        gathered_rows(slots, corners, per, owned, g, facts, cand, u_ref)
    wide = wide.astype(F32)
    local = jnp.sum(field[0, 0] * field[0, 0], keepdims=True)
    for g in range(3):
        pack = packs[g]
        rows = (pack.shape[0] - 16) // slots
        tail = slots * rows
        for s in range(slots):
            panel = pack[s * rows : (s + 1) * rows, :].astype(BF16)
            u = u_ref[g * slots + s : g * slots + s + 1, :]
            t = row_times(u, panel, 1)
            weights = pack[tail + 8 + s : tail + 9 + s, :]
            if g == 0:
                local = local + jnp.sum(t * t, keepdims=True)
                local = local + jnp.sum(weights * u * u, keepdims=True)
            for i in range(corners // 8):
                first = s * corners + 8 * i
                place = places_ref[g * total + first : g * total + first + 8, :1]
                back = jnp.sum(jnp.where(place == wide, coarse, 0.0), axis=1, keepdims=True)
                j = first // 8
                part = pack[tail : tail + 8, j * LANES : (j + 1) * LANES]
                t = t + jnp.sum(back * part, axis=0, keepdims=True)
            w = row_times(t, panel, 0) + weights * u
            for b in range(per):
                k, sign = fact_of(facts, slots, corners, per, g, s, b, owned)
                acc[pl.ds(g * 5 * owned + k, 1), :] += w[:, b * LANES : (b + 1) * LANES] * sign
    mine[...] = acc[:owned, :] + acc[9 * owned : 10 * owned, :] + acc[13 * owned : 14 * owned, :]
    for ref in late:
        ref[...] = jnp.where(lane == total + 2 * sweep, local, 0.0)
    east[...] = acc[owned : 2 * owned, :]
    west[...] = acc[2 * owned : 3 * owned, :]


def final_kernel(first, gathered_ref, rhs_ref, v0, v1, v2, w0, w1, mine, east, west, x_ref, r_ref):
    sums = gathered_ref[...]
    lane = iota((1, LANES), 1)

    def moment(i):
        return jnp.sum(jnp.where(lane == first + i, sums, 0.0), axis=1, keepdims=True)

    h00, r0, h11, h01, h22, h12 = (moment(i) for i in range(6))
    h02, r1, r2 = h11, STEP * h00, STEP * h01
    l10, l20 = h01 / h00, h02 / h00
    d1 = h11 - l10 * h01
    e12 = h12 - l10 * h02
    l21 = e12 / d1
    d2 = h22 - l20 * h02 - l21 * e12
    y1 = r1 - l10 * r0
    y2 = r2 - l20 * r0 - l21 * y1
    c2 = y2 / d2
    c1 = y1 / d1 - l21 * c2
    c0 = r0 / h00 - l10 * c1 - l20 * c2
    w2 = mine[...] + east[...] + west[...]
    x_ref[...] = c0 * v0[...] + c1 * v1[...] + c2 * v2[...]
    r_ref[...] = rhs_ref[...] - (c0 * w0[...] + c1 * w1[...] + c2 * w2)


def call(kernel, name, outs, scratch, scalars, arrays, space=pltpu.VMEM):
    vmem = pl.BlockSpec(memory_space=pltpu.VMEM)
    smem = pl.BlockSpec(memory_space=pltpu.SMEM)
    outs = [x if isinstance(x, jax.ShapeDtypeStruct) else jax.ShapeDtypeStruct(x, F32) for x in outs]
    return pl.pallas_call(
        kernel,
        out_shape=outs,
        in_specs=[smem] * len(scalars) + [pl.BlockSpec(memory_space=space)] * len(arrays),
        out_specs=[vmem] * len(outs),
        scratch_shapes=[pltpu.VMEM(x, F32) if isinstance(x, tuple) else x for x in scratch],
        compiler_params=pltpu.CompilerParams(vmem_limit_bytes=40 << 20),
        name=name,
    )(*scalars, *arrays)


def moved(x, axis, by):
    count = lax.axis_size(axis)
    return lax.ppermute(x, axis, [(i, i + by) for i in range(count) if 0 <= i + by < count])


def strided(count, by):
    return [list(range(i, count, by)) for i in range(by)]


def runs(count, size):
    return [list(range(i, i + size)) for i in range(0, count, size)]


def shards(
    panel, corner_panel, interface_diag, coarse_diag, scaling, dual_rhs, block_map, corner_map, counts
):
    slots, rows, width = panel.shape[2:]
    corners = corner_panel.shape[3]
    owned, block_size = scaling.shape[2:]
    n = coarse_diag.shape[1]
    total = slots * corners
    peers = lax.axis_size("gy")
    y = lax.axis_index("gy")
    per = block_map.shape[3]
    tile = (owned, block_size)
    facts_shape = jax.ShapeDtypeStruct((8, LANES), jnp.int32)
    facts_scratch = [pltpu.SMEM((8, LANES), jnp.int32), pltpu.SemaphoreType.DMA]
    direction, scale, rhs, pack, report, corner_rows, facts = call(
        setup_kernel,
        "setup",
        [
            tile,
            tile,
            tile,
            (slots * rows + 16, width),
            (corners + 8, LANES),
            (LANES, LANES),
            facts_shape,
        ],
        [
            pltpu.VMEM((slots, rows, width), BF16),
            pltpu.VMEM((slots, corners, rows), BF16),
            (slots, width),
            pltpu.VMEM((slots, corners), jnp.int32),
            pltpu.VMEM((slots, per), jnp.int32),
            pltpu.SMEM((1, 1), jnp.int32),
            (8, LANES),
            pltpu.SemaphoreType.DMA((8,)),
        ],
        [],
        [
            panel[0, 0],
            corner_panel[0, 0],
            interface_diag[0, 0],
            corner_map[0, 0],
            block_map[0, 0],
            counts,
            scaling[0, 0],
            dual_rhs[0, 0],
        ],
        space=pltpu.HBM,
    )
    last = rhs
    directions, images, sums = [], [], []
    packs, late = [pack], []
    for sweep in range(3):
        partial = sweep == 1
        halo = [moved(direction, "gx", -1), moved(direction, "gx", 1)]
        if not partial:
            halo += [moved(direction, "gy", -1), moved(direction, "gy", 1)]
        extra = late if sweep else [report]
        size = 4 * owned + (0 if sweep else report.shape[0])
        groups = 3 if partial else 1
        (pay,) = call(
            functools.partial(before_kernel, slots, corners, per, sweep, groups, len(halo)),
            "before",
            [(size, LANES)],
            [(5 * groups * owned, block_size), (8, width), *facts_scratch],
            [],
            [
                direction,
                last,
                corner_rows,
                facts3 if partial else facts,
                *packs[:groups],
                *halo,
                *extra,
            ],
        )
        gathered = lax.all_gather(pay, "gy")
        if not sweep:
            gathered, leaving = lax.optimization_barrier((gathered, pack))
            packs = [pack, moved(leaving, "gy", -1), moved(leaving, "gy", 1)]
            here = y.reshape(1).astype(jnp.int32)
            inverse, place_rows, places3, facts3 = call(
                functools.partial(coarse_kernel, slots, corners, 4 * owned),
                "coarse",
                [(n, n), (peers, LANES), (3 * total, LANES), facts_shape],
                [(peers * total, n), (peers * total, n)],
                [here],
                [gathered, coarse_diag],
            )
        mine, east, west, sums, *late = call(
            functools.partial(after_kernel, slots, corners, per, sweep, partial),
            "after",
            [tile] * 3 + [(1, LANES)] * (2 if partial else 1),
            [(15 * owned, block_size), (8, width), (15 * owned, block_size), *facts_scratch],
            [here],
            [gathered, place_rows, places3, facts3, inverse, *packs, *([sums] if sweep else [])],
        )
        arrived = [moved(east, "gx", 1), moved(west, "gx", -1)]
        directions.append(direction)
        if sweep < 2:
            image = mine + arrived[0] + arrived[1]
            images.append(image)
            last, direction = image, STEP * scale * image
    sums, *arrived = lax.optimization_barrier((sums, *arrived))
    across = lax.axis_size("gx")
    for group in (runs(across, 4), strided(across, 4)):
        sums = lax.all_gather(sums, "gx", axis=0, tiled=True, axis_index_groups=group)
        sums = jnp.sum(sums, axis=0, keepdims=True)
    multipliers, residual = call(
        functools.partial(final_kernel, total),
        "final",
        [tile] * 2,
        [],
        [],
        [sums, rhs, *directions, *images, mine, *arrived],
    )
    return multipliers[None, None], residual[None, None]


def solution(mesh):
    return jax.shard_map(
        shards,
        mesh=mesh,
        in_specs=(
            P("gx", "gy", None, None, None),
            P("gx", "gy", None, None, None),
            P("gx", "gy", None, None),
            P("gx", None),
            P("gx", "gy", None, None),
            P("gx", "gy", None, None),
            P("gx", "gy", None, None),
            P("gx", "gy", None, None),
            P("gx", "gy"),
        ),
        out_specs=(P("gx", "gy", None, None), P("gx", "gy", None, None)),
        check_vma=False,
    )
```

time: 1210 us -> 220 us (0.18)
  blocking collectives: 648 us -> 90.6 us
  waiting for transfers between devices: 146 us -> 7.76 us
  other arithmetic: 128 us -> 0.06 us
  matrix products: 95.9 us -> 0 us
  starting transfers between devices: 150 us -> 65.5 us
  Pallas kernels: 0 us -> 47 us
  between operations: 25.5 us -> 1.62 us
    psum x11 -> x0, blocking collectives: 648 us -> none  [the longest x3 291 us: weighted_norm(): return lax.psum(jnp.sum(residual * precond), ('gx', 'gy'))]
    another operation x18 -> x0, other arithmetic: 119 us -> none  [the longest x14 78.8 us: shards(): lower = jnp.linalg.cholesky(system)]
    all_gather x0 -> x5, blocking collectives: none -> 90.6 us  [the longest x3 64.4 us: shards(): gathered = lax.all_gather(pay, 'gy')]
    ppermute x48 -> x18, starting transfers between devices: 150 us -> 65.5 us  [moved(): lax.ppermute(x, axis, [(i, i + by) for i in range(count) if 0 <= i + by <...]
    dot_general x47 -> x0, matrix products: 76.1 us -> none  [the longest x6 56.7 us: operate(): result = jnp.einsum('sij,sj->si', schur, gathered, precision=highest)]
    ppermute x48 -> x18, waiting for transfers between devices: 82.2 us -> 7.76 us  [moved(): lax.ppermute(x, axis, [(i, i + by) for i in range(count) if 0 <= i + by <...]
    psum x1 -> x0, waiting for transfers between devices: 64.2 us -> none  [shards(): lax.psum(jnp.einsum('sod,sdp->op', spread, own_hot, precision=highest), '...]
    pallas_call x0 -> x9, Pallas kernels: none -> 47 us  [call(): pl.pallas_call(kernel, out_shape=outs, in_specs=[smem] * len(scalars) + [...]
  transfers between devices with their start and end apart: 49 -> 18, of which waited for: 24 -> 6; matrix products, arithmetic and copies ran while one was open for 2% -> 0% of each run, Pallas kernels for 0% -> 15%
where the time goes in v1:
time: 220 us; the launch traced here: 219 us
  blocking collectives  90.6 us (41%)
  starting transfers between devices  65.5 us (30%)
  Pallas kernels  47 us (21%)
  waiting for transfers between devices  7.76 us (4%)
  local copies, waits for them, and re-layouts  6.21 us (3%)
    ppermute x18, starting transfers between devices, moved(): lax.ppermute(x, axis, [(i, i + by) for i in range(count) if 0 <= i + by <...  65.5 us
    all_gather x3, blocking collectives, shards(): gathered = lax.all_gather(pay, 'gy')  64.4 us
    pallas_call x9, Pallas kernels, call(): pl.pallas_call(kernel, out_shape=outs, in_specs=[smem] * len(scalars) + [...  47 us
    all_gather x2, blocking collectives, shards(): lax.all_gather(sums, 'gx', axis=0, tiled=True, axis_index_groups=group)  26.2 us
    ppermute x18, waiting for transfers between devices, moved(): lax.ppermute(x, axis, [(i, i + by) for i in range(count) if 0 <= i + by <...  7.76 us
    unnamed x18, local copies, waits for them, and re-layouts  6.21 us
  transfers between devices with their start and end apart: 18, of which 6 were waited for; matrix products, arithmetic and copies ran while one was open for 0% of the time, Pallas kernels for 15%

profile of v1, /device:TPU:32, one launch (start us, length us, event | category | flops | bytes accessed | tf_op | source)
XLA Modules:
  0.0 218.8 jit_solution(6216718288931245766)
XLA Ops:
  1.3 0.0 copy-start.1
  1.3 1.0 copy-done.1
  2.3 0.0 copy-start.2
  2.3 0.7 copy-done.2
  3.0 0.0 copy-start.3
  3.0 0.7 copy-done.3
  3.7 0.0 copy-start.4
  3.7 0.7 copy-done.4
  4.4 0.7 copy-done.5
  5.1 0.7 copy-done.7
  5.8 0.7 copy-done.8
  6.5 0.8 setup.1
  7.3 1.7 collective-permute-start.3
  9.1 1.3 collective-permute-start.2
  10.4 3.4 %collective-permute-start.1 = (f32[8,128]{1,0:T(8,128)S(1)}, f32[8,128]{1,0:T(8,128)S(1)}, u32[]{:S(2)}, u32[]{:S(2)}) collective-permute-start(f32[8,128]{1,0:T(8,128)S(1)} %get-tuple-element.34.v_ref.v0), channel_id=1, source_target_pairs={{0,16},{16,32},{32,48},{48,64},{64,80},{80,96},{96,112},{112,128},... | collective-permute-start | bytes 12296 | tf_op jit(solution)/shard_map/ppermute | solution.py:440
  13.8 5.8 %collective-permute-start = (f32[8,128]{1,0:T(8,128)S(1)}, f32[8,128]{1,0:T(8,128)S(1)}, u32[]{:S(2)}, u32[]{:S(2)}) collective-permute-start(f32[8,128]{1,0:T(8,128)S(1)} %get-tuple-element.34.v_ref.v0), channel_id=1, source_target_pairs={{16,0},{32,16},{48,32},{64,48},{80,64},{96,80},{112,96},{128,112},... | collective-permute-start | bytes 12296 | tf_op jit(solution)/shard_map/ppermute | solution.py:440
  19.5 0.0 collective-permute-done.3.rest_4_
  19.5 0.0 collective-permute-done.2.rest_3_
  19.6 0.0 collective-permute-done.1.rest_2_
  19.6 1.3 collective-permute-done.rest_1_
  20.8 1.3 before.3
  22.1 28.5 %all-gather = f32[1024,128]{1,0:T(8,128)} all-gather(f32[64,128]{1,0:T(8,128)S(1)} %before.3), channel_id=2, replica_groups=mesh['gx'=32,'gy'=16] {'gy'}, dimensions={0}, use_global_device_ids=true | all-gather | bytes 557056 | tf_op jit(solution)/shard_map/all_gather | solution.py:527
  50.7 2.3 %collective-permute-start.5 = (f32[272,1024]{1,0:T(8,128)S(1)}, f32[272,1024]{1,0:T(8,128)S(1)}, u32[]{:S(2)}, u32[]{:S(2)}) collective-permute-start(f32[272,1024]{1,0:T(8,128)S(1)} %get-tuple-element.45.rest_0_), channel_id=1, source_target_pairs={{0,1},{1,2},{2,3},{3,4},{4,5},{5,6},{6,7},{7,8},{8,9},{9,10},{10,1... | collective-permute-start | bytes 3342344 | tf_op jit(solution)/shard_map/ppermute | solution.py:440
  53.0 1.3 collective-permute-start.4
  54.3 0.0 copy-done.6
  54.3 0.0 copy-start
  54.3 1.0 copy-done
  55.3 32.1 %coarse.1 = (f32[512,512]{1,0:T(8,128)S(1)}, f32[16,128]{1,0:T(8,128)S(1)}, f32[144,128]{1,0:T(8,128)S(1)}, s32[8,128]{1,0:T(8,128)S(1)}) custom-call(s32[1]{0:T(128)} %bitcast.y_ref, f32[16,64,128]{2,1,0:T(8,128)S(1)} %bitcast.16, f32[1,512]{1,0:T(1,128)S(1)} %copy-done.6), custom_call_target="tpu_custom_call" | custom-call | tf_op jit(solution)/shard_map/coarse/pallas_call | solution.py:427
  87.5 0.0 collective-permute-done.5.rest_2_
  87.5 0.0 collective-permute-done.4.rest_1_
  87.5 2.8 %after.3 = (f32[8,128]{1,0:T(8,128)S(1)}, f32[8,128]{1,0:T(8,128)S(1)}, f32[8,128]{1,0:T(8,128)S(1)}, f32[1,128]{1,0:T(1,128)S(1)}) custom-call(s32[1]{0:T(128)} %bitcast.y_ref, f32[16,64,128]{2,1,0:T(8,128)S(1)} %bitcast.17, f32[16,128]{1,0:T(8,128)S(1)} %get-tuple-element.41.rows_ref, f32[144,128]{1,0:T(8,128)S(1)} %get-tuple-element.42.places_ref, ...), custom_call_target="tpu_custom_call" | custom-call | tf_op jit(solution)/shard_map/after/pallas_call | solution.py:427
  90.3 1.9 collective-permute-start.6
  92.2 7.5 %collective-permute-start.7 = (f32[8,128]{1,0:T(8,128)S(1)}, f32[8,128]{1,0:T(8,128)S(1)}, u32[]{:S(2)}, u32[]{:S(2)}) collective-permute-start(f32[8,128]{1,0:T(8,128)S(1)} %get-tuple-element.48), channel_id=1, source_target_pairs={{16,0},{32,16},{48,32},{64,48},{80,64},{96,80},{112,96},{128,112},... | collective-permute-start | bytes 12296 | tf_op jit(solution)/shard_map/ppermute | solution.py:440
  99.7 0.0 collective-permute-done.6
  99.7 1.3 collective-permute-done.7
  101.0 1.9 collective-permute-start.9
  103.0 7.5 %collective-permute-start.8 = (f32[8,128]{1,0:T(8,128)S(1)}, f32[8,128]{1,0:T(8,128)S(1)}, u32[]{:S(2)}, u32[]{:S(2)}) collective-permute-start(f32[8,128]{1,0:T(8,128)S(1)} %get-tuple-element.66.v_ref.v1), channel_id=1, source_target_pairs={{16,0},{32,16},{48,32},{64,48},{80,64},{96,80},{112,96},{128,112},... | collective-permute-start | bytes 12296 | tf_op jit(solution)/shard_map/ppermute | solution.py:440
  110.5 0.0 collective-permute-done.9.rest_4_
  110.5 1.3 collective-permute-done.8.rest_3_
  111.8 2.3 %before.4 = f32[32,128]{1,0:T(8,128)S(1)} custom-call(f32[8,128]{1,0:T(8,128)S(1)} %get-tuple-element.66.v_ref.v1, f32[8,128]{1,0:T(8,128)S(1)} %get-tuple-element.67.last_ref.w0, f32[128,128]{1,0:T(8,128)S(1)} %get-tuple-element.36.corner_ref, s32[8,128]{1,0:T(8,128)S(1)} %get-tuple-element.43.facts_ref, f32[272,1024]{1,0:T(8,128)S(1)} %get-tuple-element.45.rest_0_, ...), custom_call_target="tpu_custom_call" | custom-call | tf_op jit(solution)/shard_map/before/pallas_call | solution.py:427
  114.1 17.2 %all-gather.1 = f32[512,128]{1,0:T(8,128)S(1)} all-gather(f32[32,128]{1,0:T(8,128)S(1)} %before.4), channel_id=3, replica_groups=mesh['gx'=32,'gy'=16] {'gy'}, dimensions={0}, use_global_device_ids=true | all-gather | bytes 278528 | tf_op jit(solution)/shard_map/all_gather | solution.py:527
  131.3 2.9 %after.4 = (f32[8,128]{1,0:T(8,128)S(1)}, f32[8,128]{1,0:T(8,128)S(1)}, f32[8,128]{1,0:T(8,128)S(1)}, f32[1,128]{1,0:T(1,128)S(1)}, f32[1,128]{1,0:T(1,128)S(1)}) custom-call(s32[1]{0:T(128)} %bitcast.y_ref, f32[16,32,128]{2,1,0:T(8,128)S(1)} %bitcast.19, f32[16,128]{1,0:T(8,128)S(1)} %get-tuple-element.41.rows_ref, ...), custom_call_target="tpu_custom_call" | custom-call | tf_op jit(solution)/shard_map/after/pallas_call | solution.py:427
  134.2 1.9 collective-permute-start.10
  136.1 7.5 %collective-permute-start.11 = (f32[8,128]{1,0:T(8,128)S(1)}, f32[8,128]{1,0:T(8,128)S(1)}, u32[]{:S(2)}, u32[]{:S(2)}) collective-permute-start(f32[8,128]{1,0:T(8,128)S(1)} %get-tuple-element.52), channel_id=1, source_target_pairs={{16,0},{32,16},{48,32},{64,48},{80,64},{96,80},{112,96},{128,112},... | collective-permute-start | bytes 12296 | tf_op jit(solution)/shard_map/ppermute | solution.py:440
  143.6 0.0 collective-permute-done.10
  143.6 1.3 collective-permute-done.11
  144.9 1.4 collective-permute-start.15
  146.3 1.3 collective-permute-start.14
  147.6 1.9 collective-permute-start.13
  149.5 7.4 %collective-permute-start.12 = (f32[8,128]{1,0:T(8,128)S(1)}, f32[8,128]{1,0:T(8,128)S(1)}, u32[]{:S(2)}, u32[]{:S(2)}) collective-permute-start(f32[8,128]{1,0:T(8,128)S(1)} %get-tuple-element.64.v_ref.v2), channel_id=1, source_target_pairs={{16,0},{32,16},{48,32},{64,48},{80,64},{96,80},{112,96},{128,112},... | collective-permute-start | bytes 12296 | tf_op jit(solution)/shard_map/ppermute | solution.py:440
  157.0 0.0 collective-permute-done.15.rest_4_
  157.0 0.0 collective-permute-done.14.rest_3_
  157.0 0.0 collective-permute-done.13.rest_2_
  157.0 1.3 collective-permute-done.12.rest_1_
  158.3 1.3 before.5
  159.6 18.7 %all-gather.2 = f32[512,128]{1,0:T(8,128)S(1)} all-gather(f32[32,128]{1,0:T(8,128)S(1)} %before.5), channel_id=4, replica_groups=mesh['gx'=32,'gy'=16] {'gy'}, dimensions={0}, use_global_device_ids=true | all-gather | bytes 278528 | tf_op jit(solution)/shard_map/all_gather | solution.py:527
  178.2 2.8 %after.5 = (f32[8,128]{1,0:T(8,128)S(1)}, f32[8,128]{1,0:T(8,128)S(1)}, f32[8,128]{1,0:T(8,128)S(1)}, f32[1,128]{1,0:T(1,128)S(1)}) custom-call(s32[1]{0:T(128)} %bitcast.y_ref, f32[16,32,128]{2,1,0:T(8,128)S(1)} %bitcast.18, f32[16,128]{1,0:T(8,128)S(1)} %get-tuple-element.41.rows_ref, f32[144,128]{1,0:T(8,128)S(1)} %get-tuple-element.42.places_ref, ...), custom_call_target="tpu_custom_call" | custom-call | tf_op jit(solution)/shard_map/after/pallas_call | solution.py:427
  181.1 1.9 collective-permute-start.16
  183.0 7.5 %collective-permute-start.17 = (f32[8,128]{1,0:T(8,128)S(1)}, f32[8,128]{1,0:T(8,128)S(1)}, u32[]{:S(2)}, u32[]{:S(2)}) collective-permute-start(f32[8,128]{1,0:T(8,128)S(1)} %get-tuple-element.57), channel_id=1, source_target_pairs={{16,0},{32,16},{48,32},{64,48},{80,64},{96,80},{112,96},{128,112},... | collective-permute-start | bytes 12296 | tf_op jit(solution)/shard_map/ppermute | solution.py:440
  190.5 0.0 collective-permute-done.16.east
  190.5 1.3 collective-permute-done.17.west
  191.8 6.9 %all-gather.4 = f32[4,1,128]{2,1,0:T(1,128)S(1)} all-gather(f32[1,1,128]{2,1,0:T(1,128)S(1)} %bitcast.28), channel_id=1, replica_groups={{0,16,32,48},{64,80,96,112},{128,144,160,176},{192,208,224,240},{256,27..., dimensions={0}, use_global_device_ids=true | all-gather | bytes 2560 | tf_op jit(solution)/shard_map/all_gather | solution.py:557
  198.7 19.3 %all-gather.5 = f32[8,1,128]{2,1,0:T(1,128)S(1)} all-gather(f32[1,1,128]{2,1,0:T(1,128)S(1)} %bitcast.29), channel_id=5, replica_groups={{0,64,128,192,256,320,384,448},{16,80,144,208,272,336,400,464},{32,96,1..., dimensions={0}, use_global_device_ids=true | all-gather | bytes 4608 | tf_op jit(solution)/shard_map/all_gather | solution.py:557
  218.1 0.7 final.1
  (8 shorter events, 0.1 us)
Async XLA Ops:
  1.3 1.0 copy-start.1
  2.3 0.7 copy-start.2
  3.0 0.7 copy-start.3
  3.7 0.7 copy-start.4
  4.4 0.7 copy-start.5
  5.1 0.7 copy-start.7
  5.8 0.7 copy-start.8
  6.5 47.8 %copy-start.6 = (f32[1,512]{1,0:T(1,128)S(1)}, f32[1,512]{1,0:T(1,128)}, u32[]{:S(2)}) copy-start(f32[1,512]{1,0:T(1,128)} %diag_ref.1) | copy-start | bytes 6148
  7.3 12.2 %collective-permute-start.3 = (f32[8,128]{1,0:T(8,128)S(1)}, f32[8,128]{1,0:T(8,128)S(1)}, u32[]{:S(2)}, u32[]{:S(2)}) collective-permute-start(f32[8,128]{1,0:T(8,128)S(1)} %get-tuple-element.34.v_ref.v0), channel_id=1, source_target_pairs={{0,1},{1,2},{2,3},{3,4},{4,5},{5,6},{6,7},{7,8},{8,9},{9,10},{10,1... | collective-permute-start | bytes 12296 | tf_op jit(solution)/shard_map/ppermute | solution.py:440
  9.1 10.5 %collective-permute-start.2 = (f32[8,128]{1,0:T(8,128)S(1)}, f32[8,128]{1,0:T(8,128)S(1)}, u32[]{:S(2)}, u32[]{:S(2)}) collective-permute-start(f32[8,128]{1,0:T(8,128)S(1)} %get-tuple-element.34.v_ref.v0), channel_id=1, source_target_pairs={{1,0},{2,1},{3,2},{4,3},{5,4},{6,5},{7,6},{8,7},{9,8},{10,9},{11,1... | collective-permute-start | bytes 12296 | tf_op jit(solution)/shard_map/ppermute | solution.py:440
  10.4 9.2 %collective-permute-start.1 = (f32[8,128]{1,0:T(8,128)S(1)}, f32[8,128]{1,0:T(8,128)S(1)}, u32[]{:S(2)}, u32[]{:S(2)}) collective-permute-start(f32[8,128]{1,0:T(8,128)S(1)} %get-tuple-element.34.v_ref.v0), channel_id=1, source_target_pairs={{0,16},{16,32},{32,48},{48,64},{64,80},{80,96},{96,112},{112,128},... | collective-permute-start | bytes 12296 | tf_op jit(solution)/shard_map/ppermute | solution.py:440
  13.8 7.1 %collective-permute-start = (f32[8,128]{1,0:T(8,128)S(1)}, f32[8,128]{1,0:T(8,128)S(1)}, u32[]{:S(2)}, u32[]{:S(2)}) collective-permute-start(f32[8,128]{1,0:T(8,128)S(1)} %get-tuple-element.34.v_ref.v0), channel_id=1, source_target_pairs={{16,0},{32,16},{48,32},{64,48},{80,64},{96,80},{112,96},{128,112},... | collective-permute-start | bytes 12296 | tf_op jit(solution)/shard_map/ppermute | solution.py:440
  50.7 36.8 %collective-permute-start.5 = (f32[272,1024]{1,0:T(8,128)S(1)}, f32[272,1024]{1,0:T(8,128)S(1)}, u32[]{:S(2)}, u32[]{:S(2)}) collective-permute-start(f32[272,1024]{1,0:T(8,128)S(1)} %get-tuple-element.45.rest_0_), channel_id=1, source_target_pairs={{0,1},{1,2},{2,3},{3,4},{4,5},{5,6},{6,7},{7,8},{8,9},{9,10},{10,1... | collective-permute-start | bytes 3342344 | tf_op jit(solution)/shard_map/ppermute | solution.py:440
  53.0 34.5 %collective-permute-start.4 = (f32[272,1024]{1,0:T(8,128)S(1)}, f32[272,1024]{1,0:T(8,128)S(1)}, u32[]{:S(2)}, u32[]{:S(2)}) collective-permute-start(f32[272,1024]{1,0:T(8,128)S(1)} %get-tuple-element.45.rest_0_), channel_id=1, source_target_pairs={{1,0},{2,1},{3,2},{4,3},{5,4},{6,5},{7,6},{8,7},{9,8},{10,9},{11,1... | collective-permute-start | bytes 3342344 | tf_op jit(solution)/shard_map/ppermute | solution.py:440
  54.3 1.0 copy-start
  90.3 9.4 %collective-permute-start.6 = (f32[8,128]{1,0:T(8,128)S(1)}, f32[8,128]{1,0:T(8,128)S(1)}, u32[]{:S(2)}, u32[]{:S(2)}) collective-permute-start(f32[8,128]{1,0:T(8,128)S(1)} %get-tuple-element.47), channel_id=1, source_target_pairs={{0,16},{16,32},{32,48},{48,64},{64,80},{80,96},{96,112},{112,128},... | collective-permute-start | bytes 12296 | tf_op jit(solution)/shard_map/ppermute | solution.py:440
  92.2 8.8 %collective-permute-start.7 = (f32[8,128]{1,0:T(8,128)S(1)}, f32[8,128]{1,0:T(8,128)S(1)}, u32[]{:S(2)}, u32[]{:S(2)}) collective-permute-start(f32[8,128]{1,0:T(8,128)S(1)} %get-tuple-element.48), channel_id=1, source_target_pairs={{16,0},{32,16},{48,32},{64,48},{80,64},{96,80},{112,96},{128,112},... | collective-permute-start | bytes 12296 | tf_op jit(solution)/shard_map/ppermute | solution.py:440
  101.0 9.4 %collective-permute-start.9 = (f32[8,128]{1,0:T(8,128)S(1)}, f32[8,128]{1,0:T(8,128)S(1)}, u32[]{:S(2)}, u32[]{:S(2)}) collective-permute-start(f32[8,128]{1,0:T(8,128)S(1)} %get-tuple-element.66.v_ref.v1), channel_id=1, source_target_pairs={{0,16},{16,32},{32,48},{48,64},{64,80},{80,96},{96,112},{112,128},... | collective-permute-start | bytes 12296 | tf_op jit(solution)/shard_map/ppermute | solution.py:440
  103.0 8.8 %collective-permute-start.8 = (f32[8,128]{1,0:T(8,128)S(1)}, f32[8,128]{1,0:T(8,128)S(1)}, u32[]{:S(2)}, u32[]{:S(2)}) collective-permute-start(f32[8,128]{1,0:T(8,128)S(1)} %get-tuple-element.66.v_ref.v1), channel_id=1, source_target_pairs={{16,0},{32,16},{48,32},{64,48},{80,64},{96,80},{112,96},{128,112},... | collective-permute-start | bytes 12296 | tf_op jit(solution)/shard_map/ppermute | solution.py:440
  134.2 9.4 %collective-permute-start.10 = (f32[8,128]{1,0:T(8,128)S(1)}, f32[8,128]{1,0:T(8,128)S(1)}, u32[]{:S(2)}, u32[]{:S(2)}) collective-permute-start(f32[8,128]{1,0:T(8,128)S(1)} %get-tuple-element.51), channel_id=1, source_target_pairs={{0,16},{16,32},{32,48},{48,64},{64,80},{80,96},{96,112},{112,128},... | collective-permute-start | bytes 12296 | tf_op jit(solution)/shard_map/ppermute | solution.py:440
  136.1 8.8 %collective-permute-start.11 = (f32[8,128]{1,0:T(8,128)S(1)}, f32[8,128]{1,0:T(8,128)S(1)}, u32[]{:S(2)}, u32[]{:S(2)}) collective-permute-start(f32[8,128]{1,0:T(8,128)S(1)} %get-tuple-element.52), channel_id=1, source_target_pairs={{16,0},{32,16},{48,32},{64,48},{80,64},{96,80},{112,96},{128,112},... | collective-permute-start | bytes 12296 | tf_op jit(solution)/shard_map/ppermute | solution.py:440
  144.9 12.0 %collective-permute-start.15 = (f32[8,128]{1,0:T(8,128)S(1)}, f32[8,128]{1,0:T(8,128)S(1)}, u32[]{:S(2)}, u32[]{:S(2)}) collective-permute-start(f32[8,128]{1,0:T(8,128)S(1)} %get-tuple-element.64.v_ref.v2), channel_id=1, source_target_pairs={{0,1},{1,2},{2,3},{3,4},{4,5},{5,6},{6,7},{7,8},{8,9},{9,10},{10,1... | collective-permute-start | bytes 12296 | tf_op jit(solution)/shard_map/ppermute | solution.py:440
  146.3 10.7 %collective-permute-start.14 = (f32[8,128]{1,0:T(8,128)S(1)}, f32[8,128]{1,0:T(8,128)S(1)}, u32[]{:S(2)}, u32[]{:S(2)}) collective-permute-start(f32[8,128]{1,0:T(8,128)S(1)} %get-tuple-element.64.v_ref.v2), channel_id=1, source_target_pairs={{1,0},{2,1},{3,2},{4,3},{5,4},{6,5},{7,6},{8,7},{9,8},{10,9},{11,1... | collective-permute-start | bytes 12296 | tf_op jit(solution)/shard_map/ppermute | solution.py:440
  147.6 9.4 %collective-permute-start.13 = (f32[8,128]{1,0:T(8,128)S(1)}, f32[8,128]{1,0:T(8,128)S(1)}, u32[]{:S(2)}, u32[]{:S(2)}) collective-permute-start(f32[8,128]{1,0:T(8,128)S(1)} %get-tuple-element.64.v_ref.v2), channel_id=1, source_target_pairs={{0,16},{16,32},{32,48},{48,64},{64,80},{80,96},{96,112},{112,128},... | collective-permute-start | bytes 12296 | tf_op jit(solution)/shard_map/ppermute | solution.py:440
  149.5 8.7 %collective-permute-start.12 = (f32[8,128]{1,0:T(8,128)S(1)}, f32[8,128]{1,0:T(8,128)S(1)}, u32[]{:S(2)}, u32[]{:S(2)}) collective-permute-start(f32[8,128]{1,0:T(8,128)S(1)} %get-tuple-element.64.v_ref.v2), channel_id=1, source_target_pairs={{16,0},{32,16},{48,32},{64,48},{80,64},{96,80},{112,96},{128,112},... | collective-permute-start | bytes 12296 | tf_op jit(solution)/shard_map/ppermute | solution.py:440
  181.1 9.4 %collective-permute-start.16 = (f32[8,128]{1,0:T(8,128)S(1)}, f32[8,128]{1,0:T(8,128)S(1)}, u32[]{:S(2)}, u32[]{:S(2)}) collective-permute-start(f32[8,128]{1,0:T(8,128)S(1)} %get-tuple-element.56), channel_id=1, source_target_pairs={{0,16},{16,32},{32,48},{48,64},{64,80},{80,96},{96,112},{112,128},... | collective-permute-start | bytes 12296 | tf_op jit(solution)/shard_map/ppermute | solution.py:440
  183.0 8.8 %collective-permute-start.17 = (f32[8,128]{1,0:T(8,128)S(1)}, f32[8,128]{1,0:T(8,128)S(1)}, u32[]{:S(2)}, u32[]{:S(2)}) collective-permute-start(f32[8,128]{1,0:T(8,128)S(1)} %get-tuple-element.57), channel_id=1, source_target_pairs={{16,0},{32,16},{48,32},{64,48},{80,64},{96,80},{112,96},{128,112},... | collective-permute-start | bytes 12296 | tf_op jit(solution)/shard_map/ppermute | solution.py:440

commit v2 on v1

--- a/solution.py
+++ b/solution.py
@@ -100,8 +100,7 @@
 
 
 def setup_kernel(
-    panel_hbm, corner_hbm, diag_hbm, place_hbm, map_hbm, count_hbm, scale_hbm, rhs_hbm, v_ref,
-    scale_ref, rhs_ref, pack_ref, report_ref, rows_ref, facts_ref, panel_ref, corner_ref, diag_ref,
+    panel_hbm, corner_hbm, diag_hbm, place_hbm, map_hbm, count_hbm, pack_ref, report_ref, rows_ref, facts_ref, panel_ref, corner_ref, diag_ref,
     place_ref, map_ref, count_ref, facts, sems,
 ):
     slots, rows, width = panel_ref.shape
@@ -110,8 +109,6 @@
     total = slots * corners
     at = slots * rows
     moves = (
-        (scale_hbm, scale_ref),
-        (rhs_hbm, rhs_ref),
         (corner_hbm, corner_ref),
         (place_hbm, place_ref),
         (map_hbm, map_ref),
@@ -127,7 +124,6 @@
     facts[...] = jnp.zeros_like(facts)
     for copy in copies:
         copy.wait()
-    v_ref[...] = scale_ref[...] * rhs_ref[...]
     pack_ref[at + 8 : at + 8 + slots, :] = diag_ref[...]
     lane = iota((1, LANES), 1)
     for s in range(slots):
@@ -462,13 +458,12 @@
     tile = (owned, block_size)
     facts_shape = jax.ShapeDtypeStruct((8, LANES), jnp.int32)
     facts_scratch = [pltpu.SMEM((8, LANES), jnp.int32), pltpu.SemaphoreType.DMA]
-    direction, scale, rhs, pack, report, corner_rows, facts = call(
+    rhs, scale = dual_rhs[0, 0], scaling[0, 0]
+    direction = scale * rhs
+    pack, report, corner_rows, facts = call(
         setup_kernel,
         "setup",
         [
-            tile,
-            tile,
-            tile,
             (slots * rows + 16, width),
             (corners + 8, LANES),
             (LANES, LANES),
@@ -482,7 +477,7 @@
             pltpu.VMEM((slots, per), jnp.int32),
             pltpu.SMEM((1, 1), jnp.int32),
             (8, LANES),
-            pltpu.SemaphoreType.DMA((8,)),
+            pltpu.SemaphoreType.DMA((6,)),
         ],
         [],
         [
@@ -492,8 +487,6 @@
             corner_map[0, 0],
             block_map[0, 0],
             counts,
-            scaling[0, 0],
-            dual_rhs[0, 0],
         ],
         space=pltpu.HBM,
     )
@@ -551,7 +544,6 @@
             image = mine + arrived[0] + arrived[1]
             images.append(image)
             last, direction = image, STEP * scale * image
-    sums, *arrived = lax.optimization_barrier((sums, *arrived))
     across = lax.axis_size("gx")
     for group in (runs(across, 4), strided(across, 4)):
         sums = lax.all_gather(sums, "gx", axis=0, tiled=True, axis_index_groups=group)

time: 220 us -> 213 us (0.968)
  blocking collectives: 90.6 us -> 87 us
  waiting for transfers between devices: 7.76 us -> 5.2 us
    all_gather x2, blocking collectives: 26.2 us -> 22.7 us  [shards(): lax.all_gather(sums, 'gx', axis=0, tiled=True, axis_index_groups=group)]
    ppermute x18, waiting for transfers between devices: 7.76 us -> 5.2 us  [moved(): lax.ppermute(x, axis, [(i, i + by) for i in range(count) if 0 <= i + by <...]
    unnamed x18 -> x20, local copies, waits for them, and re-layouts: 6.21 us -> 5.53 us
  transfers between devices with their start and end apart: 18 -> 18, of which waited for: 6 -> 4; matrix products, arithmetic and copies ran while one was open for 0% -> 0% of each run, Pallas kernels for 15% -> 16%
where the time goes in v2:
time: 213 us; the launch traced here: 212 us
  blocking collectives  87 us (41%)
  starting transfers between devices  65.2 us (31%)
  Pallas kernels  47 us (22%)
  local copies, waits for them, and re-layouts  5.53 us (3%)
  waiting for transfers between devices  5.2 us (2%)
    ppermute x18, starting transfers between devices, moved(): lax.ppermute(x, axis, [(i, i + by) for i in range(count) if 0 <= i + by <...  65.2 us
    all_gather x3, blocking collectives, shards(): gathered = lax.all_gather(pay, 'gy')  64.4 us
    pallas_call x9, Pallas kernels, call(): pl.pallas_call(kernel, out_shape=outs, in_specs=[smem] * len(scalars) + [...  47 us
    all_gather x2, blocking collectives, shards(): lax.all_gather(sums, 'gx', axis=0, tiled=True, axis_index_groups=group)  22.7 us
    unnamed x20, local copies, waits for them, and re-layouts  5.53 us
    ppermute x18, waiting for transfers between devices, moved(): lax.ppermute(x, axis, [(i, i + by) for i in range(count) if 0 <= i + by <...  5.2 us
  transfers between devices with their start and end apart: 18, of which 4 were waited for; matrix products, arithmetic and copies ran while one was open for 0% of the time, Pallas kernels for 16%

profile of v2, /device:TPU:32, one launch (start us, length us, event | category | flops | bytes accessed | tf_op | source)
XLA Modules:
  0.0 212.4 jit_solution(13936701926740047176)
XLA Ops:
  0.6 0.7 bitcast_multiply_fusion.v_ref.v0
  1.3 1.7 collective-permute-start.3
  3.1 1.3 collective-permute-start.2
  4.4 3.4 %collective-permute-start.1 = (f32[8,128]{1,0:T(8,128)S(1)}, f32[8,128]{1,0:T(8,128)S(1)}, u32[]{:S(2)}, u32[]{:S(2)}) collective-permute-start(f32[8,128]{1,0:T(8,128)S(1)} %bitcast_multiply_fusion.v_ref.v0), channel_id=1, source_target_pairs={{0,16},{16,32},{32,48},{48,64},{64,80},{80,96},{96,112},{112,128},... | collective-permute-start | bytes 12296 | tf_op jit(solution)/shard_map/ppermute | solution.py:436
  7.8 5.8 %collective-permute-start = (f32[8,128]{1,0:T(8,128)S(1)}, f32[8,128]{1,0:T(8,128)S(1)}, u32[]{:S(2)}, u32[]{:S(2)}) collective-permute-start(f32[8,128]{1,0:T(8,128)S(1)} %bitcast_multiply_fusion.v_ref.v0), channel_id=1, source_target_pairs={{16,0},{32,16},{48,32},{64,48},{80,64},{96,80},{112,96},{128,112},... | collective-permute-start | bytes 12296 | tf_op jit(solution)/shard_map/ppermute | solution.py:436
  14.2 0.0 copy-start.1
  14.2 1.0 copy-done.1
  15.2 0.7 copy-done.4
  16.0 0.7 copy-done.5
  16.6 0.7 copy-done.7
  17.3 0.7 copy-done.8
  18.0 0.8 setup.1
  18.8 0.0 collective-permute-done.3.rest_4_
  18.8 0.0 collective-permute-done.2.rest_3_
  18.8 0.0 collective-permute-done.1.rest_2_
  18.9 0.0 collective-permute-done.rest_1_
  18.9 0.0 copy-start.2
  18.9 0.7 copy-done.2
  19.6 1.3 before.3
  20.8 28.5 %all-gather = f32[1024,128]{1,0:T(8,128)} all-gather(f32[64,128]{1,0:T(8,128)S(1)} %before.3), channel_id=2, replica_groups=mesh['gx'=32,'gy'=16] {'gy'}, dimensions={0}, use_global_device_ids=true | all-gather | bytes 557056 | tf_op jit(solution)/shard_map/all_gather | solution.py:520
  49.4 2.3 %collective-permute-start.5 = (f32[272,1024]{1,0:T(8,128)S(1)}, f32[272,1024]{1,0:T(8,128)S(1)}, u32[]{:S(2)}, u32[]{:S(2)}) collective-permute-start(f32[272,1024]{1,0:T(8,128)S(1)} %get-tuple-element.36.rest_0_), channel_id=1, source_target_pairs={{0,1},{1,2},{2,3},{3,4},{4,5},{5,6},{6,7},{7,8},{8,9},{9,10},{10,1... | collective-permute-start | bytes 3342344 | tf_op jit(solution)/shard_map/ppermute | solution.py:436
  51.7 1.3 collective-permute-start.4
  53.0 0.0 copy-done.6
  53.0 0.0 copy-start
  53.0 1.0 copy-done
  54.0 32.1 %coarse.1 = (f32[512,512]{1,0:T(8,128)S(1)}, f32[16,128]{1,0:T(8,128)S(1)}, f32[144,128]{1,0:T(8,128)S(1)}, s32[8,128]{1,0:T(8,128)S(1)}) custom-call(s32[1]{0:T(128)} %bitcast.y_ref, f32[16,64,128]{2,1,0:T(8,128)S(1)} %bitcast.23, f32[1,512]{1,0:T(1,128)S(1)} %copy-done.6), custom_call_target="tpu_custom_call" | custom-call | tf_op jit(solution)/shard_map/coarse/pallas_call | solution.py:423
  86.2 0.0 collective-permute-done.5.rest_2_
  86.2 0.0 collective-permute-done.4.rest_1_
  86.2 0.0 copy-start.9
  86.2 2.8 %after.3 = (f32[8,128]{1,0:T(8,128)S(1)}, f32[8,128]{1,0:T(8,128)S(1)}, f32[8,128]{1,0:T(8,128)S(1)}, f32[1,128]{1,0:T(1,128)S(1)}) custom-call(s32[1]{0:T(128)} %bitcast.y_ref, f32[16,64,128]{2,1,0:T(8,128)S(1)} %bitcast.24, f32[16,128]{1,0:T(8,128)S(1)} %get-tuple-element.32.rows_ref, f32[144,128]{1,0:T(8,128)S(1)} %get-tuple-element.33.places_ref, ...), custom_call_target="tpu_custom_call" | custom-call | tf_op jit(solution)/shard_map/after/pallas_call | solution.py:423
  89.0 1.9 collective-permute-start.6
  90.9 7.2 %collective-permute-start.7 = (f32[8,128]{1,0:T(8,128)S(1)}, f32[8,128]{1,0:T(8,128)S(1)}, u32[]{:S(2)}, u32[]{:S(2)}) collective-permute-start(f32[8,128]{1,0:T(8,128)S(1)} %get-tuple-element.39), channel_id=1, source_target_pairs={{16,0},{32,16},{48,32},{64,48},{80,64},{96,80},{112,96},{128,112},... | collective-permute-start | bytes 12296 | tf_op jit(solution)/shard_map/ppermute | solution.py:436
  98.2 0.0 collective-permute-done.6
  98.2 1.3 collective-permute-done.7
  99.5 0.0 copy-done.9
  99.5 1.9 collective-permute-start.9
  101.4 7.5 %collective-permute-start.8 = (f32[8,128]{1,0:T(8,128)S(1)}, f32[8,128]{1,0:T(8,128)S(1)}, u32[]{:S(2)}, u32[]{:S(2)}) collective-permute-start(f32[8,128]{1,0:T(8,128)S(1)} %get-tuple-element.54.v_ref.v1), channel_id=1, source_target_pairs={{16,0},{32,16},{48,32},{64,48},{80,64},{96,80},{112,96},{128,112},... | collective-permute-start | bytes 12296 | tf_op jit(solution)/shard_map/ppermute | solution.py:436
  108.9 0.0 collective-permute-done.9.rest_4_
  109.0 1.3 collective-permute-done.8.rest_3_
  110.3 2.3 %before.4 = f32[32,128]{1,0:T(8,128)S(1)} custom-call(f32[8,128]{1,0:T(8,128)S(1)} %get-tuple-element.54.v_ref.v1, f32[8,128]{1,0:T(8,128)S(1)} %get-tuple-element.55.last_ref.w0, f32[128,128]{1,0:T(8,128)S(1)} %get-tuple-element.27.corner_ref, s32[8,128]{1,0:T(8,128)S(1)} %get-tuple-element.34.facts_ref, f32[272,1024]{1,0:T(8,128)S(1)} %get-tuple-element.36.rest_0_, ...), custom_call_target="tpu_custom_call" | custom-call | tf_op jit(solution)/shard_map/before/pallas_call | solution.py:423
  112.6 17.2 %all-gather.1 = f32[512,128]{1,0:T(8,128)S(1)} all-gather(f32[32,128]{1,0:T(8,128)S(1)} %before.4), channel_id=3, replica_groups=mesh['gx'=32,'gy'=16] {'gy'}, dimensions={0}, use_global_device_ids=true | all-gather | bytes 278528 | tf_op jit(solution)/shard_map/all_gather | solution.py:520
  129.8 2.9 %after.4 = (f32[8,128]{1,0:T(8,128)S(1)}, f32[8,128]{1,0:T(8,128)S(1)}, f32[8,128]{1,0:T(8,128)S(1)}, f32[1,128]{1,0:T(1,128)S(1)}, f32[1,128]{1,0:T(1,128)S(1)}) custom-call(s32[1]{0:T(128)} %bitcast.y_ref, f32[16,32,128]{2,1,0:T(8,128)S(1)} %bitcast.26, f32[16,128]{1,0:T(8,128)S(1)} %get-tuple-element.32.rows_ref, ...), custom_call_target="tpu_custom_call" | custom-call | tf_op jit(solution)/shard_map/after/pallas_call | solution.py:423
  132.7 1.9 collective-permute-start.10
  134.6 7.5 %collective-permute-start.11 = (f32[8,128]{1,0:T(8,128)S(1)}, f32[8,128]{1,0:T(8,128)S(1)}, u32[]{:S(2)}, u32[]{:S(2)}) collective-permute-start(f32[8,128]{1,0:T(8,128)S(1)} %get-tuple-element.43), channel_id=1, source_target_pairs={{16,0},{32,16},{48,32},{64,48},{80,64},{96,80},{112,96},{128,112},... | collective-permute-start | bytes 12296 | tf_op jit(solution)/shard_map/ppermute | solution.py:436
  142.1 0.0 collective-permute-done.10
  142.1 1.3 collective-permute-done.11
  143.4 1.4 collective-permute-start.15
  144.8 1.3 collective-permute-start.14
  146.1 1.9 collective-permute-start.13
  148.0 7.4 %collective-permute-start.12 = (f32[8,128]{1,0:T(8,128)S(1)}, f32[8,128]{1,0:T(8,128)S(1)}, u32[]{:S(2)}, u32[]{:S(2)}) collective-permute-start(f32[8,128]{1,0:T(8,128)S(1)} %get-tuple-element.52.v_ref.v2), channel_id=1, source_target_pairs={{16,0},{32,16},{48,32},{64,48},{80,64},{96,80},{112,96},{128,112},... | collective-permute-start | bytes 12296 | tf_op jit(solution)/shard_map/ppermute | solution.py:436
  155.4 0.0 collective-permute-done.15.rest_4_
  155.5 0.0 collective-permute-done.14.rest_3_
  155.5 0.0 collective-permute-done.13.rest_2_
  155.5 1.3 collective-permute-done.12.rest_1_
  156.8 1.3 before.5
  158.0 18.7 %all-gather.2 = f32[512,128]{1,0:T(8,128)S(1)} all-gather(f32[32,128]{1,0:T(8,128)S(1)} %before.5), channel_id=4, replica_groups=mesh['gx'=32,'gy'=16] {'gy'}, dimensions={0}, use_global_device_ids=true | all-gather | bytes 278528 | tf_op jit(solution)/shard_map/all_gather | solution.py:520
  176.7 2.8 %after.5 = (f32[8,128]{1,0:T(8,128)S(1)}, f32[8,128]{1,0:T(8,128)S(1)}, f32[8,128]{1,0:T(8,128)S(1)}, f32[1,128]{1,0:T(1,128)S(1)}) custom-call(s32[1]{0:T(128)} %bitcast.y_ref, f32[16,32,128]{2,1,0:T(8,128)S(1)} %bitcast.25, f32[16,128]{1,0:T(8,128)S(1)} %get-tuple-element.32.rows_ref, f32[144,128]{1,0:T(8,128)S(1)} %get-tuple-element.33.places_ref, ...), custom_call_target="tpu_custom_call" | custom-call | tf_op jit(solution)/shard_map/after/pallas_call | solution.py:423
  179.5 1.9 collective-permute-start.16
  181.4 7.5 %collective-permute-start.17 = (f32[8,128]{1,0:T(8,128)S(1)}, f32[8,128]{1,0:T(8,128)S(1)}, u32[]{:S(2)}, u32[]{:S(2)}) collective-permute-start(f32[8,128]{1,0:T(8,128)S(1)} %get-tuple-element.49), channel_id=1, source_target_pairs={{16,0},{32,16},{48,32},{64,48},{80,64},{96,80},{112,96},{128,112},... | collective-permute-start | bytes 12296 | tf_op jit(solution)/shard_map/ppermute | solution.py:436
  189.0 6.9 %all-gather.4 = f32[4,1,128]{2,1,0:T(1,128)S(1)} all-gather(f32[1,1,128]{2,1,0:T(1,128)S(1)} %bitcast.35), channel_id=1, replica_groups={{0,16,32,48},{64,80,96,112},{128,144,160,176},{192,208,224,240},{256,27..., dimensions={0}, use_global_device_ids=true | all-gather | bytes 2560 | tf_op jit(solution)/shard_map/all_gather | solution.py:549
  195.9 15.7 %all-gather.5 = f32[8,1,128]{2,1,0:T(1,128)S(1)} all-gather(f32[1,1,128]{2,1,0:T(1,128)S(1)} %bitcast.36), channel_id=5, replica_groups={{0,64,128,192,256,320,384,448},{16,80,144,208,272,336,400,464},{32,96,1..., dimensions={0}, use_global_device_ids=true | all-gather | bytes 4608 | tf_op jit(solution)/shard_map/all_gather | solution.py:549
  211.7 0.0 collective-permute-done.16.east
  211.7 0.0 collective-permute-done.17.west
  211.7 0.7 final.1
  (11 shorter events, 0.1 us)
Async XLA Ops:
  1.3 17.5 %collective-permute-start.3 = (f32[8,128]{1,0:T(8,128)S(1)}, f32[8,128]{1,0:T(8,128)S(1)}, u32[]{:S(2)}, u32[]{:S(2)}) collective-permute-start(f32[8,128]{1,0:T(8,128)S(1)} %bitcast_multiply_fusion.v_ref.v0), channel_id=1, source_target_pairs={{0,1},{1,2},{2,3},{3,4},{4,5},{5,6},{6,7},{7,8},{8,9},{9,10},{10,1... | collective-permute-start | bytes 12296 | tf_op jit(solution)/shard_map/ppermute | solution.py:436
  3.1 15.8 %collective-permute-start.2 = (f32[8,128]{1,0:T(8,128)S(1)}, f32[8,128]{1,0:T(8,128)S(1)}, u32[]{:S(2)}, u32[]{:S(2)}) collective-permute-start(f32[8,128]{1,0:T(8,128)S(1)} %bitcast_multiply_fusion.v_ref.v0), channel_id=1, source_target_pairs={{1,0},{2,1},{3,2},{4,3},{5,4},{6,5},{7,6},{8,7},{9,8},{10,9},{11,1... | collective-permute-start | bytes 12296 | tf_op jit(solution)/shard_map/ppermute | solution.py:436
  4.4 14.5 %collective-permute-start.1 = (f32[8,128]{1,0:T(8,128)S(1)}, f32[8,128]{1,0:T(8,128)S(1)}, u32[]{:S(2)}, u32[]{:S(2)}) collective-permute-start(f32[8,128]{1,0:T(8,128)S(1)} %bitcast_multiply_fusion.v_ref.v0), channel_id=1, source_target_pairs={{0,16},{16,32},{32,48},{48,64},{64,80},{80,96},{96,112},{112,128},... | collective-permute-start | bytes 12296 | tf_op jit(solution)/shard_map/ppermute | solution.py:436
  7.8 11.1 %collective-permute-start = (f32[8,128]{1,0:T(8,128)S(1)}, f32[8,128]{1,0:T(8,128)S(1)}, u32[]{:S(2)}, u32[]{:S(2)}) collective-permute-start(f32[8,128]{1,0:T(8,128)S(1)} %bitcast_multiply_fusion.v_ref.v0), channel_id=1, source_target_pairs={{16,0},{32,16},{48,32},{64,48},{80,64},{96,80},{112,96},{128,112},... | collective-permute-start | bytes 12296 | tf_op jit(solution)/shard_map/ppermute | solution.py:436
  14.2 1.0 copy-start.1
  15.2 0.7 copy-start.4
  15.9 0.7 copy-start.5
  16.6 0.7 copy-start.7
  17.3 0.7 copy-start.8
  18.0 35.0 %copy-start.6 = (f32[1,512]{1,0:T(1,128)S(1)}, f32[1,512]{1,0:T(1,128)}, u32[]{:S(2)}) copy-start(f32[1,512]{1,0:T(1,128)} %diag_ref.1) | copy-start | bytes 6148
  18.9 0.7 copy-start.2
  49.4 36.8 %collective-permute-start.5 = (f32[272,1024]{1,0:T(8,128)S(1)}, f32[272,1024]{1,0:T(8,128)S(1)}, u32[]{:S(2)}, u32[]{:S(2)}) collective-permute-start(f32[272,1024]{1,0:T(8,128)S(1)} %get-tuple-element.36.rest_0_), channel_id=1, source_target_pairs={{0,1},{1,2},{2,3},{3,4},{4,5},{5,6},{6,7},{7,8},{8,9},{9,10},{10,1... | collective-permute-start | bytes 3342344 | tf_op jit(solution)/shard_map/ppermute | solution.py:436
  51.7 34.5 %collective-permute-start.4 = (f32[272,1024]{1,0:T(8,128)S(1)}, f32[272,1024]{1,0:T(8,128)S(1)}, u32[]{:S(2)}, u32[]{:S(2)}) collective-permute-start(f32[272,1024]{1,0:T(8,128)S(1)} %get-tuple-element.36.rest_0_), channel_id=1, source_target_pairs={{1,0},{2,1},{3,2},{4,3},{5,4},{6,5},{7,6},{8,7},{9,8},{10,9},{11,1... | collective-permute-start | bytes 3342344 | tf_op jit(solution)/shard_map/ppermute | solution.py:436
  53.0 1.0 copy-start
  86.2 13.3 %copy-start.9 = (f32[1,1,8,128]{3,2,1,0:T(8,128)S(1)}, f32[1,1,8,128]{3,2,1,0:T(8,128)}, u32[]{:S(2)}) copy-start(f32[1,1,8,128]{3,2,1,0:T(8,128)} %param.13) | copy-start | bytes 12292
  89.0 9.2 %collective-permute-start.6 = (f32[8,128]{1,0:T(8,128)S(1)}, f32[8,128]{1,0:T(8,128)S(1)}, u32[]{:S(2)}, u32[]{:S(2)}) collective-permute-start(f32[8,128]{1,0:T(8,128)S(1)} %get-tuple-element.38), channel_id=1, source_target_pairs={{0,16},{16,32},{32,48},{48,64},{64,80},{80,96},{96,112},{112,128},... | collective-permute-start | bytes 12296 | tf_op jit(solution)/shard_map/ppermute | solution.py:436
  90.9 8.6 %collective-permute-start.7 = (f32[8,128]{1,0:T(8,128)S(1)}, f32[8,128]{1,0:T(8,128)S(1)}, u32[]{:S(2)}, u32[]{:S(2)}) collective-permute-start(f32[8,128]{1,0:T(8,128)S(1)} %get-tuple-element.39), channel_id=1, source_target_pairs={{16,0},{32,16},{48,32},{64,48},{80,64},{96,80},{112,96},{128,112},... | collective-permute-start | bytes 12296 | tf_op jit(solution)/shard_map/ppermute | solution.py:436
  99.5 9.4 %collective-permute-start.9 = (f32[8,128]{1,0:T(8,128)S(1)}, f32[8,128]{1,0:T(8,128)S(1)}, u32[]{:S(2)}, u32[]{:S(2)}) collective-permute-start(f32[8,128]{1,0:T(8,128)S(1)} %get-tuple-element.54.v_ref.v1), channel_id=1, source_target_pairs={{0,16},{16,32},{32,48},{48,64},{64,80},{80,96},{96,112},{112,128},... | collective-permute-start | bytes 12296 | tf_op jit(solution)/shard_map/ppermute | solution.py:436
  101.4 8.8 %collective-permute-start.8 = (f32[8,128]{1,0:T(8,128)S(1)}, f32[8,128]{1,0:T(8,128)S(1)}, u32[]{:S(2)}, u32[]{:S(2)}) collective-permute-start(f32[8,128]{1,0:T(8,128)S(1)} %get-tuple-element.54.v_ref.v1), channel_id=1, source_target_pairs={{16,0},{32,16},{48,32},{64,48},{80,64},{96,80},{112,96},{128,112},... | collective-permute-start | bytes 12296 | tf_op jit(solution)/shard_map/ppermute | solution.py:436
  132.7 9.4 %collective-permute-start.10 = (f32[8,128]{1,0:T(8,128)S(1)}, f32[8,128]{1,0:T(8,128)S(1)}, u32[]{:S(2)}, u32[]{:S(2)}) collective-permute-start(f32[8,128]{1,0:T(8,128)S(1)} %get-tuple-element.42), channel_id=1, source_target_pairs={{0,16},{16,32},{32,48},{48,64},{64,80},{80,96},{96,112},{112,128},... | collective-permute-start | bytes 12296 | tf_op jit(solution)/shard_map/ppermute | solution.py:436
  134.6 8.8 %collective-permute-start.11 = (f32[8,128]{1,0:T(8,128)S(1)}, f32[8,128]{1,0:T(8,128)S(1)}, u32[]{:S(2)}, u32[]{:S(2)}) collective-permute-start(f32[8,128]{1,0:T(8,128)S(1)} %get-tuple-element.43), channel_id=1, source_target_pairs={{16,0},{32,16},{48,32},{64,48},{80,64},{96,80},{112,96},{128,112},... | collective-permute-start | bytes 12296 | tf_op jit(solution)/shard_map/ppermute | solution.py:436
  143.4 12.0 %collective-permute-start.15 = (f32[8,128]{1,0:T(8,128)S(1)}, f32[8,128]{1,0:T(8,128)S(1)}, u32[]{:S(2)}, u32[]{:S(2)}) collective-permute-start(f32[8,128]{1,0:T(8,128)S(1)} %get-tuple-element.52.v_ref.v2), channel_id=1, source_target_pairs={{0,1},{1,2},{2,3},{3,4},{4,5},{5,6},{6,7},{7,8},{8,9},{9,10},{10,1... | collective-permute-start | bytes 12296 | tf_op jit(solution)/shard_map/ppermute | solution.py:436
  144.8 10.7 %collective-permute-start.14 = (f32[8,128]{1,0:T(8,128)S(1)}, f32[8,128]{1,0:T(8,128)S(1)}, u32[]{:S(2)}, u32[]{:S(2)}) collective-permute-start(f32[8,128]{1,0:T(8,128)S(1)} %get-tuple-element.52.v_ref.v2), channel_id=1, source_target_pairs={{1,0},{2,1},{3,2},{4,3},{5,4},{6,5},{7,6},{8,7},{9,8},{10,9},{11,1... | collective-permute-start | bytes 12296 | tf_op jit(solution)/shard_map/ppermute | solution.py:436
  146.1 9.4 %collective-permute-start.13 = (f32[8,128]{1,0:T(8,128)S(1)}, f32[8,128]{1,0:T(8,128)S(1)}, u32[]{:S(2)}, u32[]{:S(2)}) collective-permute-start(f32[8,128]{1,0:T(8,128)S(1)} %get-tuple-element.52.v_ref.v2), channel_id=1, source_target_pairs={{0,16},{16,32},{32,48},{48,64},{64,80},{80,96},{96,112},{112,128},... | collective-permute-start | bytes 12296 | tf_op jit(solution)/shard_map/ppermute | solution.py:436
  148.0 8.7 %collective-permute-start.12 = (f32[8,128]{1,0:T(8,128)S(1)}, f32[8,128]{1,0:T(8,128)S(1)}, u32[]{:S(2)}, u32[]{:S(2)}) collective-permute-start(f32[8,128]{1,0:T(8,128)S(1)} %get-tuple-element.52.v_ref.v2), channel_id=1, source_target_pairs={{16,0},{32,16},{48,32},{64,48},{80,64},{96,80},{112,96},{128,112},... | collective-permute-start | bytes 12296 | tf_op jit(solution)/shard_map/ppermute | solution.py:436
  176.7 35.0 %copy-start.3 = (f32[1,1,8,128]{3,2,1,0:T(8,128)S(1)}, f32[1,1,8,128]{3,2,1,0:T(8,128)}, u32[]{:S(2)}) copy-start(f32[1,1,8,128]{3,2,1,0:T(8,128)} %param.14) | copy-start | bytes 12292
  179.5 32.1 %collective-permute-start.16 = (f32[8,128]{1,0:T(8,128)S(1)}, f32[8,128]{1,0:T(8,128)S(1)}, u32[]{:S(2)}, u32[]{:S(2)}) collective-permute-start(f32[8,128]{1,0:T(8,128)S(1)} %get-tuple-element.48), channel_id=1, source_target_pairs={{0,16},{16,32},{32,48},{48,64},{64,80},{80,96},{96,112},{112,128},... | collective-permute-start | bytes 12296 | tf_op jit(solution)/shard_map/ppermute | solution.py:436
  181.4 30.2 %collective-permute-start.17 = (f32[8,128]{1,0:T(8,128)S(1)}, f32[8,128]{1,0:T(8,128)S(1)}, u32[]{:S(2)}, u32[]{:S(2)}) collective-permute-start(f32[8,128]{1,0:T(8,128)S(1)} %get-tuple-element.49), channel_id=1, source_target_pairs={{16,0},{32,16},{48,32},{64,48},{80,64},{96,80},{112,96},{128,112},... | collective-permute-start | bytes 12296 | tf_op jit(solution)/shard_map/ppermute | solution.py:436

commit v3 on v2

--- a/solution.py
+++ b/solution.py
@@ -211,6 +211,16 @@
             hots, piece.astype(BF16), (((0,), (0,)), ((), ())), preferred_element_type=F32
         )
     out_ref[...] = system
+    eliminated(out_ref, 0, 1)
+
+
+def rest_kernel(system_ref, out_ref):
+    out_ref[...] = system_ref[...]
+    eliminated(out_ref, 1, out_ref.shape[0] // LANES)
+
+
+def eliminated(out_ref, first, last):
+    n = out_ref.shape[0]
     b = LANES
 
     def eliminate(k, carry):
@@ -227,7 +237,7 @@
         out_ref[pl.ds(ro, b), :] = fresh
         return carry
 
-    lax.fori_loop(0, n // b, eliminate, 0)
+    lax.fori_loop(first, last, eliminate, 0)
 
 
 def fact_of(facts, slots, corners, per, g, s, b, owned):
@@ -519,10 +529,8 @@
         )
         gathered = lax.all_gather(pay, "gy")
         if not sweep:
-            gathered, leaving = lax.optimization_barrier((gathered, pack))
-            packs = [pack, moved(leaving, "gy", -1), moved(leaving, "gy", 1)]
             here = y.reshape(1).astype(jnp.int32)
-            inverse, place_rows, places3, facts3 = call(
+            started, place_rows, places3, facts3 = call(
                 functools.partial(coarse_kernel, slots, corners, 4 * owned),
                 "coarse",
                 [(n, n), (peers, LANES), (3 * total, LANES), facts_shape],
@@ -530,6 +538,9 @@
                 [here],
                 [gathered, coarse_diag],
             )
+            started, leaving = lax.optimization_barrier((started, pack))
+            packs = [pack, moved(leaving, "gy", -1), moved(leaving, "gy", 1)]
+            (inverse,) = call(rest_kernel, "rest", [(n, n)], [], [], [started])
         mine, east, west, sums, *late = call(
             functools.partial(after_kernel, slots, corners, per, sweep, partial),
             "after",

time: 213 us -> 211 us (level)
    unnamed x20 -> x18, local copies, waits for them, and re-layouts: 5.53 us -> 4.49 us
    pallas_call x9 -> x10, Pallas kernels: 47 us -> 46.9 us  [call(): pl.pallas_call(kernel, out_shape=outs, in_specs=[smem] * len(scalars) + [...]
  transfers between devices with their start and end apart: 18 -> 18, of which waited for: 4 -> 4; matrix products, arithmetic and copies ran while one was open for 0% -> 0% of each run, Pallas kernels for 16% -> 11%
where the time goes in v3:
time: 211 us; the launch traced here: 210 us
  blocking collectives  85.4 us (40%)
  starting transfers between devices  65.4 us (31%)
  Pallas kernels  46.9 us (22%)
  waiting for transfers between devices  5.2 us (2%)
  local copies, waits for them, and re-layouts  4.49 us (2%)
    ppermute x18, starting transfers between devices, moved(): lax.ppermute(x, axis, [(i, i + by) for i in range(count) if 0 <= i + by <...  65.4 us
    all_gather x3, blocking collectives, shards(): gathered = lax.all_gather(pay, 'gy')  62.8 us
    pallas_call x10, Pallas kernels, call(): pl.pallas_call(kernel, out_shape=outs, in_specs=[smem] * len(scalars) + [...  46.9 us
    all_gather x2, blocking collectives, shards(): lax.all_gather(sums, 'gx', axis=0, tiled=True, axis_index_groups=group)  22.7 us
    ppermute x18, waiting for transfers between devices, moved(): lax.ppermute(x, axis, [(i, i + by) for i in range(count) if 0 <= i + by <...  5.2 us
    unnamed x18, local copies, waits for them, and re-layouts  4.49 us
  transfers between devices with their start and end apart: 18, of which 4 were waited for; matrix products, arithmetic and copies ran while one was open for 0% of the time, Pallas kernels for 11%

profile of v3, /device:TPU:32, one launch (start us, length us, event | category | flops | bytes accessed | tf_op | source)
XLA Modules:
  0.0 209.9 jit_solution(7708727010129467790)
XLA Ops:
  0.6 0.7 bitcast_multiply_fusion.v_ref.v0
  1.3 1.7 collective-permute-start.3
  3.1 1.3 collective-permute-start.2
  4.4 3.4 %collective-permute-start.1 = (f32[8,128]{1,0:T(8,128)S(1)}, f32[8,128]{1,0:T(8,128)S(1)}, u32[]{:S(2)}, u32[]{:S(2)}) collective-permute-start(f32[8,128]{1,0:T(8,128)S(1)} %bitcast_multiply_fusion.v_ref.v0), channel_id=1, source_target_pairs={{0,16},{16,32},{32,48},{48,64},{64,80},{80,96},{96,112},{112,128},... | collective-permute-start | bytes 12296 | tf_op jit(solution)/shard_map/ppermute | solution.py:446
  7.8 5.8 %collective-permute-start = (f32[8,128]{1,0:T(8,128)S(1)}, f32[8,128]{1,0:T(8,128)S(1)}, u32[]{:S(2)}, u32[]{:S(2)}) collective-permute-start(f32[8,128]{1,0:T(8,128)S(1)} %bitcast_multiply_fusion.v_ref.v0), channel_id=1, source_target_pairs={{16,0},{32,16},{48,32},{64,48},{80,64},{96,80},{112,96},{128,112},... | collective-permute-start | bytes 12296 | tf_op jit(solution)/shard_map/ppermute | solution.py:446
  14.2 0.0 copy-start
  14.2 1.0 copy-done
  15.2 0.7 copy-done.3
  16.0 0.7 copy-done.4
  16.7 0.7 copy-done.6
  17.3 0.7 copy-done.7
  18.0 0.8 setup.1
  18.8 0.0 collective-permute-done.3.rest_4_
  18.8 0.0 collective-permute-done.2.rest_3_
  18.9 0.0 collective-permute-done.1.rest_2_
  18.9 0.0 collective-permute-done.rest_1_
  18.9 0.0 copy-start.1
  18.9 0.7 copy-done.1
  19.6 1.3 before.3
  20.9 27.1 %all-gather = f32[1024,128]{1,0:T(8,128)S(1)} all-gather(f32[64,128]{1,0:T(8,128)S(1)} %before.3), channel_id=2, replica_groups=mesh['gx'=32,'gy'=16] {'gy'}, dimensions={0}, use_global_device_ids=true | all-gather | bytes 557056 | tf_op jit(solution)/shard_map/all_gather | solution.py:530
  48.0 0.0 copy-done.5
  48.0 9.6 %coarse.1 = (f32[512,512]{1,0:T(8,128)S(1)}, f32[16,128]{1,0:T(8,128)S(1)}, f32[144,128]{1,0:T(8,128)S(1)}, s32[8,128]{1,0:T(8,128)S(1)}) custom-call(s32[1]{0:T(128)} %bitcast.y_ref, f32[16,64,128]{2,1,0:T(8,128)S(1)} %bitcast.23, f32[1,512]{1,0:T(1,128)S(1)} %copy-done.5), custom_call_target="tpu_custom_call" | custom-call | tf_op jit(solution)/shard_map/coarse/pallas_call | solution.py:433
  57.6 2.3 %collective-permute-start.5 = (f32[272,1024]{1,0:T(8,128)S(1)}, f32[272,1024]{1,0:T(8,128)S(1)}, u32[]{:S(2)}, u32[]{:S(2)}) collective-permute-start(f32[272,1024]{1,0:T(8,128)S(1)} %get-tuple-element.36.rest_0_), channel_id=1, source_target_pairs={{0,1},{1,2},{2,3},{3,4},{4,5},{5,6},{6,7},{7,8},{8,9},{9,10},{10,1... | collective-permute-start | bytes 3342344 | tf_op jit(solution)/shard_map/ppermute | solution.py:446
  60.0 1.5 collective-permute-start.4
  61.4 22.4 %rest.1.inverse_ref = f32[512,512]{1,0:T(8,128)S(1)} custom-call(f32[512,512]{1,0:T(8,128)S(1)} %get-tuple-element.35.system_ref), custom_call_target="tpu_custom_call" | custom-call | tf_op jit(solution)/shard_map/rest/pallas_call | solution.py:433
  83.8 0.0 collective-permute-done.5.rest_2_
  83.8 0.0 collective-permute-done.4.rest_1_
  83.9 0.0 copy-start.8
  83.9 2.8 %after.3 = (f32[8,128]{1,0:T(8,128)S(1)}, f32[8,128]{1,0:T(8,128)S(1)}, f32[8,128]{1,0:T(8,128)S(1)}, f32[1,128]{1,0:T(1,128)S(1)}) custom-call(s32[1]{0:T(128)} %bitcast.y_ref, f32[16,64,128]{2,1,0:T(8,128)S(1)} %bitcast.24, f32[16,128]{1,0:T(8,128)S(1)} %get-tuple-element.31.rows_ref, f32[144,128]{1,0:T(8,128)S(1)} %get-tuple-element.32.places_ref, ...), custom_call_target="tpu_custom_call" | custom-call | tf_op jit(solution)/shard_map/after/pallas_call | solution.py:433
  86.7 1.9 collective-permute-start.6
  88.6 7.2 %collective-permute-start.7 = (f32[8,128]{1,0:T(8,128)S(1)}, f32[8,128]{1,0:T(8,128)S(1)}, u32[]{:S(2)}, u32[]{:S(2)}) collective-permute-start(f32[8,128]{1,0:T(8,128)S(1)} %get-tuple-element.39), channel_id=1, source_target_pairs={{16,0},{32,16},{48,32},{64,48},{80,64},{96,80},{112,96},{128,112},... | collective-permute-start | bytes 12296 | tf_op jit(solution)/shard_map/ppermute | solution.py:446
  95.9 0.0 collective-permute-done.6
  95.9 1.3 collective-permute-done.7
  97.2 0.0 copy-done.8
  97.2 1.9 collective-permute-start.9
  99.1 7.5 %collective-permute-start.8 = (f32[8,128]{1,0:T(8,128)S(1)}, f32[8,128]{1,0:T(8,128)S(1)}, u32[]{:S(2)}, u32[]{:S(2)}) collective-permute-start(f32[8,128]{1,0:T(8,128)S(1)} %get-tuple-element.54.v_ref.v1), channel_id=1, source_target_pairs={{16,0},{32,16},{48,32},{64,48},{80,64},{96,80},{112,96},{128,112},... | collective-permute-start | bytes 12296 | tf_op jit(solution)/shard_map/ppermute | solution.py:446
  106.6 0.0 collective-permute-done.9.rest_4_
  106.6 1.3 collective-permute-done.8.rest_3_
  107.9 2.3 %before.4 = f32[32,128]{1,0:T(8,128)S(1)} custom-call(f32[8,128]{1,0:T(8,128)S(1)} %get-tuple-element.54.v_ref.v1, f32[8,128]{1,0:T(8,128)S(1)} %get-tuple-element.55.last_ref.w0, f32[128,128]{1,0:T(8,128)S(1)} %get-tuple-element.27.corner_ref, s32[8,128]{1,0:T(8,128)S(1)} %get-tuple-element.33.facts_ref, f32[272,1024]{1,0:T(8,128)S(1)} %get-tuple-element.36.rest_0_, ...), custom_call_target="tpu_custom_call" | custom-call | tf_op jit(solution)/shard_map/before/pallas_call | solution.py:433
  110.3 17.0 %all-gather.1 = f32[512,128]{1,0:T(8,128)S(1)} all-gather(f32[32,128]{1,0:T(8,128)S(1)} %before.4), channel_id=3, replica_groups=mesh['gx'=32,'gy'=16] {'gy'}, dimensions={0}, use_global_device_ids=true | all-gather | bytes 278528 | tf_op jit(solution)/shard_map/all_gather | solution.py:530
  127.3 2.9 %after.4 = (f32[8,128]{1,0:T(8,128)S(1)}, f32[8,128]{1,0:T(8,128)S(1)}, f32[8,128]{1,0:T(8,128)S(1)}, f32[1,128]{1,0:T(1,128)S(1)}, f32[1,128]{1,0:T(1,128)S(1)}) custom-call(s32[1]{0:T(128)} %bitcast.y_ref, f32[16,32,128]{2,1,0:T(8,128)S(1)} %bitcast.26, f32[16,128]{1,0:T(8,128)S(1)} %get-tuple-element.31.rows_ref, ...), custom_call_target="tpu_custom_call" | custom-call | tf_op jit(solution)/shard_map/after/pallas_call | solution.py:433
  130.1 1.9 collective-permute-start.10
  132.1 7.5 %collective-permute-start.11 = (f32[8,128]{1,0:T(8,128)S(1)}, f32[8,128]{1,0:T(8,128)S(1)}, u32[]{:S(2)}, u32[]{:S(2)}) collective-permute-start(f32[8,128]{1,0:T(8,128)S(1)} %get-tuple-element.43), channel_id=1, source_target_pairs={{16,0},{32,16},{48,32},{64,48},{80,64},{96,80},{112,96},{128,112},... | collective-permute-start | bytes 12296 | tf_op jit(solution)/shard_map/ppermute | solution.py:446
  139.6 0.0 collective-permute-done.10
  139.6 1.3 collective-permute-done.11
  140.9 1.4 collective-permute-start.15
  142.3 1.3 collective-permute-start.14
  143.6 1.9 collective-permute-start.13
  145.5 7.4 %collective-permute-start.12 = (f32[8,128]{1,0:T(8,128)S(1)}, f32[8,128]{1,0:T(8,128)S(1)}, u32[]{:S(2)}, u32[]{:S(2)}) collective-permute-start(f32[8,128]{1,0:T(8,128)S(1)} %get-tuple-element.52.v_ref.v2), channel_id=1, source_target_pairs={{16,0},{32,16},{48,32},{64,48},{80,64},{96,80},{112,96},{128,112},... | collective-permute-start | bytes 12296 | tf_op jit(solution)/shard_map/ppermute | solution.py:446
  152.9 0.0 collective-permute-done.15.rest_4_
  152.9 0.0 collective-permute-done.14.rest_3_
  153.0 0.0 collective-permute-done.13.rest_2_
  153.0 1.3 collective-permute-done.12.rest_1_
  154.2 1.3 before.5
  155.5 18.6 %all-gather.2 = f32[512,128]{1,0:T(8,128)S(1)} all-gather(f32[32,128]{1,0:T(8,128)S(1)} %before.5), channel_id=4, replica_groups=mesh['gx'=32,'gy'=16] {'gy'}, dimensions={0}, use_global_device_ids=true | all-gather | bytes 278528 | tf_op jit(solution)/shard_map/all_gather | solution.py:530
  174.2 2.8 %after.5 = (f32[8,128]{1,0:T(8,128)S(1)}, f32[8,128]{1,0:T(8,128)S(1)}, f32[8,128]{1,0:T(8,128)S(1)}, f32[1,128]{1,0:T(1,128)S(1)}) custom-call(s32[1]{0:T(128)} %bitcast.y_ref, f32[16,32,128]{2,1,0:T(8,128)S(1)} %bitcast.25, f32[16,128]{1,0:T(8,128)S(1)} %get-tuple-element.31.rows_ref, f32[144,128]{1,0:T(8,128)S(1)} %get-tuple-element.32.places_ref, ...), custom_call_target="tpu_custom_call" | custom-call | tf_op jit(solution)/shard_map/after/pallas_call | solution.py:433
  177.0 1.9 collective-permute-start.16
  178.9 7.5 %collective-permute-start.17 = (f32[8,128]{1,0:T(8,128)S(1)}, f32[8,128]{1,0:T(8,128)S(1)}, u32[]{:S(2)}, u32[]{:S(2)}) collective-permute-start(f32[8,128]{1,0:T(8,128)S(1)} %get-tuple-element.49), channel_id=1, source_target_pairs={{16,0},{32,16},{48,32},{64,48},{80,64},{96,80},{112,96},{128,112},... | collective-permute-start | bytes 12296 | tf_op jit(solution)/shard_map/ppermute | solution.py:446
  186.4 6.9 %all-gather.4 = f32[4,1,128]{2,1,0:T(1,128)S(1)} all-gather(f32[1,1,128]{2,1,0:T(1,128)S(1)} %bitcast.35), channel_id=1, replica_groups={{0,16,32,48},{64,80,96,112},{128,144,160,176},{192,208,224,240},{256,27..., dimensions={0}, use_global_device_ids=true | all-gather | bytes 2560 | tf_op jit(solution)/shard_map/all_gather | solution.py:560
  193.4 15.7 %all-gather.5 = f32[8,1,128]{2,1,0:T(1,128)S(1)} all-gather(f32[1,1,128]{2,1,0:T(1,128)S(1)} %bitcast.36), channel_id=5, replica_groups={{0,64,128,192,256,320,384,448},{16,80,144,208,272,336,400,464},{32,96,1..., dimensions={0}, use_global_device_ids=true | all-gather | bytes 4608 | tf_op jit(solution)/shard_map/all_gather | solution.py:560
  209.1 0.0 collective-permute-done.16.east
  209.1 0.0 collective-permute-done.17.west
  209.2 0.0 copy-done.2
  209.2 0.7 final.1
  (10 shorter events, 0.1 us)
Async XLA Ops:
  1.3 17.5 %collective-permute-start.3 = (f32[8,128]{1,0:T(8,128)S(1)}, f32[8,128]{1,0:T(8,128)S(1)}, u32[]{:S(2)}, u32[]{:S(2)}) collective-permute-start(f32[8,128]{1,0:T(8,128)S(1)} %bitcast_multiply_fusion.v_ref.v0), channel_id=1, source_target_pairs={{0,1},{1,2},{2,3},{3,4},{4,5},{5,6},{6,7},{7,8},{8,9},{9,10},{10,1... | collective-permute-start | bytes 12296 | tf_op jit(solution)/shard_map/ppermute | solution.py:446
  3.1 15.8 %collective-permute-start.2 = (f32[8,128]{1,0:T(8,128)S(1)}, f32[8,128]{1,0:T(8,128)S(1)}, u32[]{:S(2)}, u32[]{:S(2)}) collective-permute-start(f32[8,128]{1,0:T(8,128)S(1)} %bitcast_multiply_fusion.v_ref.v0), channel_id=1, source_target_pairs={{1,0},{2,1},{3,2},{4,3},{5,4},{6,5},{7,6},{8,7},{9,8},{10,9},{11,1... | collective-permute-start | bytes 12296 | tf_op jit(solution)/shard_map/ppermute | solution.py:446
  4.4 14.5 %collective-permute-start.1 = (f32[8,128]{1,0:T(8,128)S(1)}, f32[8,128]{1,0:T(8,128)S(1)}, u32[]{:S(2)}, u32[]{:S(2)}) collective-permute-start(f32[8,128]{1,0:T(8,128)S(1)} %bitcast_multiply_fusion.v_ref.v0), channel_id=1, source_target_pairs={{0,16},{16,32},{32,48},{48,64},{64,80},{80,96},{96,112},{112,128},... | collective-permute-start | bytes 12296 | tf_op jit(solution)/shard_map/ppermute | solution.py:446
  7.8 11.1 %collective-permute-start = (f32[8,128]{1,0:T(8,128)S(1)}, f32[8,128]{1,0:T(8,128)S(1)}, u32[]{:S(2)}, u32[]{:S(2)}) collective-permute-start(f32[8,128]{1,0:T(8,128)S(1)} %bitcast_multiply_fusion.v_ref.v0), channel_id=1, source_target_pairs={{16,0},{32,16},{48,32},{64,48},{80,64},{96,80},{112,96},{128,112},... | collective-permute-start | bytes 12296 | tf_op jit(solution)/shard_map/ppermute | solution.py:446
  14.2 1.0 copy-start
  15.2 0.7 copy-start.3
  16.0 0.7 copy-start.4
  16.7 0.7 copy-start.6
  17.3 0.7 copy-start.7
  18.0 30.0 %copy-start.5 = (f32[1,512]{1,0:T(1,128)S(1)}, f32[1,512]{1,0:T(1,128)}, u32[]{:S(2)}) copy-start(f32[1,512]{1,0:T(1,128)} %diag_ref.1) | copy-start | bytes 6148
  18.9 0.7 copy-start.1
  57.6 26.2 %collective-permute-start.5 = (f32[272,1024]{1,0:T(8,128)S(1)}, f32[272,1024]{1,0:T(8,128)S(1)}, u32[]{:S(2)}, u32[]{:S(2)}) collective-permute-start(f32[272,1024]{1,0:T(8,128)S(1)} %get-tuple-element.36.rest_0_), channel_id=1, source_target_pairs={{0,1},{1,2},{2,3},{3,4},{4,5},{5,6},{6,7},{7,8},{8,9},{9,10},{10,1... | collective-permute-start | bytes 3342344 | tf_op jit(solution)/shard_map/ppermute | solution.py:446
  60.0 23.9 %collective-permute-start.4 = (f32[272,1024]{1,0:T(8,128)S(1)}, f32[272,1024]{1,0:T(8,128)S(1)}, u32[]{:S(2)}, u32[]{:S(2)}) collective-permute-start(f32[272,1024]{1,0:T(8,128)S(1)} %get-tuple-element.36.rest_0_), channel_id=1, source_target_pairs={{1,0},{2,1},{3,2},{4,3},{5,4},{6,5},{7,6},{8,7},{9,8},{10,9},{11,1... | collective-permute-start | bytes 3342344 | tf_op jit(solution)/shard_map/ppermute | solution.py:446
  83.9 13.3 %copy-start.8 = (f32[1,1,8,128]{3,2,1,0:T(8,128)S(1)}, f32[1,1,8,128]{3,2,1,0:T(8,128)}, u32[]{:S(2)}) copy-start(f32[1,1,8,128]{3,2,1,0:T(8,128)} %param.13) | copy-start | bytes 12292
  86.7 9.2 %collective-permute-start.6 = (f32[8,128]{1,0:T(8,128)S(1)}, f32[8,128]{1,0:T(8,128)S(1)}, u32[]{:S(2)}, u32[]{:S(2)}) collective-permute-start(f32[8,128]{1,0:T(8,128)S(1)} %get-tuple-element.38), channel_id=1, source_target_pairs={{0,16},{16,32},{32,48},{48,64},{64,80},{80,96},{96,112},{112,128},... | collective-permute-start | bytes 12296 | tf_op jit(solution)/shard_map/ppermute | solution.py:446
  88.6 8.6 %collective-permute-start.7 = (f32[8,128]{1,0:T(8,128)S(1)}, f32[8,128]{1,0:T(8,128)S(1)}, u32[]{:S(2)}, u32[]{:S(2)}) collective-permute-start(f32[8,128]{1,0:T(8,128)S(1)} %get-tuple-element.39), channel_id=1, source_target_pairs={{16,0},{32,16},{48,32},{64,48},{80,64},{96,80},{112,96},{128,112},... | collective-permute-start | bytes 12296 | tf_op jit(solution)/shard_map/ppermute | solution.py:446
  97.2 9.4 %collective-permute-start.9 = (f32[8,128]{1,0:T(8,128)S(1)}, f32[8,128]{1,0:T(8,128)S(1)}, u32[]{:S(2)}, u32[]{:S(2)}) collective-permute-start(f32[8,128]{1,0:T(8,128)S(1)} %get-tuple-element.54.v_ref.v1), channel_id=1, source_target_pairs={{0,16},{16,32},{32,48},{48,64},{64,80},{80,96},{96,112},{112,128},... | collective-permute-start | bytes 12296 | tf_op jit(solution)/shard_map/ppermute | solution.py:446
  99.1 8.8 %collective-permute-start.8 = (f32[8,128]{1,0:T(8,128)S(1)}, f32[8,128]{1,0:T(8,128)S(1)}, u32[]{:S(2)}, u32[]{:S(2)}) collective-permute-start(f32[8,128]{1,0:T(8,128)S(1)} %get-tuple-element.54.v_ref.v1), channel_id=1, source_target_pairs={{16,0},{32,16},{48,32},{64,48},{80,64},{96,80},{112,96},{128,112},... | collective-permute-start | bytes 12296 | tf_op jit(solution)/shard_map/ppermute | solution.py:446
  130.1 9.4 %collective-permute-start.10 = (f32[8,128]{1,0:T(8,128)S(1)}, f32[8,128]{1,0:T(8,128)S(1)}, u32[]{:S(2)}, u32[]{:S(2)}) collective-permute-start(f32[8,128]{1,0:T(8,128)S(1)} %get-tuple-element.42), channel_id=1, source_target_pairs={{0,16},{16,32},{32,48},{48,64},{64,80},{80,96},{96,112},{112,128},... | collective-permute-start | bytes 12296 | tf_op jit(solution)/shard_map/ppermute | solution.py:446
  132.1 8.8 %collective-permute-start.11 = (f32[8,128]{1,0:T(8,128)S(1)}, f32[8,128]{1,0:T(8,128)S(1)}, u32[]{:S(2)}, u32[]{:S(2)}) collective-permute-start(f32[8,128]{1,0:T(8,128)S(1)} %get-tuple-element.43), channel_id=1, source_target_pairs={{16,0},{32,16},{48,32},{64,48},{80,64},{96,80},{112,96},{128,112},... | collective-permute-start | bytes 12296 | tf_op jit(solution)/shard_map/ppermute | solution.py:446
  140.9 12.0 %collective-permute-start.15 = (f32[8,128]{1,0:T(8,128)S(1)}, f32[8,128]{1,0:T(8,128)S(1)}, u32[]{:S(2)}, u32[]{:S(2)}) collective-permute-start(f32[8,128]{1,0:T(8,128)S(1)} %get-tuple-element.52.v_ref.v2), channel_id=1, source_target_pairs={{0,1},{1,2},{2,3},{3,4},{4,5},{5,6},{6,7},{7,8},{8,9},{9,10},{10,1... | collective-permute-start | bytes 12296 | tf_op jit(solution)/shard_map/ppermute | solution.py:446
  142.3 10.7 %collective-permute-start.14 = (f32[8,128]{1,0:T(8,128)S(1)}, f32[8,128]{1,0:T(8,128)S(1)}, u32[]{:S(2)}, u32[]{:S(2)}) collective-permute-start(f32[8,128]{1,0:T(8,128)S(1)} %get-tuple-element.52.v_ref.v2), channel_id=1, source_target_pairs={{1,0},{2,1},{3,2},{4,3},{5,4},{6,5},{7,6},{8,7},{9,8},{10,9},{11,1... | collective-permute-start | bytes 12296 | tf_op jit(solution)/shard_map/ppermute | solution.py:446
  143.6 9.4 %collective-permute-start.13 = (f32[8,128]{1,0:T(8,128)S(1)}, f32[8,128]{1,0:T(8,128)S(1)}, u32[]{:S(2)}, u32[]{:S(2)}) collective-permute-start(f32[8,128]{1,0:T(8,128)S(1)} %get-tuple-element.52.v_ref.v2), channel_id=1, source_target_pairs={{0,16},{16,32},{32,48},{48,64},{64,80},{80,96},{96,112},{112,128},... | collective-permute-start | bytes 12296 | tf_op jit(solution)/shard_map/ppermute | solution.py:446
  145.5 8.7 %collective-permute-start.12 = (f32[8,128]{1,0:T(8,128)S(1)}, f32[8,128]{1,0:T(8,128)S(1)}, u32[]{:S(2)}, u32[]{:S(2)}) collective-permute-start(f32[8,128]{1,0:T(8,128)S(1)} %get-tuple-element.52.v_ref.v2), channel_id=1, source_target_pairs={{16,0},{32,16},{48,32},{64,48},{80,64},{96,80},{112,96},{128,112},... | collective-permute-start | bytes 12296 | tf_op jit(solution)/shard_map/ppermute | solution.py:446
  174.2 35.0 %copy-start.2 = (f32[1,1,8,128]{3,2,1,0:T(8,128)S(1)}, f32[1,1,8,128]{3,2,1,0:T(8,128)}, u32[]{:S(2)}) copy-start(f32[1,1,8,128]{3,2,1,0:T(8,128)} %param.14) | copy-start | bytes 12292
  177.0 32.2 %collective-permute-start.16 = (f32[8,128]{1,0:T(8,128)S(1)}, f32[8,128]{1,0:T(8,128)S(1)}, u32[]{:S(2)}, u32[]{:S(2)}) collective-permute-start(f32[8,128]{1,0:T(8,128)S(1)} %get-tuple-element.48), channel_id=1, source_target_pairs={{0,16},{16,32},{32,48},{48,64},{64,80},{80,96},{96,112},{112,128},... | collective-permute-start | bytes 12296 | tf_op jit(solution)/shard_map/ppermute | solution.py:446
  178.9 30.2 %collective-permute-start.17 = (f32[8,128]{1,0:T(8,128)S(1)}, f32[8,128]{1,0:T(8,128)S(1)}, u32[]{:S(2)}, u32[]{:S(2)}) collective-permute-start(f32[8,128]{1,0:T(8,128)S(1)} %get-tuple-element.49), channel_id=1, source_target_pairs={{16,0},{32,16},{48,32},{64,48},{80,64},{96,80},{112,96},{128,112},... | collective-permute-start | bytes 12296 | tf_op jit(solution)/shard_map/ppermute | solution.py:446

commit v4 on v3

--- a/solution.py
+++ b/solution.py
@@ -321,11 +321,18 @@
 ):
     packs, rest = rest[:3], rest[3:]
     before, rest = rest[: 1 if sweep else 0], rest[1 if sweep else 0 :]
-    late, (cand, u_ref, acc, facts, sem) = rest[4:-5], rest[-5:]
-    mine, east, west, sums_ref = rest[:4]
+    outs, (cand, u_ref, acc, facts, sem) = rest[:-5], rest[-5:]
+    last = len(outs) == 2
+    mine, late = outs[0], outs[4:]
+    owned = mine.shape[0]
+    if last:
+        sums_ref = outs[1].at[:1, :]
+        east, west = outs[1].at[owned : 2 * owned, :], outs[1].at[2 * owned :, :]
+        outs[1][:owned, :] = jnp.zeros((owned, LANES), F32)
+    else:
+        east, west, sums_ref = outs[1:4]
     copy = pltpu.make_async_copy(facts_ref, facts, sem)
     copy.start()
-    owned = mine.shape[0]
     total = slots * corners
     n = inverse_ref.shape[0]
     count = gathered_ref.shape[0]
@@ -402,8 +409,24 @@
     west[...] = acc[2 * owned : 3 * owned, :]
 
 
-def final_kernel(first, gathered_ref, rhs_ref, v0, v1, v2, w0, w1, mine, east, west, x_ref, r_ref):
-    sums = gathered_ref[...]
+def final_kernel(first, x_ref, near_ref, far_ref, rhs_ref, v0, v1, v2, w0, w1, mine, m_ref, r_ref):
+    run, runs_here = near_ref.shape[0], far_ref.shape[0]
+    owned = mine.shape[0]
+    x = x_ref[0]
+    at, row = x % run, x // run
+    low, high_end = slice(owned, 2 * owned), slice(2 * owned, 3 * owned)
+    from_west = jnp.where(
+        at > 0,
+        near_ref[jnp.maximum(at - 1, 0), low, :],
+        far_ref[jnp.maximum(row - 1, 0), low, :] * jnp.where(row > 0, 1.0, 0.0),
+    )
+    from_east = jnp.where(
+        at < run - 1,
+        near_ref[jnp.minimum(at + 1, run - 1), high_end, :],
+        far_ref[jnp.minimum(row + 1, runs_here - 1), high_end, :]
+        * jnp.where(row < runs_here - 1, 1.0, 0.0),
+    )
+    sums = jnp.sum(far_ref[:, 0, :], axis=0, keepdims=True)
     lane = iota((1, LANES), 1)
 
     def moment(i):
@@ -421,8 +444,8 @@
     c2 = y2 / d2
     c1 = y1 / d1 - l21 * c2
     c0 = r0 / h00 - l10 * c1 - l20 * c2
-    w2 = mine[...] + east[...] + west[...]
-    x_ref[...] = c0 * v0[...] + c1 * v1[...] + c2 * v2[...]
+    w2 = mine[...] + from_west + from_east
+    m_ref[...] = c0 * v0[...] + c1 * v1[...] + c2 * v2[...]
     r_ref[...] = rhs_ref[...] - (c0 * w0[...] + c1 * w1[...] + c2 * w2)
 
 
@@ -541,31 +564,44 @@
             started, leaving = lax.optimization_barrier((started, pack))
             packs = [pack, moved(leaving, "gy", -1), moved(leaving, "gy", 1)]
             (inverse,) = call(rest_kernel, "rest", [(n, n)], [], [], [started])
-        mine, east, west, sums, *late = call(
+        outs = [tile] * 3 + [(1, LANES)] * (2 if partial else 1)
+        if sweep == 2:
+            outs = [tile, (3 * owned, LANES)]
+        mine, *outs = call(
             functools.partial(after_kernel, slots, corners, per, sweep, partial),
             "after",
-            [tile] * 3 + [(1, LANES)] * (2 if partial else 1),
+            outs,
             [(15 * owned, block_size), (8, width), (15 * owned, block_size), *facts_scratch],
             [here],
             [gathered, place_rows, places3, facts3, inverse, *packs, *([sums] if sweep else [])],
         )
-        arrived = [moved(east, "gx", 1), moved(west, "gx", -1)]
+        if sweep < 2:
+            east, west, sums, *late = outs
+            arrived = [moved(east, "gx", 1), moved(west, "gx", -1)]
         directions.append(direction)
         if sweep < 2:
             image = mine + arrived[0] + arrived[1]
             images.append(image)
             last, direction = image, STEP * scale * image
-    across = lax.axis_size("gx")
-    for group in (runs(across, 4), strided(across, 4)):
-        sums = lax.all_gather(sums, "gx", axis=0, tiled=True, axis_index_groups=group)
-        sums = jnp.sum(sums, axis=0, keepdims=True)
+    across, run = lax.axis_size("gx"), 4
+    near = lax.all_gather(outs[0], "gx", axis_index_groups=runs(across, run))
+    ends = jnp.concatenate(
+        [
+            jnp.sum(near[:, :owned], axis=0),
+            near[run - 1, owned : 2 * owned],
+            near[0, 2 * owned :],
+        ],
+        axis=0,
+    )
+    far = lax.all_gather(ends, "gx", axis_index_groups=strided(across, run))
+    place = lax.axis_index("gx").reshape(1).astype(jnp.int32)
     multipliers, residual = call(
         functools.partial(final_kernel, total),
         "final",
         [tile] * 2,
         [],
-        [],
-        [sums, rhs, *directions, *images, mine, *arrived],
+        [place],
+        [near, far, rhs, *directions, *images, mine],
     )
     return multipliers[None, None], residual[None, None]
 

time: 211 us -> 219 us (1.038)
  the two profiles are of different devices: /device:TPU:32 before, /device:TPU:26 now
where the time goes in v4:
time: 219 us; the launch traced here: 218 us
  blocking collectives  102 us (47%)
  Pallas kernels  47.4 us (22%)
  starting transfers between devices  41 us (19%)
  waiting for transfers between devices  20.5 us (9%)
  local copies, waits for them, and re-layouts  4.5 us (2%)
    all_gather x3, blocking collectives, shards(): gathered = lax.all_gather(pay, 'gy')  62.8 us
    pallas_call x10, Pallas kernels, call(): pl.pallas_call(kernel, out_shape=outs, in_specs=[smem] * len(scalars) + [...  47.4 us
    ppermute x16, starting transfers between devices, moved(): lax.ppermute(x, axis, [(i, i + by) for i in range(count) if 0 <= i + by <...  41 us
    all_gather x1, blocking collectives, shards(): far = lax.all_gather(ends, 'gx', axis_index_groups=strided(across, run))  24.6 us
    ppermute x16, waiting for transfers between devices, moved(): lax.ppermute(x, axis, [(i, i + by) for i in range(count) if 0 <= i + by <...  20.5 us
    all_gather x1, blocking collectives, shards(): near = lax.all_gather(outs[0], 'gx', axis_index_groups=runs(across, run))  14.6 us
    unnamed x22, local copies, waits for them, and re-layouts  4.5 us
  transfers between devices with their start and end apart: 16, of which 4 were waited for; matrix products, arithmetic and copies ran while one was open for 0% of the time, Pallas kernels for 11%

profile of v4, /device:TPU:26, one launch (start us, length us, event | category | flops | bytes accessed | tf_op | source)
XLA Modules:
  0.0 217.7 jit_solution(7331505584615527255)
XLA Ops:
  0.6 0.7 bitcast_multiply_fusion.v_ref.v0
  1.3 1.7 collective-permute-start.3
  3.1 1.3 collective-permute-start.2
  4.4 3.4 %collective-permute-start.1 = (f32[8,128]{1,0:T(8,128)S(1)}, f32[8,128]{1,0:T(8,128)S(1)}, u32[]{:S(2)}, u32[]{:S(2)}) collective-permute-start(f32[8,128]{1,0:T(8,128)S(1)} %bitcast_multiply_fusion.v_ref.v0), channel_id=1, source_target_pairs={{0,16},{16,32},{32,48},{48,64},{64,80},{80,96},{96,112},{112,128},... | collective-permute-start | bytes 12296 | tf_op jit(solution)/shard_map/ppermute | solution.py:469
  7.8 2.4 %collective-permute-start = (f32[8,128]{1,0:T(8,128)S(1)}, f32[8,128]{1,0:T(8,128)S(1)}, u32[]{:S(2)}, u32[]{:S(2)}) collective-permute-start(f32[8,128]{1,0:T(8,128)S(1)} %bitcast_multiply_fusion.v_ref.v0), channel_id=1, source_target_pairs={{16,0},{32,16},{48,32},{64,48},{80,64},{96,80},{112,96},{128,112},... | collective-permute-start | bytes 12296 | tf_op jit(solution)/shard_map/ppermute | solution.py:469
  10.9 0.0 copy-start.2
  10.9 1.0 copy-done.2
  11.9 0.7 copy-done.5
  12.6 0.7 copy-done.6
  13.3 0.7 copy-done.8
  14.0 0.7 copy-done.9
  14.7 0.8 setup.1
  15.5 0.0 collective-permute-done.3.rest_4_
  15.5 0.0 collective-permute-done.2.rest_3_
  15.5 0.0 collective-permute-done.1.rest_2_
  15.5 0.0 collective-permute-done.rest_1_
  15.6 0.0 copy-start.3
  15.6 0.7 copy-done.3
  16.2 1.3 before.3
  17.5 27.1 %all-gather = f32[1024,128]{1,0:T(8,128)S(1)} all-gather(f32[64,128]{1,0:T(8,128)S(1)} %before.3), channel_id=2, replica_groups=mesh['gx'=32,'gy'=16] {'gy'}, dimensions={0}, use_global_device_ids=true | all-gather | bytes 557056 | tf_op jit(solution)/shard_map/all_gather | solution.py:553
  44.7 0.0 copy-done.7
  44.7 9.6 %coarse.1 = (f32[512,512]{1,0:T(8,128)S(1)}, f32[16,128]{1,0:T(8,128)S(1)}, f32[144,128]{1,0:T(8,128)S(1)}, s32[8,128]{1,0:T(8,128)S(1)}) custom-call(s32[1]{0:T(128)} %bitcast.1.y_ref, f32[16,64,128]{2,1,0:T(8,128)S(1)} %bitcast.27, f32[1,512]{1,0:T(1,128)S(1)} %copy-done.7), custom_call_target="tpu_custom_call" | custom-call | tf_op jit(solution)/shard_map/coarse/pallas_call | solution.py:456
  54.3 2.3 %collective-permute-start.5 = (f32[272,1024]{1,0:T(8,128)S(1)}, f32[272,1024]{1,0:T(8,128)S(1)}, u32[]{:S(2)}, u32[]{:S(2)}) collective-permute-start(f32[272,1024]{1,0:T(8,128)S(1)} %get-tuple-element.34.rest_0_), channel_id=1, source_target_pairs={{0,1},{1,2},{2,3},{3,4},{4,5},{5,6},{6,7},{7,8},{8,9},{9,10},{10,1... | collective-permute-start | bytes 3342344 | tf_op jit(solution)/shard_map/ppermute | solution.py:469
  56.6 1.5 collective-permute-start.4
  58.1 22.4 %rest.1.inverse_ref = f32[512,512]{1,0:T(8,128)S(1)} custom-call(f32[512,512]{1,0:T(8,128)S(1)} %get-tuple-element.33.system_ref), custom_call_target="tpu_custom_call" | custom-call | tf_op jit(solution)/shard_map/rest/pallas_call | solution.py:456
  80.5 0.0 copy-start
  80.5 0.0 collective-permute-done.5.rest_2_
  80.5 0.0 collective-permute-done.4.rest_1_
  80.5 0.0 copy-start.10
  80.5 2.8 %after.3 = (f32[8,128]{1,0:T(8,128)S(1)}, f32[8,128]{1,0:T(8,128)S(1)}, f32[8,128]{1,0:T(8,128)S(1)}, f32[1,128]{1,0:T(1,128)S(1)}) custom-call(s32[1]{0:T(128)} %bitcast.1.y_ref, f32[16,64,128]{2,1,0:T(8,128)S(1)} %bitcast.28, f32[16,128]{1,0:T(8,128)S(1)} %get-tuple-element.29.rows_ref, f32[144,128]{1,0:T(8,128)S(1)} %get-tuple-element.30.places_ref, ...), custom_call_target="tpu_custom_call" | custom-call | tf_op jit(solution)/shard_map/after/pallas_call | solution.py:456
  83.3 3.4 %collective-permute-start.6 = (f32[8,128]{1,0:T(8,128)S(1)}, f32[8,128]{1,0:T(8,128)S(1)}, u32[]{:S(2)}, u32[]{:S(2)}) collective-permute-start(f32[8,128]{1,0:T(8,128)S(1)} %get-tuple-element.36), channel_id=1, source_target_pairs={{0,16},{16,32},{32,48},{48,64},{64,80},{80,96},{96,112},{112,128},... | collective-permute-start | bytes 12296 | tf_op jit(solution)/shard_map/ppermute | solution.py:469
  86.8 3.1 %collective-permute-start.7 = (f32[8,128]{1,0:T(8,128)S(1)}, f32[8,128]{1,0:T(8,128)S(1)}, u32[]{:S(2)}, u32[]{:S(2)}) collective-permute-start(f32[8,128]{1,0:T(8,128)S(1)} %get-tuple-element.37), channel_id=1, source_target_pairs={{16,0},{32,16},{48,32},{64,48},{80,64},{96,80},{112,96},{128,112},... | collective-permute-start | bytes 12296 | tf_op jit(solution)/shard_map/ppermute | solution.py:469
  89.8 0.0 collective-permute-done.6
  89.9 3.8 %collective-permute-done.7 = f32[8,128]{1,0:T(8,128)S(1)} collective-permute-done((f32[8,128]{1,0:T(8,128)S(1)}, f32[8,128]{1,0:T(8,128)S(1)}, u32[]{:S(2)}, u32[]{:S(2)}) %collective-permute-start.7) | collective-permute-done | bytes 4128 | tf_op jit(solution)/shard_map/ppermute | solution.py:469
  93.7 0.0 copy-done.10
  93.7 5.7 %collective-permute-start.9 = (f32[8,128]{1,0:T(8,128)S(1)}, f32[8,128]{1,0:T(8,128)S(1)}, u32[]{:S(2)}, u32[]{:S(2)}) collective-permute-start(f32[8,128]{1,0:T(8,128)S(1)} %get-tuple-element.50.v_ref.v1), channel_id=1, source_target_pairs={{0,16},{16,32},{32,48},{48,64},{64,80},{80,96},{96,112},{112,128},... | collective-permute-start | bytes 12296 | tf_op jit(solution)/shard_map/ppermute | solution.py:469
  99.4 1.9 collective-permute-start.8
  101.3 0.0 collective-permute-done.9.rest_4_
  101.3 6.9 %collective-permute-done.8.rest_3_ = f32[8,128]{1,0:T(8,128)S(1)} collective-permute-done((f32[8,128]{1,0:T(8,128)S(1)}, f32[8,128]{1,0:T(8,128)S(1)}, u32[]{:S(2)}, u32[]{:S(2)}) %collective-permute-start.8) | collective-permute-done | bytes 4128 | tf_op jit(solution)/shard_map/ppermute | solution.py:469
  108.2 2.3 %before.4 = f32[32,128]{1,0:T(8,128)S(1)} custom-call(f32[8,128]{1,0:T(8,128)S(1)} %get-tuple-element.50.v_ref.v1, f32[8,128]{1,0:T(8,128)S(1)} %get-tuple-element.51.last_ref.w0, f32[128,128]{1,0:T(8,128)S(1)} %get-tuple-element.25.corner_ref, s32[8,128]{1,0:T(8,128)S(1)} %get-tuple-element.31.facts_ref, f32[272,1024]{1,0:T(8,128)S(1)} %get-tuple-element.34.rest_0_, ...), custom_call_target="tpu_custom_call" | custom-call | tf_op jit(solution)/shard_map/before/pallas_call | solution.py:456
  110.6 17.0 %all-gather.1 = f32[512,128]{1,0:T(8,128)S(1)} all-gather(f32[32,128]{1,0:T(8,128)S(1)} %before.4), channel_id=3, replica_groups=mesh['gx'=32,'gy'=16] {'gy'}, dimensions={0}, use_global_device_ids=true | all-gather | bytes 278528 | tf_op jit(solution)/shard_map/all_gather | solution.py:553
  127.6 0.0 copy-done
  127.6 2.9 %after.4 = (f32[8,128]{1,0:T(8,128)S(1)}, f32[8,128]{1,0:T(8,128)S(1)}, f32[8,128]{1,0:T(8,128)S(1)}, f32[1,128]{1,0:T(1,128)S(1)}, f32[1,128]{1,0:T(1,128)S(1)}) custom-call(s32[1]{0:T(128)} %bitcast.1.y_ref, f32[16,32,128]{2,1,0:T(8,128)S(1)} %bitcast.30, f32[16,128]{1,0:T(8,128)S(1)} %get-tuple-element.29.rows_ref, ...), custom_call_target="tpu_custom_call" | custom-call | tf_op jit(solution)/shard_map/after/pallas_call | solution.py:456
  130.4 3.9 %collective-permute-start.10 = (f32[8,128]{1,0:T(8,128)S(1)}, f32[8,128]{1,0:T(8,128)S(1)}, u32[]{:S(2)}, u32[]{:S(2)}) collective-permute-start(f32[8,128]{1,0:T(8,128)S(1)} %get-tuple-element.40), channel_id=1, source_target_pairs={{0,16},{16,32},{32,48},{48,64},{64,80},{80,96},{96,112},{112,128},... | collective-permute-start | bytes 12296 | tf_op jit(solution)/shard_map/ppermute | solution.py:469
  134.4 1.9 collective-permute-start.11
  136.3 0.0 collective-permute-done.10
  136.3 4.9 %collective-permute-done.11 = f32[8,128]{1,0:T(8,128)S(1)} collective-permute-done((f32[8,128]{1,0:T(8,128)S(1)}, f32[8,128]{1,0:T(8,128)S(1)}, u32[]{:S(2)}, u32[]{:S(2)}) %collective-permute-start.11) | collective-permute-done | bytes 4128 | tf_op jit(solution)/shard_map/ppermute | solution.py:469
  141.2 1.3 collective-permute-start.15
  142.5 1.3 collective-permute-start.14
  143.8 3.9 %collective-permute-start.13 = (f32[8,128]{1,0:T(8,128)S(1)}, f32[8,128]{1,0:T(8,128)S(1)}, u32[]{:S(2)}, u32[]{:S(2)}) collective-permute-start(f32[8,128]{1,0:T(8,128)S(1)} %get-tuple-element.48.v_ref.v2), channel_id=1, source_target_pairs={{0,16},{16,32},{32,48},{48,64},{64,80},{80,96},{96,112},{112,128},... | collective-permute-start | bytes 12296 | tf_op jit(solution)/shard_map/ppermute | solution.py:469
  147.7 1.9 collective-permute-start.12
  149.6 0.0 copy-start.1
  149.7 0.0 collective-permute-done.15.rest_4_
  149.7 0.0 collective-permute-done.14.rest_3_
  149.7 0.0 collective-permute-done.13.rest_2_
  149.7 4.8 %collective-permute-done.12.rest_1_ = f32[8,128]{1,0:T(8,128)S(1)} collective-permute-done((f32[8,128]{1,0:T(8,128)S(1)}, f32[8,128]{1,0:T(8,128)S(1)}, u32[]{:S(2)}, u32[]{:S(2)}) %collective-permute-start.12) | collective-permute-done | bytes 4128 | tf_op jit(solution)/shard_map/ppermute | solution.py:469
  154.5 1.3 before.5
  155.8 18.7 %all-gather.2 = f32[512,128]{1,0:T(8,128)S(1)} all-gather(f32[32,128]{1,0:T(8,128)S(1)} %before.5), channel_id=4, replica_groups=mesh['gx'=32,'gy'=16] {'gy'}, dimensions={0}, use_global_device_ids=true | all-gather | bytes 278528 | tf_op jit(solution)/shard_map/all_gather | solution.py:553
  174.5 0.0 copy-done.1
  174.5 3.3 %after.5 = (f32[8,128]{1,0:T(8,128)S(1)}, f32[24,128]{1,0:T(8,128)S(1)}) custom-call(s32[1]{0:T(128)} %bitcast.1.y_ref, f32[16,32,128]{2,1,0:T(8,128)S(1)} %bitcast.29, f32[16,128]{1,0:T(8,128)S(1)} %get-tuple-element.29.rows_ref, f32[144,128]{1,0:T(8,128)S(1)} %get-tuple-element.30.places_ref, s32[8,128]{1,0:T(8,128)S(1)} %get-tuple-element.31.facts_ref, ...), custom_call_target="tpu_custom_call" | custom-call | tf_op jit(solution)/shard_map/after/pallas_call | solution.py:456
  177.8 14.6 %all-gather.3 = f32[96,128]{1,0:T(8,128)S(1)} all-gather(f32[24,128]{1,0:T(8,128)S(1)} %get-tuple-element.44), channel_id=5, replica_groups={{0,16,32,48},{64,80,96,112},{128,144,160,176},{192,208,224,240},{256,27..., dimensions={0}, use_global_device_ids=true | all-gather | bytes 61440 | tf_op jit(solution)/shard_map/all_gather | solution.py:587
  192.4 24.6 %all-gather.4 = f32[192,128]{1,0:T(8,128)S(1)} all-gather(f32[24,128]{1,0:T(8,128)S(1)} %pad_maximum_fusion), channel_id=6, replica_groups={{0,64,128,192,256,320,384,448},{16,80,144,208,272,336,400,464},{32,96,1..., dimensions={0}, use_global_device_ids=true | all-gather | bytes 110592 | tf_op jit(solution)/shard_map/all_gather | solution.py:596
  217.0 0.0 copy-done.4
  217.0 0.7 final.1
  (11 shorter events, 0.0 us)
Async XLA Ops:
  1.3 14.2 %collective-permute-start.3 = (f32[8,128]{1,0:T(8,128)S(1)}, f32[8,128]{1,0:T(8,128)S(1)}, u32[]{:S(2)}, u32[]{:S(2)}) collective-permute-start(f32[8,128]{1,0:T(8,128)S(1)} %bitcast_multiply_fusion.v_ref.v0), channel_id=1, source_target_pairs={{0,1},{1,2},{2,3},{3,4},{4,5},{5,6},{6,7},{7,8},{8,9},{9,10},{10,1... | collective-permute-start | bytes 12296 | tf_op jit(solution)/shard_map/ppermute | solution.py:469
  3.1 12.5 %collective-permute-start.2 = (f32[8,128]{1,0:T(8,128)S(1)}, f32[8,128]{1,0:T(8,128)S(1)}, u32[]{:S(2)}, u32[]{:S(2)}) collective-permute-start(f32[8,128]{1,0:T(8,128)S(1)} %bitcast_multiply_fusion.v_ref.v0), channel_id=1, source_target_pairs={{1,0},{2,1},{3,2},{4,3},{5,4},{6,5},{7,6},{8,7},{9,8},{10,9},{11,1... | collective-permute-start | bytes 12296 | tf_op jit(solution)/shard_map/ppermute | solution.py:469
  4.4 11.2 %collective-permute-start.1 = (f32[8,128]{1,0:T(8,128)S(1)}, f32[8,128]{1,0:T(8,128)S(1)}, u32[]{:S(2)}, u32[]{:S(2)}) collective-permute-start(f32[8,128]{1,0:T(8,128)S(1)} %bitcast_multiply_fusion.v_ref.v0), channel_id=1, source_target_pairs={{0,16},{16,32},{32,48},{48,64},{64,80},{80,96},{96,112},{112,128},... | collective-permute-start | bytes 12296 | tf_op jit(solution)/shard_map/ppermute | solution.py:469
  7.8 7.8 %collective-permute-start = (f32[8,128]{1,0:T(8,128)S(1)}, f32[8,128]{1,0:T(8,128)S(1)}, u32[]{:S(2)}, u32[]{:S(2)}) collective-permute-start(f32[8,128]{1,0:T(8,128)S(1)} %bitcast_multiply_fusion.v_ref.v0), channel_id=1, source_target_pairs={{16,0},{32,16},{48,32},{64,48},{80,64},{96,80},{112,96},{128,112},... | collective-permute-start | bytes 12296 | tf_op jit(solution)/shard_map/ppermute | solution.py:469
  10.9 1.0 copy-start.2
  11.9 0.7 copy-start.5
  12.6 0.7 copy-start.6
  13.3 0.7 copy-start.8
  14.0 0.7 copy-start.9
  14.7 30.0 %copy-start.7 = (f32[1,512]{1,0:T(1,128)S(1)}, f32[1,512]{1,0:T(1,128)}, u32[]{:S(2)}) copy-start(f32[1,512]{1,0:T(1,128)} %diag_ref.1) | copy-start | bytes 6148
  15.6 0.7 copy-start.3
  54.3 26.2 %collective-permute-start.5 = (f32[272,1024]{1,0:T(8,128)S(1)}, f32[272,1024]{1,0:T(8,128)S(1)}, u32[]{:S(2)}, u32[]{:S(2)}) collective-permute-start(f32[272,1024]{1,0:T(8,128)S(1)} %get-tuple-element.34.rest_0_), channel_id=1, source_target_pairs={{0,1},{1,2},{2,3},{3,4},{4,5},{5,6},{6,7},{7,8},{8,9},{9,10},{10,1... | collective-permute-start | bytes 3342344 | tf_op jit(solution)/shard_map/ppermute | solution.py:469
  56.6 23.9 %collective-permute-start.4 = (f32[272,1024]{1,0:T(8,128)S(1)}, f32[272,1024]{1,0:T(8,128)S(1)}, u32[]{:S(2)}, u32[]{:S(2)}) collective-permute-start(f32[272,1024]{1,0:T(8,128)S(1)} %get-tuple-element.34.rest_0_), channel_id=1, source_target_pairs={{1,0},{2,1},{3,2},{4,3},{5,4},{6,5},{7,6},{8,7},{9,8},{10,9},{11,1... | collective-permute-start | bytes 3342344 | tf_op jit(solution)/shard_map/ppermute | solution.py:469
  80.5 47.1 %copy-start = (f32[512,512]{1,0:T(8,128)}, f32[512,512]{1,0:T(8,128)S(1)}, u32[]{:S(2)}) copy-start(f32[512,512]{1,0:T(8,128)S(1)} %rest.1.inverse_ref) | copy-start | bytes 3145732
  80.5 13.2 %copy-start.10 = (f32[1,1,8,128]{3,2,1,0:T(8,128)S(1)}, f32[1,1,8,128]{3,2,1,0:T(8,128)}, u32[]{:S(2)}) copy-start(f32[1,1,8,128]{3,2,1,0:T(8,128)} %param.13) | copy-start | bytes 12292
  83.3 6.5 %collective-permute-start.6 = (f32[8,128]{1,0:T(8,128)S(1)}, f32[8,128]{1,0:T(8,128)S(1)}, u32[]{:S(2)}, u32[]{:S(2)}) collective-permute-start(f32[8,128]{1,0:T(8,128)S(1)} %get-tuple-element.36), channel_id=1, source_target_pairs={{0,16},{16,32},{32,48},{48,64},{64,80},{80,96},{96,112},{112,128},... | collective-permute-start | bytes 12296 | tf_op jit(solution)/shard_map/ppermute | solution.py:469
  86.8 6.9 %collective-permute-start.7 = (f32[8,128]{1,0:T(8,128)S(1)}, f32[8,128]{1,0:T(8,128)S(1)}, u32[]{:S(2)}, u32[]{:S(2)}) collective-permute-start(f32[8,128]{1,0:T(8,128)S(1)} %get-tuple-element.37), channel_id=1, source_target_pairs={{16,0},{32,16},{48,32},{64,48},{80,64},{96,80},{112,96},{128,112},... | collective-permute-start | bytes 12296 | tf_op jit(solution)/shard_map/ppermute | solution.py:469
  93.7 7.6 %collective-permute-start.9 = (f32[8,128]{1,0:T(8,128)S(1)}, f32[8,128]{1,0:T(8,128)S(1)}, u32[]{:S(2)}, u32[]{:S(2)}) collective-permute-start(f32[8,128]{1,0:T(8,128)S(1)} %get-tuple-element.50.v_ref.v1), channel_id=1, source_target_pairs={{0,16},{16,32},{32,48},{48,64},{64,80},{80,96},{96,112},{112,128},... | collective-permute-start | bytes 12296 | tf_op jit(solution)/shard_map/ppermute | solution.py:469
  99.4 8.8 %collective-permute-start.8 = (f32[8,128]{1,0:T(8,128)S(1)}, f32[8,128]{1,0:T(8,128)S(1)}, u32[]{:S(2)}, u32[]{:S(2)}) collective-permute-start(f32[8,128]{1,0:T(8,128)S(1)} %get-tuple-element.50.v_ref.v1), channel_id=1, source_target_pairs={{16,0},{32,16},{48,32},{64,48},{80,64},{96,80},{112,96},{128,112},... | collective-permute-start | bytes 12296 | tf_op jit(solution)/shard_map/ppermute | solution.py:469
  130.4 5.9 %collective-permute-start.10 = (f32[8,128]{1,0:T(8,128)S(1)}, f32[8,128]{1,0:T(8,128)S(1)}, u32[]{:S(2)}, u32[]{:S(2)}) collective-permute-start(f32[8,128]{1,0:T(8,128)S(1)} %get-tuple-element.40), channel_id=1, source_target_pairs={{0,16},{16,32},{32,48},{48,64},{64,80},{80,96},{96,112},{112,128},... | collective-permute-start | bytes 12296 | tf_op jit(solution)/shard_map/ppermute | solution.py:469
  134.4 6.8 %collective-permute-start.11 = (f32[8,128]{1,0:T(8,128)S(1)}, f32[8,128]{1,0:T(8,128)S(1)}, u32[]{:S(2)}, u32[]{:S(2)}) collective-permute-start(f32[8,128]{1,0:T(8,128)S(1)} %get-tuple-element.41), channel_id=1, source_target_pairs={{16,0},{32,16},{48,32},{64,48},{80,64},{96,80},{112,96},{128,112},... | collective-permute-start | bytes 12296 | tf_op jit(solution)/shard_map/ppermute | solution.py:469
  141.2 8.5 %collective-permute-start.15 = (f32[8,128]{1,0:T(8,128)S(1)}, f32[8,128]{1,0:T(8,128)S(1)}, u32[]{:S(2)}, u32[]{:S(2)}) collective-permute-start(f32[8,128]{1,0:T(8,128)S(1)} %get-tuple-element.48.v_ref.v2), channel_id=1, source_target_pairs={{0,1},{1,2},{2,3},{3,4},{4,5},{5,6},{6,7},{7,8},{8,9},{9,10},{10,1... | collective-permute-start | bytes 12296 | tf_op jit(solution)/shard_map/ppermute | solution.py:469
  142.5 7.2 %collective-permute-start.14 = (f32[8,128]{1,0:T(8,128)S(1)}, f32[8,128]{1,0:T(8,128)S(1)}, u32[]{:S(2)}, u32[]{:S(2)}) collective-permute-start(f32[8,128]{1,0:T(8,128)S(1)} %get-tuple-element.48.v_ref.v2), channel_id=1, source_target_pairs={{1,0},{2,1},{3,2},{4,3},{5,4},{6,5},{7,6},{8,7},{9,8},{10,9},{11,1... | collective-permute-start | bytes 12296 | tf_op jit(solution)/shard_map/ppermute | solution.py:469
  143.8 5.9 %collective-permute-start.13 = (f32[8,128]{1,0:T(8,128)S(1)}, f32[8,128]{1,0:T(8,128)S(1)}, u32[]{:S(2)}, u32[]{:S(2)}) collective-permute-start(f32[8,128]{1,0:T(8,128)S(1)} %get-tuple-element.48.v_ref.v2), channel_id=1, source_target_pairs={{0,16},{16,32},{32,48},{48,64},{64,80},{80,96},{96,112},{112,128},... | collective-permute-start | bytes 12296 | tf_op jit(solution)/shard_map/ppermute | solution.py:469
  147.7 6.8 %collective-permute-start.12 = (f32[8,128]{1,0:T(8,128)S(1)}, f32[8,128]{1,0:T(8,128)S(1)}, u32[]{:S(2)}, u32[]{:S(2)}) collective-permute-start(f32[8,128]{1,0:T(8,128)S(1)} %get-tuple-element.48.v_ref.v2), channel_id=1, source_target_pairs={{16,0},{32,16},{48,32},{64,48},{80,64},{96,80},{112,96},{128,112},... | collective-permute-start | bytes 12296 | tf_op jit(solution)/shard_map/ppermute | solution.py:469
  149.6 24.9 %copy-start.1 = (f32[512,512]{1,0:T(8,128)S(1)}, f32[512,512]{1,0:T(8,128)}, u32[]{:S(2)}) copy-start(f32[512,512]{1,0:T(8,128)} %copy-done) | copy-start | bytes 3145732
  174.5 42.5 %copy-start.4 = (f32[1,1,8,128]{3,2,1,0:T(8,128)S(1)}, f32[1,1,8,128]{3,2,1,0:T(8,128)}, u32[]{:S(2)}) copy-start(f32[1,1,8,128]{3,2,1,0:T(8,128)} %param.14) | copy-start | bytes 12292

commit v5 on v3

--- a/solution.py
+++ b/solution.py
@@ -152,8 +152,7 @@
         part = jnp.where(lane == total + s, column, part)
         fact = fact + (pltpu.roll(row, first, 1) if s else row)
         fact = fact + pltpu.roll(facts[slots + s : slots + s + 1, :], total + s * per, 1)
-    report_ref[:corners, :] = part
-    report_ref[corners:, :] = jnp.broadcast_to(fact, (8, LANES))
+    report_ref[...] = part
     facts_ref[...] = jnp.broadcast_to(fact.astype(jnp.int32), (8, LANES))
 
 
@@ -180,11 +179,12 @@
 ):
     count = gathered_ref.shape[0]
     total = slots * corners
+    told = start * 3 // 4 + 1
     n = diag_ref.shape[1]
     lane = iota((1, n), 1).astype(F32)
     for y in range(count):
         part = gathered_ref[y, start : start + corners, :]
-        rows_ref[y : y + 1, :] = gathered_ref[y, start + corners : start + corners + 1, :]
+        rows_ref[y : y + 1, :] = gathered_ref[y, told : told + 1, :]
         for s in range(slots):
             block = part[:, s * corners : (s + 1) * corners]
             place = part[:, total + s : total + s + 1]
@@ -196,7 +196,7 @@
     for g, by in enumerate((0, 1, -1)):
         there = y_ref[0] + by
         y = jnp.clip(there, 0, count - 1)
-        fact = gathered_ref[y, start + corners : start + corners + 1, :].astype(jnp.int32)
+        fact = gathered_ref[y, told : told + 1, :].astype(jnp.int32)
         facts_ref[g : g + 1, :] = jnp.where((there >= 0) & (there < count), fact, 0)
         part = gathered_ref[y, start : start + corners, :]
         for s in range(slots):
@@ -310,6 +310,8 @@
         else:
             pay_ref[4 * owned :, :] = ref[...]
     block = jnp.where(at == 0, pay, 0.0)
+    if not sweep:
+        block = jnp.where(at == 1, facts_ref[:1, :].astype(F32), block)
     for g in range(1, groups):
         block = jnp.where(at == g, pays[g], block)
     pay_ref[3 * owned : 4 * owned, :] = block
@@ -403,7 +405,7 @@
 
 
 def final_kernel(first, gathered_ref, rhs_ref, v0, v1, v2, w0, w1, mine, east, west, x_ref, r_ref):
-    sums = gathered_ref[...]
+    sums = jnp.sum(gathered_ref[...], axis=0, keepdims=True)
     lane = iota((1, LANES), 1)
 
     def moment(i):
@@ -475,7 +477,7 @@
         "setup",
         [
             (slots * rows + 16, width),
-            (corners + 8, LANES),
+            (corners, LANES),
             (LANES, LANES),
             facts_shape,
         ],
@@ -556,9 +558,9 @@
             images.append(image)
             last, direction = image, STEP * scale * image
     across = lax.axis_size("gx")
-    for group in (runs(across, 4), strided(across, 4)):
-        sums = lax.all_gather(sums, "gx", axis=0, tiled=True, axis_index_groups=group)
-        sums = jnp.sum(sums, axis=0, keepdims=True)
+    sums = lax.all_gather(sums, "gx", axis=0, tiled=True, axis_index_groups=runs(across, 4))
+    sums = jnp.sum(sums, axis=0, keepdims=True)
+    sums = lax.all_gather(sums, "gx", axis=0, tiled=True, axis_index_groups=strided(across, 4))
     multipliers, residual = call(
         functools.partial(final_kernel, total),
         "final",

time: 211 us -> 211 us (level)
  no operation moved by 1% of the time
where the time goes in v5:
time: 211 us; the launch traced here: 210 us
  blocking collectives  85.3 us (40%)
  starting transfers between devices  65.4 us (31%)
  Pallas kernels  46.9 us (22%)
  waiting for transfers between devices  5.2 us (2%)
  local copies, waits for them, and re-layouts  4.49 us (2%)
    ppermute x18, starting transfers between devices, moved(): lax.ppermute(x, axis, [(i, i + by) for i in range(count) if 0 <= i + by <...  65.4 us
    all_gather x3, blocking collectives, shards(): gathered = lax.all_gather(pay, 'gy')  62.6 us
    pallas_call x10, Pallas kernels, call(): pl.pallas_call(kernel, out_shape=outs, in_specs=[smem] * len(scalars) + [...  46.9 us
    all_gather x1, blocking collectives, shards(): lax.all_gather(sums, 'gx', axis=0, tiled=True, axis_index_groups=strided(...  15.7 us
    all_gather x1, blocking collectives, shards(): lax.all_gather(sums, 'gx', axis=0, tiled=True, axis_index_groups=runs(acr...  6.92 us
    ppermute x18, waiting for transfers between devices, moved(): lax.ppermute(x, axis, [(i, i + by) for i in range(count) if 0 <= i + by <...  5.2 us
    unnamed x18, local copies, waits for them, and re-layouts  4.49 us
  transfers between devices with their start and end apart: 18, of which 4 were waited for; matrix products, arithmetic and copies ran while one was open for 0% of the time, Pallas kernels for 11%

profile of v5, /device:TPU:32, one launch (start us, length us, event | category | flops | bytes accessed | tf_op | source)
XLA Modules:
  0.0 209.7 jit_solution(2046047332672595453)
XLA Ops:
  0.6 0.7 bitcast_multiply_fusion.v_ref.v0
  1.3 1.7 collective-permute-start.3
  3.1 1.3 collective-permute-start.2
  4.4 3.4 %collective-permute-start.1 = (f32[8,128]{1,0:T(8,128)S(1)}, f32[8,128]{1,0:T(8,128)S(1)}, u32[]{:S(2)}, u32[]{:S(2)}) collective-permute-start(f32[8,128]{1,0:T(8,128)S(1)} %bitcast_multiply_fusion.v_ref.v0), channel_id=1, source_target_pairs={{0,16},{16,32},{32,48},{48,64},{64,80},{80,96},{96,112},{112,128},... | collective-permute-start | bytes 12296 | tf_op jit(solution)/shard_map/ppermute | solution.py:448
  7.8 5.8 %collective-permute-start = (f32[8,128]{1,0:T(8,128)S(1)}, f32[8,128]{1,0:T(8,128)S(1)}, u32[]{:S(2)}, u32[]{:S(2)}) collective-permute-start(f32[8,128]{1,0:T(8,128)S(1)} %bitcast_multiply_fusion.v_ref.v0), channel_id=1, source_target_pairs={{16,0},{32,16},{48,32},{64,48},{80,64},{96,80},{112,96},{128,112},... | collective-permute-start | bytes 12296 | tf_op jit(solution)/shard_map/ppermute | solution.py:448
  14.2 0.0 copy-start
  14.2 1.0 copy-done
  15.2 0.7 copy-done.3
  16.0 0.7 copy-done.4
  16.7 0.7 copy-done.6
  17.3 0.7 copy-done.7
  18.0 0.8 setup.1
  18.8 0.0 collective-permute-done.3.rest_4_
  18.8 0.0 collective-permute-done.2.rest_3_
  18.9 0.0 collective-permute-done.1.rest_2_
  18.9 0.0 collective-permute-done.rest_1_
  18.9 0.0 copy-start.1
  18.9 0.7 copy-done.1
  19.6 1.3 before.3
  20.9 26.9 %all-gather = f32[896,128]{1,0:T(8,128)S(1)} all-gather(f32[56,128]{1,0:T(8,128)S(1)} %before.3), channel_id=2, replica_groups=mesh['gx'=32,'gy'=16] {'gy'}, dimensions={0}, use_global_device_ids=true | all-gather | bytes 487424 | tf_op jit(solution)/shard_map/all_gather | solution.py:532
  47.8 0.0 copy-done.5
  47.8 9.6 %coarse.1 = (f32[512,512]{1,0:T(8,128)S(1)}, f32[16,128]{1,0:T(8,128)S(1)}, f32[144,128]{1,0:T(8,128)S(1)}, s32[8,128]{1,0:T(8,128)S(1)}) custom-call(s32[1]{0:T(128)} %bitcast.y_ref, f32[16,56,128]{2,1,0:T(8,128)S(1)} %bitcast.23, f32[1,512]{1,0:T(1,128)S(1)} %copy-done.5), custom_call_target="tpu_custom_call" | custom-call | tf_op jit(solution)/shard_map/coarse/pallas_call | solution.py:435
  57.4 2.3 %collective-permute-start.5 = (f32[272,1024]{1,0:T(8,128)S(1)}, f32[272,1024]{1,0:T(8,128)S(1)}, u32[]{:S(2)}, u32[]{:S(2)}) collective-permute-start(f32[272,1024]{1,0:T(8,128)S(1)} %get-tuple-element.36.rest_0_), channel_id=1, source_target_pairs={{0,1},{1,2},{2,3},{3,4},{4,5},{5,6},{6,7},{7,8},{8,9},{9,10},{10,1... | collective-permute-start | bytes 3342344 | tf_op jit(solution)/shard_map/ppermute | solution.py:448
  59.8 1.5 collective-permute-start.4
  61.2 22.4 %rest.1.inverse_ref = f32[512,512]{1,0:T(8,128)S(1)} custom-call(f32[512,512]{1,0:T(8,128)S(1)} %get-tuple-element.35.system_ref), custom_call_target="tpu_custom_call" | custom-call | tf_op jit(solution)/shard_map/rest/pallas_call | solution.py:435
  83.6 0.0 collective-permute-done.5.rest_2_
  83.6 0.0 collective-permute-done.4.rest_1_
  83.7 0.0 copy-start.8
  83.7 2.8 %after.3 = (f32[8,128]{1,0:T(8,128)S(1)}, f32[8,128]{1,0:T(8,128)S(1)}, f32[8,128]{1,0:T(8,128)S(1)}, f32[1,128]{1,0:T(1,128)S(1)}) custom-call(s32[1]{0:T(128)} %bitcast.y_ref, f32[16,56,128]{2,1,0:T(8,128)S(1)} %bitcast.24, f32[16,128]{1,0:T(8,128)S(1)} %get-tuple-element.31.rows_ref, f32[144,128]{1,0:T(8,128)S(1)} %get-tuple-element.32.places_ref, ...), custom_call_target="tpu_custom_call" | custom-call | tf_op jit(solution)/shard_map/after/pallas_call | solution.py:435
  86.5 1.9 collective-permute-start.6
  88.4 7.2 %collective-permute-start.7 = (f32[8,128]{1,0:T(8,128)S(1)}, f32[8,128]{1,0:T(8,128)S(1)}, u32[]{:S(2)}, u32[]{:S(2)}) collective-permute-start(f32[8,128]{1,0:T(8,128)S(1)} %get-tuple-element.39), channel_id=1, source_target_pairs={{16,0},{32,16},{48,32},{64,48},{80,64},{96,80},{112,96},{128,112},... | collective-permute-start | bytes 12296 | tf_op jit(solution)/shard_map/ppermute | solution.py:448
  95.7 0.0 collective-permute-done.6
  95.7 1.3 collective-permute-done.7
  97.0 0.0 copy-done.8
  97.0 1.9 collective-permute-start.9
  98.9 7.5 %collective-permute-start.8 = (f32[8,128]{1,0:T(8,128)S(1)}, f32[8,128]{1,0:T(8,128)S(1)}, u32[]{:S(2)}, u32[]{:S(2)}) collective-permute-start(f32[8,128]{1,0:T(8,128)S(1)} %get-tuple-element.54.v_ref.v1), channel_id=1, source_target_pairs={{16,0},{32,16},{48,32},{64,48},{80,64},{96,80},{112,96},{128,112},... | collective-permute-start | bytes 12296 | tf_op jit(solution)/shard_map/ppermute | solution.py:448
  106.4 0.0 collective-permute-done.9.rest_4_
  106.4 1.3 collective-permute-done.8.rest_3_
  107.7 2.3 %before.4 = f32[32,128]{1,0:T(8,128)S(1)} custom-call(f32[8,128]{1,0:T(8,128)S(1)} %get-tuple-element.54.v_ref.v1, f32[8,128]{1,0:T(8,128)S(1)} %get-tuple-element.55.last_ref.w0, f32[128,128]{1,0:T(8,128)S(1)} %get-tuple-element.27.corner_ref, s32[8,128]{1,0:T(8,128)S(1)} %get-tuple-element.33.facts_ref, f32[272,1024]{1,0:T(8,128)S(1)} %get-tuple-element.36.rest_0_, ...), custom_call_target="tpu_custom_call" | custom-call | tf_op jit(solution)/shard_map/before/pallas_call | solution.py:435
  110.1 17.0 %all-gather.1 = f32[512,128]{1,0:T(8,128)S(1)} all-gather(f32[32,128]{1,0:T(8,128)S(1)} %before.4), channel_id=3, replica_groups=mesh['gx'=32,'gy'=16] {'gy'}, dimensions={0}, use_global_device_ids=true | all-gather | bytes 278528 | tf_op jit(solution)/shard_map/all_gather | solution.py:532
  127.1 2.9 %after.4 = (f32[8,128]{1,0:T(8,128)S(1)}, f32[8,128]{1,0:T(8,128)S(1)}, f32[8,128]{1,0:T(8,128)S(1)}, f32[1,128]{1,0:T(1,128)S(1)}, f32[1,128]{1,0:T(1,128)S(1)}) custom-call(s32[1]{0:T(128)} %bitcast.y_ref, f32[16,32,128]{2,1,0:T(8,128)S(1)} %bitcast.26, f32[16,128]{1,0:T(8,128)S(1)} %get-tuple-element.31.rows_ref, ...), custom_call_target="tpu_custom_call" | custom-call | tf_op jit(solution)/shard_map/after/pallas_call | solution.py:435
  129.9 1.9 collective-permute-start.10
  131.9 7.5 %collective-permute-start.11 = (f32[8,128]{1,0:T(8,128)S(1)}, f32[8,128]{1,0:T(8,128)S(1)}, u32[]{:S(2)}, u32[]{:S(2)}) collective-permute-start(f32[8,128]{1,0:T(8,128)S(1)} %get-tuple-element.43), channel_id=1, source_target_pairs={{16,0},{32,16},{48,32},{64,48},{80,64},{96,80},{112,96},{128,112},... | collective-permute-start | bytes 12296 | tf_op jit(solution)/shard_map/ppermute | solution.py:448
  139.4 0.0 collective-permute-done.10
  139.4 1.3 collective-permute-done.11
  140.7 1.4 collective-permute-start.15
  142.1 1.3 collective-permute-start.14
  143.4 1.9 collective-permute-start.13
  145.3 7.4 %collective-permute-start.12 = (f32[8,128]{1,0:T(8,128)S(1)}, f32[8,128]{1,0:T(8,128)S(1)}, u32[]{:S(2)}, u32[]{:S(2)}) collective-permute-start(f32[8,128]{1,0:T(8,128)S(1)} %get-tuple-element.52.v_ref.v2), channel_id=1, source_target_pairs={{16,0},{32,16},{48,32},{64,48},{80,64},{96,80},{112,96},{128,112},... | collective-permute-start | bytes 12296 | tf_op jit(solution)/shard_map/ppermute | solution.py:448
  152.7 0.0 collective-permute-done.15.rest_4_
  152.7 0.0 collective-permute-done.14.rest_3_
  152.8 0.0 collective-permute-done.13.rest_2_
  152.8 1.3 collective-permute-done.12.rest_1_
  154.0 1.3 before.5
  155.3 18.7 %all-gather.2 = f32[512,128]{1,0:T(8,128)S(1)} all-gather(f32[32,128]{1,0:T(8,128)S(1)} %before.5), channel_id=4, replica_groups=mesh['gx'=32,'gy'=16] {'gy'}, dimensions={0}, use_global_device_ids=true | all-gather | bytes 278528 | tf_op jit(solution)/shard_map/all_gather | solution.py:532
  174.0 2.8 %after.5 = (f32[8,128]{1,0:T(8,128)S(1)}, f32[8,128]{1,0:T(8,128)S(1)}, f32[8,128]{1,0:T(8,128)S(1)}, f32[1,128]{1,0:T(1,128)S(1)}) custom-call(s32[1]{0:T(128)} %bitcast.y_ref, f32[16,32,128]{2,1,0:T(8,128)S(1)} %bitcast.25, f32[16,128]{1,0:T(8,128)S(1)} %get-tuple-element.31.rows_ref, f32[144,128]{1,0:T(8,128)S(1)} %get-tuple-element.32.places_ref, ...), custom_call_target="tpu_custom_call" | custom-call | tf_op jit(solution)/shard_map/after/pallas_call | solution.py:435
  176.8 1.9 collective-permute-start.16
  178.7 7.5 %collective-permute-start.17 = (f32[8,128]{1,0:T(8,128)S(1)}, f32[8,128]{1,0:T(8,128)S(1)}, u32[]{:S(2)}, u32[]{:S(2)}) collective-permute-start(f32[8,128]{1,0:T(8,128)S(1)} %get-tuple-element.49), channel_id=1, source_target_pairs={{16,0},{32,16},{48,32},{64,48},{80,64},{96,80},{112,96},{128,112},... | collective-permute-start | bytes 12296 | tf_op jit(solution)/shard_map/ppermute | solution.py:448
  186.2 6.9 %all-gather.4 = f32[4,1,128]{2,1,0:T(1,128)S(1)} all-gather(f32[1,1,128]{2,1,0:T(1,128)S(1)} %bitcast.35), channel_id=1, replica_groups={{0,16,32,48},{64,80,96,112},{128,144,160,176},{192,208,224,240},{256,27..., dimensions={0}, use_global_device_ids=true | all-gather | bytes 2560 | tf_op jit(solution)/shard_map/all_gather | solution.py:561
  193.2 15.7 %all-gather.5 = f32[8,1,128]{2,1,0:T(1,128)S(1)} all-gather(f32[1,1,128]{2,1,0:T(1,128)S(1)} %bitcast.36), channel_id=5, replica_groups={{0,64,128,192,256,320,384,448},{16,80,144,208,272,336,400,464},{32,96,1..., dimensions={0}, use_global_device_ids=true | all-gather | bytes 4608 | tf_op jit(solution)/shard_map/all_gather | solution.py:563
  208.9 0.0 collective-permute-done.16.east
  208.9 0.0 collective-permute-done.17.west
  208.9 0.0 copy-done.2
  208.9 0.7 final.1
  (9 shorter events, 0.0 us)
Async XLA Ops:
  1.3 17.5 %collective-permute-start.3 = (f32[8,128]{1,0:T(8,128)S(1)}, f32[8,128]{1,0:T(8,128)S(1)}, u32[]{:S(2)}, u32[]{:S(2)}) collective-permute-start(f32[8,128]{1,0:T(8,128)S(1)} %bitcast_multiply_fusion.v_ref.v0), channel_id=1, source_target_pairs={{0,1},{1,2},{2,3},{3,4},{4,5},{5,6},{6,7},{7,8},{8,9},{9,10},{10,1... | collective-permute-start | bytes 12296 | tf_op jit(solution)/shard_map/ppermute | solution.py:448
  3.1 15.8 %collective-permute-start.2 = (f32[8,128]{1,0:T(8,128)S(1)}, f32[8,128]{1,0:T(8,128)S(1)}, u32[]{:S(2)}, u32[]{:S(2)}) collective-permute-start(f32[8,128]{1,0:T(8,128)S(1)} %bitcast_multiply_fusion.v_ref.v0), channel_id=1, source_target_pairs={{1,0},{2,1},{3,2},{4,3},{5,4},{6,5},{7,6},{8,7},{9,8},{10,9},{11,1... | collective-permute-start | bytes 12296 | tf_op jit(solution)/shard_map/ppermute | solution.py:448
  4.4 14.5 %collective-permute-start.1 = (f32[8,128]{1,0:T(8,128)S(1)}, f32[8,128]{1,0:T(8,128)S(1)}, u32[]{:S(2)}, u32[]{:S(2)}) collective-permute-start(f32[8,128]{1,0:T(8,128)S(1)} %bitcast_multiply_fusion.v_ref.v0), channel_id=1, source_target_pairs={{0,16},{16,32},{32,48},{48,64},{64,80},{80,96},{96,112},{112,128},... | collective-permute-start | bytes 12296 | tf_op jit(solution)/shard_map/ppermute | solution.py:448
  7.8 11.1 %collective-permute-start = (f32[8,128]{1,0:T(8,128)S(1)}, f32[8,128]{1,0:T(8,128)S(1)}, u32[]{:S(2)}, u32[]{:S(2)}) collective-permute-start(f32[8,128]{1,0:T(8,128)S(1)} %bitcast_multiply_fusion.v_ref.v0), channel_id=1, source_target_pairs={{16,0},{32,16},{48,32},{64,48},{80,64},{96,80},{112,96},{128,112},... | collective-permute-start | bytes 12296 | tf_op jit(solution)/shard_map/ppermute | solution.py:448
  14.2 1.0 copy-start
  15.2 0.7 copy-start.3
  16.0 0.7 copy-start.4
  16.7 0.7 copy-start.6
  17.3 0.7 copy-start.7
  18.0 29.8 %copy-start.5 = (f32[1,512]{1,0:T(1,128)S(1)}, f32[1,512]{1,0:T(1,128)}, u32[]{:S(2)}) copy-start(f32[1,512]{1,0:T(1,128)} %diag_ref.1) | copy-start | bytes 6148
  18.9 0.7 copy-start.1
  57.4 26.2 %collective-permute-start.5 = (f32[272,1024]{1,0:T(8,128)S(1)}, f32[272,1024]{1,0:T(8,128)S(1)}, u32[]{:S(2)}, u32[]{:S(2)}) collective-permute-start(f32[272,1024]{1,0:T(8,128)S(1)} %get-tuple-element.36.rest_0_), channel_id=1, source_target_pairs={{0,1},{1,2},{2,3},{3,4},{4,5},{5,6},{6,7},{7,8},{8,9},{9,10},{10,1... | collective-permute-start | bytes 3342344 | tf_op jit(solution)/shard_map/ppermute | solution.py:448
  59.8 23.9 %collective-permute-start.4 = (f32[272,1024]{1,0:T(8,128)S(1)}, f32[272,1024]{1,0:T(8,128)S(1)}, u32[]{:S(2)}, u32[]{:S(2)}) collective-permute-start(f32[272,1024]{1,0:T(8,128)S(1)} %get-tuple-element.36.rest_0_), channel_id=1, source_target_pairs={{1,0},{2,1},{3,2},{4,3},{5,4},{6,5},{7,6},{8,7},{9,8},{10,9},{11,1... | collective-permute-start | bytes 3342344 | tf_op jit(solution)/shard_map/ppermute | solution.py:448
  83.7 13.3 %copy-start.8 = (f32[1,1,8,128]{3,2,1,0:T(8,128)S(1)}, f32[1,1,8,128]{3,2,1,0:T(8,128)}, u32[]{:S(2)}) copy-start(f32[1,1,8,128]{3,2,1,0:T(8,128)} %param.13) | copy-start | bytes 12292
  86.5 9.2 %collective-permute-start.6 = (f32[8,128]{1,0:T(8,128)S(1)}, f32[8,128]{1,0:T(8,128)S(1)}, u32[]{:S(2)}, u32[]{:S(2)}) collective-permute-start(f32[8,128]{1,0:T(8,128)S(1)} %get-tuple-element.38), channel_id=1, source_target_pairs={{0,16},{16,32},{32,48},{48,64},{64,80},{80,96},{96,112},{112,128},... | collective-permute-start | bytes 12296 | tf_op jit(solution)/shard_map/ppermute | solution.py:448
  88.4 8.6 %collective-permute-start.7 = (f32[8,128]{1,0:T(8,128)S(1)}, f32[8,128]{1,0:T(8,128)S(1)}, u32[]{:S(2)}, u32[]{:S(2)}) collective-permute-start(f32[8,128]{1,0:T(8,128)S(1)} %get-tuple-element.39), channel_id=1, source_target_pairs={{16,0},{32,16},{48,32},{64,48},{80,64},{96,80},{112,96},{128,112},... | collective-permute-start | bytes 12296 | tf_op jit(solution)/shard_map/ppermute | solution.py:448
  97.0 9.4 %collective-permute-start.9 = (f32[8,128]{1,0:T(8,128)S(1)}, f32[8,128]{1,0:T(8,128)S(1)}, u32[]{:S(2)}, u32[]{:S(2)}) collective-permute-start(f32[8,128]{1,0:T(8,128)S(1)} %get-tuple-element.54.v_ref.v1), channel_id=1, source_target_pairs={{0,16},{16,32},{32,48},{48,64},{64,80},{80,96},{96,112},{112,128},... | collective-permute-start | bytes 12296 | tf_op jit(solution)/shard_map/ppermute | solution.py:448
  98.9 8.8 %collective-permute-start.8 = (f32[8,128]{1,0:T(8,128)S(1)}, f32[8,128]{1,0:T(8,128)S(1)}, u32[]{:S(2)}, u32[]{:S(2)}) collective-permute-start(f32[8,128]{1,0:T(8,128)S(1)} %get-tuple-element.54.v_ref.v1), channel_id=1, source_target_pairs={{16,0},{32,16},{48,32},{64,48},{80,64},{96,80},{112,96},{128,112},... | collective-permute-start | bytes 12296 | tf_op jit(solution)/shard_map/ppermute | solution.py:448
  129.9 9.4 %collective-permute-start.10 = (f32[8,128]{1,0:T(8,128)S(1)}, f32[8,128]{1,0:T(8,128)S(1)}, u32[]{:S(2)}, u32[]{:S(2)}) collective-permute-start(f32[8,128]{1,0:T(8,128)S(1)} %get-tuple-element.42), channel_id=1, source_target_pairs={{0,16},{16,32},{32,48},{48,64},{64,80},{80,96},{96,112},{112,128},... | collective-permute-start | bytes 12296 | tf_op jit(solution)/shard_map/ppermute | solution.py:448
  131.9 8.8 %collective-permute-start.11 = (f32[8,128]{1,0:T(8,128)S(1)}, f32[8,128]{1,0:T(8,128)S(1)}, u32[]{:S(2)}, u32[]{:S(2)}) collective-permute-start(f32[8,128]{1,0:T(8,128)S(1)} %get-tuple-element.43), channel_id=1, source_target_pairs={{16,0},{32,16},{48,32},{64,48},{80,64},{96,80},{112,96},{128,112},... | collective-permute-start | bytes 12296 | tf_op jit(solution)/shard_map/ppermute | solution.py:448
  140.7 12.0 %collective-permute-start.15 = (f32[8,128]{1,0:T(8,128)S(1)}, f32[8,128]{1,0:T(8,128)S(1)}, u32[]{:S(2)}, u32[]{:S(2)}) collective-permute-start(f32[8,128]{1,0:T(8,128)S(1)} %get-tuple-element.52.v_ref.v2), channel_id=1, source_target_pairs={{0,1},{1,2},{2,3},{3,4},{4,5},{5,6},{6,7},{7,8},{8,9},{9,10},{10,1... | collective-permute-start | bytes 12296 | tf_op jit(solution)/shard_map/ppermute | solution.py:448
  142.1 10.7 %collective-permute-start.14 = (f32[8,128]{1,0:T(8,128)S(1)}, f32[8,128]{1,0:T(8,128)S(1)}, u32[]{:S(2)}, u32[]{:S(2)}) collective-permute-start(f32[8,128]{1,0:T(8,128)S(1)} %get-tuple-element.52.v_ref.v2), channel_id=1, source_target_pairs={{1,0},{2,1},{3,2},{4,3},{5,4},{6,5},{7,6},{8,7},{9,8},{10,9},{11,1... | collective-permute-start | bytes 12296 | tf_op jit(solution)/shard_map/ppermute | solution.py:448
  143.4 9.4 %collective-permute-start.13 = (f32[8,128]{1,0:T(8,128)S(1)}, f32[8,128]{1,0:T(8,128)S(1)}, u32[]{:S(2)}, u32[]{:S(2)}) collective-permute-start(f32[8,128]{1,0:T(8,128)S(1)} %get-tuple-element.52.v_ref.v2), channel_id=1, source_target_pairs={{0,16},{16,32},{32,48},{48,64},{64,80},{80,96},{96,112},{112,128},... | collective-permute-start | bytes 12296 | tf_op jit(solution)/shard_map/ppermute | solution.py:448
  145.3 8.7 %collective-permute-start.12 = (f32[8,128]{1,0:T(8,128)S(1)}, f32[8,128]{1,0:T(8,128)S(1)}, u32[]{:S(2)}, u32[]{:S(2)}) collective-permute-start(f32[8,128]{1,0:T(8,128)S(1)} %get-tuple-element.52.v_ref.v2), channel_id=1, source_target_pairs={{16,0},{32,16},{48,32},{64,48},{80,64},{96,80},{112,96},{128,112},... | collective-permute-start | bytes 12296 | tf_op jit(solution)/shard_map/ppermute | solution.py:448
  174.0 34.9 %copy-start.2 = (f32[1,1,8,128]{3,2,1,0:T(8,128)S(1)}, f32[1,1,8,128]{3,2,1,0:T(8,128)}, u32[]{:S(2)}) copy-start(f32[1,1,8,128]{3,2,1,0:T(8,128)} %param.14) | copy-start | bytes 12292
  176.8 32.1 %collective-permute-start.16 = (f32[8,128]{1,0:T(8,128)S(1)}, f32[8,128]{1,0:T(8,128)S(1)}, u32[]{:S(2)}, u32[]{:S(2)}) collective-permute-start(f32[8,128]{1,0:T(8,128)S(1)} %get-tuple-element.48), channel_id=1, source_target_pairs={{0,16},{16,32},{32,48},{48,64},{64,80},{80,96},{96,112},{112,128},... | collective-permute-start | bytes 12296 | tf_op jit(solution)/shard_map/ppermute | solution.py:448
  178.7 30.2 %collective-permute-start.17 = (f32[8,128]{1,0:T(8,128)S(1)}, f32[8,128]{1,0:T(8,128)S(1)}, u32[]{:S(2)}, u32[]{:S(2)}) collective-permute-start(f32[8,128]{1,0:T(8,128)S(1)} %get-tuple-element.49), channel_id=1, source_target_pairs={{16,0},{32,16},{48,32},{64,48},{80,64},{96,80},{112,96},{128,112},... | collective-permute-start | bytes 12296 | tf_op jit(solution)/shard_map/ppermute | solution.py:448

commit v6 on v3

--- a/solution.py
+++ b/solution.py
@@ -211,12 +211,12 @@
             hots, piece.astype(BF16), (((0,), (0,)), ((), ())), preferred_element_type=F32
         )
     out_ref[...] = system
-    eliminated(out_ref, 0, 1)
+    eliminated(out_ref, 0, 2)
 
 
 def rest_kernel(system_ref, out_ref):
     out_ref[...] = system_ref[...]
-    eliminated(out_ref, 1, out_ref.shape[0] // LANES)
+    eliminated(out_ref, 2, out_ref.shape[0] // LANES)
 
 
 def eliminated(out_ref, first, last):

time: 211 us -> 211 us (level)
  transfers between devices with their start and end apart: 18 -> 18, of which waited for: 4 -> 4; matrix products, arithmetic and copies ran while one was open for 0% -> 0% of each run, Pallas kernels for 11% -> 7%
where the time goes in v6:
time: 211 us; the launch traced here: 210 us
  blocking collectives  85.4 us (40%)
  starting transfers between devices  65.4 us (31%)
  Pallas kernels  47.1 us (22%)
  waiting for transfers between devices  5.2 us (2%)
  local copies, waits for them, and re-layouts  4.49 us (2%)
    ppermute x18, starting transfers between devices, moved(): lax.ppermute(x, axis, [(i, i + by) for i in range(count) if 0 <= i + by <...  65.4 us
    all_gather x3, blocking collectives, shards(): gathered = lax.all_gather(pay, 'gy')  62.8 us
    pallas_call x10, Pallas kernels, call(): pl.pallas_call(kernel, out_shape=outs, in_specs=[smem] * len(scalars) + [...  47.1 us
    all_gather x2, blocking collectives, shards(): lax.all_gather(sums, 'gx', axis=0, tiled=True, axis_index_groups=group)  22.7 us
    ppermute x18, waiting for transfers between devices, moved(): lax.ppermute(x, axis, [(i, i + by) for i in range(count) if 0 <= i + by <...  5.2 us
    unnamed x18, local copies, waits for them, and re-layouts  4.49 us
  transfers between devices with their start and end apart: 18, of which 4 were waited for; matrix products, arithmetic and copies ran while one was open for 0% of the time, Pallas kernels for 7%

profile of v6, /device:TPU:32, one launch (start us, length us, event | category | flops | bytes accessed | tf_op | source)
XLA Modules:
  0.0 210.1 jit_solution(11689662124098151587)
XLA Ops:
  0.6 0.7 bitcast_multiply_fusion.v_ref.v0
  1.3 1.7 collective-permute-start.3
  3.1 1.3 collective-permute-start.2
  4.4 3.4 %collective-permute-start.1 = (f32[8,128]{1,0:T(8,128)S(1)}, f32[8,128]{1,0:T(8,128)S(1)}, u32[]{:S(2)}, u32[]{:S(2)}) collective-permute-start(f32[8,128]{1,0:T(8,128)S(1)} %bitcast_multiply_fusion.v_ref.v0), channel_id=1, source_target_pairs={{0,16},{16,32},{32,48},{48,64},{64,80},{80,96},{96,112},{112,128},... | collective-permute-start | bytes 12296 | tf_op jit(solution)/shard_map/ppermute | solution.py:446
  7.8 5.8 %collective-permute-start = (f32[8,128]{1,0:T(8,128)S(1)}, f32[8,128]{1,0:T(8,128)S(1)}, u32[]{:S(2)}, u32[]{:S(2)}) collective-permute-start(f32[8,128]{1,0:T(8,128)S(1)} %bitcast_multiply_fusion.v_ref.v0), channel_id=1, source_target_pairs={{16,0},{32,16},{48,32},{64,48},{80,64},{96,80},{112,96},{128,112},... | collective-permute-start | bytes 12296 | tf_op jit(solution)/shard_map/ppermute | solution.py:446
  14.2 0.0 copy-start
  14.2 1.0 copy-done
  15.2 0.7 copy-done.3
  16.0 0.7 copy-done.4
  16.7 0.7 copy-done.6
  17.3 0.7 copy-done.7
  18.0 0.8 setup.1
  18.8 0.0 collective-permute-done.3.rest_4_
  18.8 0.0 collective-permute-done.2.rest_3_
  18.9 0.0 collective-permute-done.1.rest_2_
  18.9 0.0 collective-permute-done.rest_1_
  18.9 0.0 copy-start.1
  18.9 0.7 copy-done.1
  19.6 1.3 before.3
  20.9 27.1 %all-gather = f32[1024,128]{1,0:T(8,128)S(1)} all-gather(f32[64,128]{1,0:T(8,128)S(1)} %before.3), channel_id=2, replica_groups=mesh['gx'=32,'gy'=16] {'gy'}, dimensions={0}, use_global_device_ids=true | all-gather | bytes 557056 | tf_op jit(solution)/shard_map/all_gather | solution.py:530
  48.0 0.0 copy-done.5
  48.0 17.2 %coarse.1 = (f32[512,512]{1,0:T(8,128)S(1)}, f32[16,128]{1,0:T(8,128)S(1)}, f32[144,128]{1,0:T(8,128)S(1)}, s32[8,128]{1,0:T(8,128)S(1)}) custom-call(s32[1]{0:T(128)} %bitcast.y_ref, f32[16,64,128]{2,1,0:T(8,128)S(1)} %bitcast.23, f32[1,512]{1,0:T(1,128)S(1)} %copy-done.5), custom_call_target="tpu_custom_call" | custom-call | tf_op jit(solution)/shard_map/coarse/pallas_call | solution.py:433
  65.2 2.3 %collective-permute-start.5 = (f32[272,1024]{1,0:T(8,128)S(1)}, f32[272,1024]{1,0:T(8,128)S(1)}, u32[]{:S(2)}, u32[]{:S(2)}) collective-permute-start(f32[272,1024]{1,0:T(8,128)S(1)} %get-tuple-element.36.rest_0_), channel_id=1, source_target_pairs={{0,1},{1,2},{2,3},{3,4},{4,5},{5,6},{6,7},{7,8},{8,9},{9,10},{10,1... | collective-permute-start | bytes 3342344 | tf_op jit(solution)/shard_map/ppermute | solution.py:446
  67.6 1.5 collective-permute-start.4
  69.1 14.9 %rest.1.inverse_ref = f32[512,512]{1,0:T(8,128)S(1)} custom-call(f32[512,512]{1,0:T(8,128)S(1)} %get-tuple-element.35.system_ref), custom_call_target="tpu_custom_call" | custom-call | tf_op jit(solution)/shard_map/rest/pallas_call | solution.py:433
  84.0 0.0 collective-permute-done.5.rest_2_
  84.0 0.0 collective-permute-done.4.rest_1_
  84.0 0.0 copy-start.8
  84.0 2.8 %after.3 = (f32[8,128]{1,0:T(8,128)S(1)}, f32[8,128]{1,0:T(8,128)S(1)}, f32[8,128]{1,0:T(8,128)S(1)}, f32[1,128]{1,0:T(1,128)S(1)}) custom-call(s32[1]{0:T(128)} %bitcast.y_ref, f32[16,64,128]{2,1,0:T(8,128)S(1)} %bitcast.24, f32[16,128]{1,0:T(8,128)S(1)} %get-tuple-element.31.rows_ref, f32[144,128]{1,0:T(8,128)S(1)} %get-tuple-element.32.places_ref, ...), custom_call_target="tpu_custom_call" | custom-call | tf_op jit(solution)/shard_map/after/pallas_call | solution.py:433
  86.9 1.9 collective-permute-start.6
  88.8 7.2 %collective-permute-start.7 = (f32[8,128]{1,0:T(8,128)S(1)}, f32[8,128]{1,0:T(8,128)S(1)}, u32[]{:S(2)}, u32[]{:S(2)}) collective-permute-start(f32[8,128]{1,0:T(8,128)S(1)} %get-tuple-element.39), channel_id=1, source_target_pairs={{16,0},{32,16},{48,32},{64,48},{80,64},{96,80},{112,96},{128,112},... | collective-permute-start | bytes 12296 | tf_op jit(solution)/shard_map/ppermute | solution.py:446
  96.0 0.0 collective-permute-done.6
  96.0 1.3 collective-permute-done.7
  97.3 0.0 copy-done.8
  97.3 1.9 collective-permute-start.9
  99.3 7.5 %collective-permute-start.8 = (f32[8,128]{1,0:T(8,128)S(1)}, f32[8,128]{1,0:T(8,128)S(1)}, u32[]{:S(2)}, u32[]{:S(2)}) collective-permute-start(f32[8,128]{1,0:T(8,128)S(1)} %get-tuple-element.54.v_ref.v1), channel_id=1, source_target_pairs={{16,0},{32,16},{48,32},{64,48},{80,64},{96,80},{112,96},{128,112},... | collective-permute-start | bytes 12296 | tf_op jit(solution)/shard_map/ppermute | solution.py:446
  106.8 0.0 collective-permute-done.9.rest_4_
  106.8 1.3 collective-permute-done.8.rest_3_
  108.1 2.3 %before.4 = f32[32,128]{1,0:T(8,128)S(1)} custom-call(f32[8,128]{1,0:T(8,128)S(1)} %get-tuple-element.54.v_ref.v1, f32[8,128]{1,0:T(8,128)S(1)} %get-tuple-element.55.last_ref.w0, f32[128,128]{1,0:T(8,128)S(1)} %get-tuple-element.27.corner_ref, s32[8,128]{1,0:T(8,128)S(1)} %get-tuple-element.33.facts_ref, f32[272,1024]{1,0:T(8,128)S(1)} %get-tuple-element.36.rest_0_, ...), custom_call_target="tpu_custom_call" | custom-call | tf_op jit(solution)/shard_map/before/pallas_call | solution.py:433
  110.4 17.0 %all-gather.1 = f32[512,128]{1,0:T(8,128)S(1)} all-gather(f32[32,128]{1,0:T(8,128)S(1)} %before.4), channel_id=3, replica_groups=mesh['gx'=32,'gy'=16] {'gy'}, dimensions={0}, use_global_device_ids=true | all-gather | bytes 278528 | tf_op jit(solution)/shard_map/all_gather | solution.py:530
  127.4 2.9 %after.4 = (f32[8,128]{1,0:T(8,128)S(1)}, f32[8,128]{1,0:T(8,128)S(1)}, f32[8,128]{1,0:T(8,128)S(1)}, f32[1,128]{1,0:T(1,128)S(1)}, f32[1,128]{1,0:T(1,128)S(1)}) custom-call(s32[1]{0:T(128)} %bitcast.y_ref, f32[16,32,128]{2,1,0:T(8,128)S(1)} %bitcast.26, f32[16,128]{1,0:T(8,128)S(1)} %get-tuple-element.31.rows_ref, ...), custom_call_target="tpu_custom_call" | custom-call | tf_op jit(solution)/shard_map/after/pallas_call | solution.py:433
  130.3 1.9 collective-permute-start.10
  132.2 7.5 %collective-permute-start.11 = (f32[8,128]{1,0:T(8,128)S(1)}, f32[8,128]{1,0:T(8,128)S(1)}, u32[]{:S(2)}, u32[]{:S(2)}) collective-permute-start(f32[8,128]{1,0:T(8,128)S(1)} %get-tuple-element.43), channel_id=1, source_target_pairs={{16,0},{32,16},{48,32},{64,48},{80,64},{96,80},{112,96},{128,112},... | collective-permute-start | bytes 12296 | tf_op jit(solution)/shard_map/ppermute | solution.py:446
  139.8 0.0 collective-permute-done.10
  139.8 1.3 collective-permute-done.11
  141.1 1.4 collective-permute-start.15
  142.4 1.3 collective-permute-start.14
  143.7 1.9 collective-permute-start.13
  145.7 7.4 %collective-permute-start.12 = (f32[8,128]{1,0:T(8,128)S(1)}, f32[8,128]{1,0:T(8,128)S(1)}, u32[]{:S(2)}, u32[]{:S(2)}) collective-permute-start(f32[8,128]{1,0:T(8,128)S(1)} %get-tuple-element.52.v_ref.v2), channel_id=1, source_target_pairs={{16,0},{32,16},{48,32},{64,48},{80,64},{96,80},{112,96},{128,112},... | collective-permute-start | bytes 12296 | tf_op jit(solution)/shard_map/ppermute | solution.py:446
  153.1 0.0 collective-permute-done.15.rest_4_
  153.1 0.0 collective-permute-done.14.rest_3_
  153.1 0.0 collective-permute-done.13.rest_2_
  153.1 1.3 collective-permute-done.12.rest_1_
  154.4 1.3 before.5
  155.7 18.7 %all-gather.2 = f32[512,128]{1,0:T(8,128)S(1)} all-gather(f32[32,128]{1,0:T(8,128)S(1)} %before.5), channel_id=4, replica_groups=mesh['gx'=32,'gy'=16] {'gy'}, dimensions={0}, use_global_device_ids=true | all-gather | bytes 278528 | tf_op jit(solution)/shard_map/all_gather | solution.py:530
  174.4 2.8 %after.5 = (f32[8,128]{1,0:T(8,128)S(1)}, f32[8,128]{1,0:T(8,128)S(1)}, f32[8,128]{1,0:T(8,128)S(1)}, f32[1,128]{1,0:T(1,128)S(1)}) custom-call(s32[1]{0:T(128)} %bitcast.y_ref, f32[16,32,128]{2,1,0:T(8,128)S(1)} %bitcast.25, f32[16,128]{1,0:T(8,128)S(1)} %get-tuple-element.31.rows_ref, f32[144,128]{1,0:T(8,128)S(1)} %get-tuple-element.32.places_ref, ...), custom_call_target="tpu_custom_call" | custom-call | tf_op jit(solution)/shard_map/after/pallas_call | solution.py:433
  177.2 1.9 collective-permute-start.16
  179.1 7.5 %collective-permute-start.17 = (f32[8,128]{1,0:T(8,128)S(1)}, f32[8,128]{1,0:T(8,128)S(1)}, u32[]{:S(2)}, u32[]{:S(2)}) collective-permute-start(f32[8,128]{1,0:T(8,128)S(1)} %get-tuple-element.49), channel_id=1, source_target_pairs={{16,0},{32,16},{48,32},{64,48},{80,64},{96,80},{112,96},{128,112},... | collective-permute-start | bytes 12296 | tf_op jit(solution)/shard_map/ppermute | solution.py:446
  186.6 6.9 %all-gather.4 = f32[4,1,128]{2,1,0:T(1,128)S(1)} all-gather(f32[1,1,128]{2,1,0:T(1,128)S(1)} %bitcast.35), channel_id=1, replica_groups={{0,16,32,48},{64,80,96,112},{128,144,160,176},{192,208,224,240},{256,27..., dimensions={0}, use_global_device_ids=true | all-gather | bytes 2560 | tf_op jit(solution)/shard_map/all_gather | solution.py:560
  193.6 15.7 %all-gather.5 = f32[8,1,128]{2,1,0:T(1,128)S(1)} all-gather(f32[1,1,128]{2,1,0:T(1,128)S(1)} %bitcast.36), channel_id=5, replica_groups={{0,64,128,192,256,320,384,448},{16,80,144,208,272,336,400,464},{32,96,1..., dimensions={0}, use_global_device_ids=true | all-gather | bytes 4608 | tf_op jit(solution)/shard_map/all_gather | solution.py:560
  209.3 0.0 collective-permute-done.16.east
  209.3 0.0 collective-permute-done.17.west
  209.3 0.0 copy-done.2
  209.3 0.7 final.1
  (10 shorter events, 0.1 us)
Async XLA Ops:
  1.3 17.5 %collective-permute-start.3 = (f32[8,128]{1,0:T(8,128)S(1)}, f32[8,128]{1,0:T(8,128)S(1)}, u32[]{:S(2)}, u32[]{:S(2)}) collective-permute-start(f32[8,128]{1,0:T(8,128)S(1)} %bitcast_multiply_fusion.v_ref.v0), channel_id=1, source_target_pairs={{0,1},{1,2},{2,3},{3,4},{4,5},{5,6},{6,7},{7,8},{8,9},{9,10},{10,1... | collective-permute-start | bytes 12296 | tf_op jit(solution)/shard_map/ppermute | solution.py:446
  3.1 15.8 %collective-permute-start.2 = (f32[8,128]{1,0:T(8,128)S(1)}, f32[8,128]{1,0:T(8,128)S(1)}, u32[]{:S(2)}, u32[]{:S(2)}) collective-permute-start(f32[8,128]{1,0:T(8,128)S(1)} %bitcast_multiply_fusion.v_ref.v0), channel_id=1, source_target_pairs={{1,0},{2,1},{3,2},{4,3},{5,4},{6,5},{7,6},{8,7},{9,8},{10,9},{11,1... | collective-permute-start | bytes 12296 | tf_op jit(solution)/shard_map/ppermute | solution.py:446
  4.4 14.5 %collective-permute-start.1 = (f32[8,128]{1,0:T(8,128)S(1)}, f32[8,128]{1,0:T(8,128)S(1)}, u32[]{:S(2)}, u32[]{:S(2)}) collective-permute-start(f32[8,128]{1,0:T(8,128)S(1)} %bitcast_multiply_fusion.v_ref.v0), channel_id=1, source_target_pairs={{0,16},{16,32},{32,48},{48,64},{64,80},{80,96},{96,112},{112,128},... | collective-permute-start | bytes 12296 | tf_op jit(solution)/shard_map/ppermute | solution.py:446
  7.8 11.1 %collective-permute-start = (f32[8,128]{1,0:T(8,128)S(1)}, f32[8,128]{1,0:T(8,128)S(1)}, u32[]{:S(2)}, u32[]{:S(2)}) collective-permute-start(f32[8,128]{1,0:T(8,128)S(1)} %bitcast_multiply_fusion.v_ref.v0), channel_id=1, source_target_pairs={{16,0},{32,16},{48,32},{64,48},{80,64},{96,80},{112,96},{128,112},... | collective-permute-start | bytes 12296 | tf_op jit(solution)/shard_map/ppermute | solution.py:446
  14.2 1.0 copy-start
  15.2 0.7 copy-start.3
  16.0 0.7 copy-start.4
  16.7 0.7 copy-start.6
  17.3 0.7 copy-start.7
  18.0 30.0 %copy-start.5 = (f32[1,512]{1,0:T(1,128)S(1)}, f32[1,512]{1,0:T(1,128)}, u32[]{:S(2)}) copy-start(f32[1,512]{1,0:T(1,128)} %diag_ref.1) | copy-start | bytes 6148
  18.9 0.7 copy-start.1
  65.2 18.8 %collective-permute-start.5 = (f32[272,1024]{1,0:T(8,128)S(1)}, f32[272,1024]{1,0:T(8,128)S(1)}, u32[]{:S(2)}, u32[]{:S(2)}) collective-permute-start(f32[272,1024]{1,0:T(8,128)S(1)} %get-tuple-element.36.rest_0_), channel_id=1, source_target_pairs={{0,1},{1,2},{2,3},{3,4},{4,5},{5,6},{6,7},{7,8},{8,9},{9,10},{10,1... | collective-permute-start | bytes 3342344 | tf_op jit(solution)/shard_map/ppermute | solution.py:446
  67.6 16.4 %collective-permute-start.4 = (f32[272,1024]{1,0:T(8,128)S(1)}, f32[272,1024]{1,0:T(8,128)S(1)}, u32[]{:S(2)}, u32[]{:S(2)}) collective-permute-start(f32[272,1024]{1,0:T(8,128)S(1)} %get-tuple-element.36.rest_0_), channel_id=1, source_target_pairs={{1,0},{2,1},{3,2},{4,3},{5,4},{6,5},{7,6},{8,7},{9,8},{10,9},{11,1... | collective-permute-start | bytes 3342344 | tf_op jit(solution)/shard_map/ppermute | solution.py:446
  84.0 13.3 %copy-start.8 = (f32[1,1,8,128]{3,2,1,0:T(8,128)S(1)}, f32[1,1,8,128]{3,2,1,0:T(8,128)}, u32[]{:S(2)}) copy-start(f32[1,1,8,128]{3,2,1,0:T(8,128)} %param.13) | copy-start | bytes 12292
  86.9 9.2 %collective-permute-start.6 = (f32[8,128]{1,0:T(8,128)S(1)}, f32[8,128]{1,0:T(8,128)S(1)}, u32[]{:S(2)}, u32[]{:S(2)}) collective-permute-start(f32[8,128]{1,0:T(8,128)S(1)} %get-tuple-element.38), channel_id=1, source_target_pairs={{0,16},{16,32},{32,48},{48,64},{64,80},{80,96},{96,112},{112,128},... | collective-permute-start | bytes 12296 | tf_op jit(solution)/shard_map/ppermute | solution.py:446
  88.8 8.6 %collective-permute-start.7 = (f32[8,128]{1,0:T(8,128)S(1)}, f32[8,128]{1,0:T(8,128)S(1)}, u32[]{:S(2)}, u32[]{:S(2)}) collective-permute-start(f32[8,128]{1,0:T(8,128)S(1)} %get-tuple-element.39), channel_id=1, source_target_pairs={{16,0},{32,16},{48,32},{64,48},{80,64},{96,80},{112,96},{128,112},... | collective-permute-start | bytes 12296 | tf_op jit(solution)/shard_map/ppermute | solution.py:446
  97.3 9.4 %collective-permute-start.9 = (f32[8,128]{1,0:T(8,128)S(1)}, f32[8,128]{1,0:T(8,128)S(1)}, u32[]{:S(2)}, u32[]{:S(2)}) collective-permute-start(f32[8,128]{1,0:T(8,128)S(1)} %get-tuple-element.54.v_ref.v1), channel_id=1, source_target_pairs={{0,16},{16,32},{32,48},{48,64},{64,80},{80,96},{96,112},{112,128},... | collective-permute-start | bytes 12296 | tf_op jit(solution)/shard_map/ppermute | solution.py:446
  99.3 8.8 %collective-permute-start.8 = (f32[8,128]{1,0:T(8,128)S(1)}, f32[8,128]{1,0:T(8,128)S(1)}, u32[]{:S(2)}, u32[]{:S(2)}) collective-permute-start(f32[8,128]{1,0:T(8,128)S(1)} %get-tuple-element.54.v_ref.v1), channel_id=1, source_target_pairs={{16,0},{32,16},{48,32},{64,48},{80,64},{96,80},{112,96},{128,112},... | collective-permute-start | bytes 12296 | tf_op jit(solution)/shard_map/ppermute | solution.py:446
  130.3 9.4 %collective-permute-start.10 = (f32[8,128]{1,0:T(8,128)S(1)}, f32[8,128]{1,0:T(8,128)S(1)}, u32[]{:S(2)}, u32[]{:S(2)}) collective-permute-start(f32[8,128]{1,0:T(8,128)S(1)} %get-tuple-element.42), channel_id=1, source_target_pairs={{0,16},{16,32},{32,48},{48,64},{64,80},{80,96},{96,112},{112,128},... | collective-permute-start | bytes 12296 | tf_op jit(solution)/shard_map/ppermute | solution.py:446
  132.2 8.8 %collective-permute-start.11 = (f32[8,128]{1,0:T(8,128)S(1)}, f32[8,128]{1,0:T(8,128)S(1)}, u32[]{:S(2)}, u32[]{:S(2)}) collective-permute-start(f32[8,128]{1,0:T(8,128)S(1)} %get-tuple-element.43), channel_id=1, source_target_pairs={{16,0},{32,16},{48,32},{64,48},{80,64},{96,80},{112,96},{128,112},... | collective-permute-start | bytes 12296 | tf_op jit(solution)/shard_map/ppermute | solution.py:446
  141.1 12.0 %collective-permute-start.15 = (f32[8,128]{1,0:T(8,128)S(1)}, f32[8,128]{1,0:T(8,128)S(1)}, u32[]{:S(2)}, u32[]{:S(2)}) collective-permute-start(f32[8,128]{1,0:T(8,128)S(1)} %get-tuple-element.52.v_ref.v2), channel_id=1, source_target_pairs={{0,1},{1,2},{2,3},{3,4},{4,5},{5,6},{6,7},{7,8},{8,9},{9,10},{10,1... | collective-permute-start | bytes 12296 | tf_op jit(solution)/shard_map/ppermute | solution.py:446
  142.4 10.7 %collective-permute-start.14 = (f32[8,128]{1,0:T(8,128)S(1)}, f32[8,128]{1,0:T(8,128)S(1)}, u32[]{:S(2)}, u32[]{:S(2)}) collective-permute-start(f32[8,128]{1,0:T(8,128)S(1)} %get-tuple-element.52.v_ref.v2), channel_id=1, source_target_pairs={{1,0},{2,1},{3,2},{4,3},{5,4},{6,5},{7,6},{8,7},{9,8},{10,9},{11,1... | collective-permute-start | bytes 12296 | tf_op jit(solution)/shard_map/ppermute | solution.py:446
  143.7 9.4 %collective-permute-start.13 = (f32[8,128]{1,0:T(8,128)S(1)}, f32[8,128]{1,0:T(8,128)S(1)}, u32[]{:S(2)}, u32[]{:S(2)}) collective-permute-start(f32[8,128]{1,0:T(8,128)S(1)} %get-tuple-element.52.v_ref.v2), channel_id=1, source_target_pairs={{0,16},{16,32},{32,48},{48,64},{64,80},{80,96},{96,112},{112,128},... | collective-permute-start | bytes 12296 | tf_op jit(solution)/shard_map/ppermute | solution.py:446
  145.7 8.7 %collective-permute-start.12 = (f32[8,128]{1,0:T(8,128)S(1)}, f32[8,128]{1,0:T(8,128)S(1)}, u32[]{:S(2)}, u32[]{:S(2)}) collective-permute-start(f32[8,128]{1,0:T(8,128)S(1)} %get-tuple-element.52.v_ref.v2), channel_id=1, source_target_pairs={{16,0},{32,16},{48,32},{64,48},{80,64},{96,80},{112,96},{128,112},... | collective-permute-start | bytes 12296 | tf_op jit(solution)/shard_map/ppermute | solution.py:446
  174.4 35.0 %copy-start.2 = (f32[1,1,8,128]{3,2,1,0:T(8,128)S(1)}, f32[1,1,8,128]{3,2,1,0:T(8,128)}, u32[]{:S(2)}) copy-start(f32[1,1,8,128]{3,2,1,0:T(8,128)} %param.14) | copy-start | bytes 12292
  177.2 32.2 %collective-permute-start.16 = (f32[8,128]{1,0:T(8,128)S(1)}, f32[8,128]{1,0:T(8,128)S(1)}, u32[]{:S(2)}, u32[]{:S(2)}) collective-permute-start(f32[8,128]{1,0:T(8,128)S(1)} %get-tuple-element.48), channel_id=1, source_target_pairs={{0,16},{16,32},{32,48},{48,64},{64,80},{80,96},{96,112},{112,128},... | collective-permute-start | bytes 12296 | tf_op jit(solution)/shard_map/ppermute | solution.py:446
  179.1 30.2 %collective-permute-start.17 = (f32[8,128]{1,0:T(8,128)S(1)}, f32[8,128]{1,0:T(8,128)S(1)}, u32[]{:S(2)}, u32[]{:S(2)}) collective-permute-start(f32[8,128]{1,0:T(8,128)S(1)} %get-tuple-element.49), channel_id=1, source_target_pairs={{16,0},{32,16},{48,32},{64,48},{80,64},{96,80},{112,96},{128,112},... | collective-permute-start | bytes 12296 | tf_op jit(solution)/shard_map/ppermute | solution.py:446
